TPU v7x, 512 devices: a whole 4x8x8 slice. The times are simulated.
512 devices in a mesh: dp: 64 (over x, y, core), rows: 8 (over z).
Axes of the slice: x: 4, y: 8, z: 8, core: 2. Of those that a mesh axis runs over, the one named last changes fastest.
Arguments:
- features: bfloat16 [64, 40, 64, 1024], P('dp', 'rows'), may hold values from -6 to 6
- halting_map: int32 [64, 40, 64], P('dp', 'rows'), may hold values from 1 to 23, as said below
- grad_out: bfloat16 [64, 40, 64, 1024], P('dp', 'rows'), may hold values from -16 to 16
- weight_reduce: bfloat16 [256, 1024], replicated, may hold values from -0.1875 to 0.1875
- weight_conv: bfloat16 [256, 2304], replicated, may hold values from -0.125 to 0.125
- weight_expand: bfloat16 [1024, 256], replicated, may hold values from -0.375 to 0.375
Outputs:
- unit_out: bfloat16 [64, 40, 64, 1024], P('dp', 'rows')
- grad_in: bfloat16 [64, 40, 64, 1024], P('dp', 'rows')
- grad_conv: float32 [256, 2304], P('dp')
- grad_expand: float32 [1024, 256], P('dp')
Inputs may be any that keep to these rules, and one draw needn't show every extreme that they name: `halting_map`: the number of units still active at each position; its largest value occurs in every sample.
All inputs are finite; a program needn't handle non-finite values.
Results may differ from a plain program's by a relative error of at most 0.034.
The roundings to bfloat16 on the way count: a program that leaves them out, or rounds other values in their place, can miss the bound.
Values may be sent and summed in bfloat16 or wider, within the bound.
No kernel may reach another device: no remote copies, remote signals or barrier semaphores. Data moves between devices by JAX's collectives and lax.ppermute only.
A program may use at most 64 MiB of HBM per device.

v0:
```python
import jax
import jax.numpy as jnp
from jax import lax
from jax.sharding import PartitionSpec as P

UNIT = 5


def padded_2(cells, sides, width):
    for axis, dim in sides:
        count = lax.axis_size(axis)
        ends = count - 1
        head = lax.slice_in_dim(cells, 0, width, axis=dim)
        tail = lax.slice_in_dim(cells, cells.shape[dim] - width, cells.shape[dim], axis=dim)
        cells = jnp.concatenate(
            [
                lax.ppermute(tail, axis, [(i, (i + 1) % count) for i in range(ends)]),
                cells,
                lax.ppermute(head, axis, [((i + 1) % count, i) for i in range(ends)]),
            ],
            axis=dim,
        )
    return cells


def window_columns(padded):
    sample_count, padded_rows, col_count, chan_count = padded.shape
    row_count = padded_rows - 2
    widened = jnp.pad(padded, ((0, 0), (0, 0), (1, 1), (0, 0)))
    pieces = [
        widened[:, row_off : row_off + row_count, col_off : col_off + col_count, :]
        for row_off in range(3)
        for col_off in range(3)
    ]
    return jnp.concatenate(pieces, axis=3).reshape(
        sample_count * row_count * col_count, 9 * chan_count
    )


def flipped_kernel(weight_conv):
    width_f = weight_conv.shape[0]
    kernel = weight_conv.reshape(width_f, 3, 3, -1)[:, ::-1, ::-1, :]
    return jnp.transpose(kernel, (1, 2, 0, 3)).reshape(9 * width_f, -1)


def local(features, halting_map, grad_out, weight_reduce, weight_conv, weight_expand):
    sample_count, row_count, col_count, chan_count = features.shape
    width_f = weight_reduce.shape[0]
    positions = sample_count * row_count * col_count
    flat_in = features.reshape(positions, chan_count)
    active = (halting_map > UNIT).astype(jnp.float32).reshape(positions, 1)
    pre_one = jnp.dot(flat_in, weight_reduce.T, preferred_element_type=jnp.float32)
    hidden_one = jnp.maximum(pre_one, 0.0).astype(jnp.bfloat16)
    hidden_grid = hidden_one.reshape(sample_count, row_count, col_count, width_f)
    padded_one = padded_2(hidden_grid, (("rows", 1),), 1)
    columns = window_columns(padded_one)
    pre_two = jnp.dot(columns, weight_conv.T, preferred_element_type=jnp.float32)
    hidden_two = jnp.maximum(pre_two, 0.0).astype(jnp.bfloat16)
    branch = jnp.dot(hidden_two, weight_expand.T, preferred_element_type=jnp.float32)
    unit_out = (flat_in.astype(jnp.float32) + active * branch).astype(jnp.bfloat16)
    upstream = grad_out.reshape(positions, chan_count)
    gated = (active * upstream.astype(jnp.float32)).astype(jnp.bfloat16)
    expand_part = jnp.dot(gated.T, hidden_two, preferred_element_type=jnp.float32)
    back_two = jnp.dot(gated, weight_expand, preferred_element_type=jnp.float32)
    grad_two = jnp.where(pre_two > 0, back_two, 0.0).astype(jnp.bfloat16)
    conv_part = jnp.dot(grad_two.T, columns, preferred_element_type=jnp.float32)
    grad_grid = grad_two.reshape(sample_count, row_count, col_count, width_f)
    padded_two = padded_2(grad_grid, (("rows", 1),), 1)
    grad_hidden = jnp.dot(
        window_columns(padded_two), flipped_kernel(weight_conv), preferred_element_type=jnp.float32
    )
    grad_one = jnp.where(pre_one > 0, grad_hidden, 0.0).astype(jnp.bfloat16)
    back_one = jnp.dot(grad_one, weight_reduce, preferred_element_type=jnp.float32)
    grad_in = (upstream.astype(jnp.float32) + back_one).astype(jnp.bfloat16)
    conv_block, expand_block = (
        lax.psum_scatter(conv_part, "dp", scatter_dimension=0, tiled=True),
        lax.psum_scatter(expand_part, "dp", scatter_dimension=0, tiled=True),
    )
    grad_conv, grad_expand = lax.psum((conv_block, expand_block), "rows")
    out_shape = (sample_count, row_count, col_count, chan_count)
    return (unit_out.reshape(out_shape), grad_in.reshape(out_shape), grad_conv, grad_expand)


def solution(mesh):
    in_specs = (
        P("dp", "rows", None, None),
        P("dp", "rows", None),
        P("dp", "rows", None, None),
        P(),
        P(),
        P(),
    )
    out_specs = (
        P("dp", "rows", None, None),
        P("dp", "rows", None, None),
        P("dp", None),
        P("dp", None),
    )
    return jax.shard_map(local, mesh=mesh, in_specs=in_specs, out_specs=out_specs, check_vma=False)
```

profile of v0, /device:TPU:16, one launch (start us, length us, event | category | flops | bytes accessed | tf_op | source)
XLA Modules:
  0.0 421.0 jit_solution(8814190197359499175)
XLA Ops:
  7.2 0.0 copy-start
  7.2 0.0 copy-start.8
  7.2 0.0 copy-start.3
  7.2 0.0 all-reduce.6.cloned.1.call-start
  7.2 1.0 copy-done
  8.2 2.2 maximum_convert_fusion.1
  10.4 4.3 %collective-permute-start = (bf16[1,1,64,256]{3,2,1,0:T(8,128)(2,1)S(1)}, bf16[1,1,64,256]{3,2,1,0:T(8,128)(2,1)S(1)}, u32[]{:S(2)}, u32[]{:S(2)}) collective-permute-start(bf16[1,1,64,256]{3,2,1,0:T(8,128)(2,1)S(1)} %get-tuple-element.24), channel_id=1, source_target_pairs={{0,1},{1,2},{2,3},{3,4},{4,5},{5,6},{6,7},{8,9},{9,10},{10,11},{11... | collective-permute-start | bytes 98312 | tf_op jit(solution)/shard_map/ppermute | solution.py:17
  14.7 1.3 collective-permute-start.1
  16.0 0.0 copy-done.8
  16.0 0.1 reshape.63
  16.1 0.0 copy-done.3
  16.1 0.2 fusion.3
  16.3 0.0 collective-permute-done
  16.3 4.6 %collective-permute-done.1 = bf16[1,1,64,256]{3,2,1,0:T(8,128)(2,1)S(1)} collective-permute-done((bf16[1,1,64,256]{3,2,1,0:T(8,128)(2,1)S(1)}, bf16[1,1,64,256]{3,2,1,0:T(8,128)(2,1)S(1)}, u32[]{:S(2)}, u32[]{:S(2)}) %collective-permute-start.1) | collective-permute-done | bytes 32800 | tf_op jit(solution)/shard_map/ppermute | solution.py:19
  20.8 0.1 select_maximum_fusion.2
  20.9 0.1 fusion.16
  21.1 0.0 copy-start.7
  21.3 1.1 copy-done.7
  22.3 0.0 copy-start.5
  22.3 0.6 fusion.19
  22.9 0.5 copy-done.5
  23.4 0.3 fusion.5
  23.7 2.2 fusion.20
  25.9 0.0 all-reduce.6.cloned.1.call-update
  26.0 0.0 reduce-scatter.2.cloned.1.call-start
  26.0 1.4 copy.12
  27.5 1.3 reverse_bitcast_fusion
  28.8 0.0 copy-start.2
  28.8 1.5 copy.13
  30.4 1.3 dynamic-slice
  32.3 4.3 %collective-permute-start.2 = (bf16[1,1,64,256]{3,2,1,0:T(8,128)(2,1)S(1)}, bf16[1,1,64,256]{3,2,1,0:T(8,128)(2,1)S(1)}, u32[]{:S(2)}, u32[]{:S(2)}) collective-permute-start(bf16[1,1,64,256]{3,2,1,0:T(8,128)(2,1)S(1)} %get-tuple-element.20), channel_id=1, source_target_pairs={{0,1},{1,2},{2,3},{3,4},{4,5},{5,6},{6,7},{8,9},{9,10},{10,11},{11... | collective-permute-start | bytes 98312 | tf_op jit(solution)/shard_map/ppermute | solution.py:17
  36.6 1.3 collective-permute-start.3
  37.9 0.0 copy-done.2
  37.9 2.3 fusion.2
  40.1 1.5 fusion.10
  41.7 0.0 reduce-scatter.2.cloned.1.call-update
  41.7 0.0 collective-permute-done.2
  41.7 2.3 collective-permute-done.3
  44.0 0.1 select_maximum_fusion
  44.0 0.1 fusion.15
  44.2 0.7 constant_dynamic-update-slice_fusion.17
  44.9 0.0 copy-start.1
  44.9 0.0 copy-start.4
  44.9 0.0 copy-start.6
  44.9 0.7 constant_dynamic-update-slice_fusion.16
  45.6 0.7 constant_dynamic-update-slice_fusion.15
  46.3 0.7 constant_dynamic-update-slice_fusion.14
  47.0 0.7 constant_dynamic-update-slice_fusion.13
  47.7 0.7 constant_dynamic-update-slice_fusion.12
  48.4 0.7 constant_dynamic-update-slice_fusion.11
  49.1 0.7 constant_dynamic-update-slice_fusion.10
  49.8 0.7 constant_dynamic-update-slice_fusion.9
  50.6 0.0 copy-done.1
  50.6 0.0 copy-done.4
  50.6 0.0 copy-done.6
  50.6 3.3 fusion.1
  53.8 173.4 %all-reduce.6.cloned.1.call-done = f32[256,2304]{1,0:T(8,128)} async-done(((f32[256,2304]{1,0:T(8,128)}), f32[256,2304]{1,0:T(8,128)}) %all-reduce.6.cloned.1.call-update) | async-done | bytes 2359312
  227.3 0.9 constant_dynamic-slice_fusion
  228.2 153.6 %reduce-scatter.2.cloned.1.call-done = f32[16,256]{1,0:T(8,128)} async-done(((f32[1024,256]{1,0:T(8,128)}), f32[16,256]{1,0:T(8,128)}) %reduce-scatter.2.cloned.1.call-update) | async-done | bytes 16400 | tf_op jit(solution)/shard_map/reduce_scatter | solution.py:77
  381.7 32.4 %all-reduce.3 = (f32[4,2304]{1,0:T(4,128)}, f32[16,256]{1,0:T(8,128)}) all-reduce(f32[4,2304]{1,0:T(4,128)S(1)} %constant_dynamic-slice_fusion, f32[16,256]{1,0:T(8,128)} %reduce-scatter.2.cloned.1.call-done), channel_id=1, replica_groups=mesh['dp'=64,'rows'=8] {'rows'}, use_global_device_ids=true, to_apply=%region_1.2 | all-reduce | flops 13312 | bytes 106496 | tf_op jit(solution)/shard_map/psum | solution.py:79
  (14 shorter events, 0.2 us)
Async XLA Ops:
  7.2 1.0 copy-start
  7.2 8.8 %copy-start.8 = (s32[1,5,64]{2,0,1:T(1,128)S(1)}, s32[1,5,64]{2,0,1:T(1,128)}, u32[]{:S(2)}) copy-start(s32[1,5,64]{2,0,1:T(1,128)} %param.7) | copy-start | bytes 3844
  7.2 8.9 %copy-start.3 = (bf16[1,5,64,1024]{3,2,1,0:T(8,128)(2,1)S(1)}, bf16[1,5,64,1024]{3,2,1,0:T(8,128)(2,1)}, u32[]{:S(2)}) copy-start(bf16[1,5,64,1024]{3,2,1,0:T(8,128)(2,1)} %param.8) | copy-start | bytes 1966084
  7.2 220.1 %all-reduce.6.cloned.1.call-start = ((), (), s32[]{:S(2)}) async-start(), calls=%async_computation.2 | async-start | bytes 4718592
  10.4 5.9 %collective-permute-start = (bf16[1,1,64,256]{3,2,1,0:T(8,128)(2,1)S(1)}, bf16[1,1,64,256]{3,2,1,0:T(8,128)(2,1)S(1)}, u32[]{:S(2)}, u32[]{:S(2)}) collective-permute-start(bf16[1,1,64,256]{3,2,1,0:T(8,128)(2,1)S(1)} %get-tuple-element.24), channel_id=1, source_target_pairs={{0,1},{1,2},{2,3},{3,4},{4,5},{5,6},{6,7},{8,9},{9,10},{10,11},{11... | collective-permute-start | bytes 98312 | tf_op jit(solution)/shard_map/ppermute | solution.py:17
  14.7 6.2 %collective-permute-start.1 = (bf16[1,1,64,256]{3,2,1,0:T(8,128)(2,1)S(1)}, bf16[1,1,64,256]{3,2,1,0:T(8,128)(2,1)S(1)}, u32[]{:S(2)}, u32[]{:S(2)}) collective-permute-start(bf16[1,1,64,256]{3,2,1,0:T(8,128)(2,1)S(1)} %get-tuple-element.25), channel_id=1, source_target_pairs={{1,0},{2,1},{3,2},{4,3},{5,4},{6,5},{7,6},{9,8},{10,9},{11,10},{12... | collective-permute-start | bytes 98312 | tf_op jit(solution)/shard_map/ppermute | solution.py:19
  21.1 1.3 copy-start.7
  22.3 1.0 copy-start.5
  26.0 355.8 %reduce-scatter.2.cloned.1.call-start = ((), (), s32[]{:S(2)}) async-start(), calls=%async_computation.1 | async-start | bytes 1064960 | tf_op jit(solution)/shard_map/reduce_scatter | solution.py:77
  28.8 9.1 %copy-start.2 = (bf16[1,5,64,1024]{3,2,1,0:T(8,128)(2,1)S(1)}, bf16[1,5,64,1024]{3,2,1,0:T(8,128)(2,1)}, u32[]{:S(2)}) copy-start(bf16[1,5,64,1024]{3,2,1,0:T(8,128)(2,1)} %param.6) | copy-start | bytes 1966084
  32.3 9.4 %collective-permute-start.2 = (bf16[1,1,64,256]{3,2,1,0:T(8,128)(2,1)S(1)}, bf16[1,1,64,256]{3,2,1,0:T(8,128)(2,1)S(1)}, u32[]{:S(2)}, u32[]{:S(2)}) collective-permute-start(bf16[1,1,64,256]{3,2,1,0:T(8,128)(2,1)S(1)} %get-tuple-element.20), channel_id=1, source_target_pairs={{0,1},{1,2},{2,3},{3,4},{4,5},{5,6},{6,7},{8,9},{9,10},{10,11},{11... | collective-permute-start | bytes 98312 | tf_op jit(solution)/shard_map/ppermute | solution.py:17
  36.6 7.4 %collective-permute-start.3 = (bf16[1,1,64,256]{3,2,1,0:T(8,128)(2,1)S(1)}, bf16[1,1,64,256]{3,2,1,0:T(8,128)(2,1)S(1)}, u32[]{:S(2)}, u32[]{:S(2)}) collective-permute-start(bf16[1,1,64,256]{3,2,1,0:T(8,128)(2,1)S(1)} %get-tuple-element.21), channel_id=1, source_target_pairs={{1,0},{2,1},{3,2},{4,3},{5,4},{6,5},{7,6},{9,8},{10,9},{11,10},{12... | collective-permute-start | bytes 98312 | tf_op jit(solution)/shard_map/ppermute | solution.py:19
  44.9 5.7 %copy-start.1 = (bf16[3,3,256,256]{3,2,1,0:T(8,128)(2,1)S(1)}, bf16[3,3,256,256]{3,2,1,0:T(8,128)(2,1)}, u32[]{:S(2)}) copy-start(bf16[3,3,256,256]{3,2,1,0:T(8,128)(2,1)} %copy.13) | copy-start | bytes 3538948
  44.9 5.7 %copy-start.4 = (bf16[1,5,64,1024]{3,2,1,0:T(8,128)(2,1)S(1)}, bf16[1,5,64,1024]{3,2,1,0:T(8,128)(2,1)}, u32[]{:S(2)}) copy-start(bf16[1,5,64,1024]{3,2,1,0:T(8,128)(2,1)} %param.8) | copy-start | bytes 1966084
  44.9 5.7 %copy-start.6 = (f32[320,256]{1,0:T(8,128)S(1)}, f32[320,256]{1,0:T(8,128)}, u32[]{:S(2)}) copy-start(f32[320,256]{1,0:T(8,128)} %get-tuple-element.27) | copy-start | bytes 983044
Sparse Core Ops, SparseCore 0:
  26.1 201.1 all-reduce.5
  231.8 149.8 reduce-scatter.1
where the time goes:
time: 422 us; the launch traced here: 421 us
  waiting for transfers between devices  334 us (79%)
  blocking collectives  32.4 us (8%)
  local copies, waits for them, and re-layouts  15.8 us (4%)
  between operations  15 us (4%)
  matrix products  12.4 us (3%)
  starting transfers between devices  11.2 us (3%)
    unnamed x3, waiting for transfers between devices  173 us
    reduce_scatter x1, waiting for transfers between devices, local(): lax.psum_scatter(expand_part, 'dp', scatter_dimension=0, tiled=True)  154 us
    psum x1, blocking collectives, local(): grad_conv, grad_expand = lax.psum((conv_block, expand_block), 'rows')  32.4 us
    unnamed x37, local copies, waits for them, and re-layouts  11.9 us
    ppermute x2, starting transfers between devices, padded_2(): lax.ppermute(tail, axis, [(i, (i + 1) % count) for i in range(ends)])  8.54 us
  transfers between devices with their start and end apart: 6, of which 4 were waited for; matrix products, arithmetic and copies ran while one was open for 5% of the time, Pallas kernels for 0%

commit v1 on v0

v1 whole, which is shorter than its diff:
```python
import functools

import jax
import jax.numpy as jnp
from jax import lax
from jax.experimental import pallas as pl
from jax.experimental.pallas import tpu as pltpu
from jax.sharding import PartitionSpec as P

UNIT = 5
BF = jnp.bfloat16
F32 = jnp.float32

NX, NY, NC, NZ = 4, 8, 2, 8
VMEM = pltpu.CompilerParams(vmem_limit_bytes=56 * 1024 * 1024)


def dp_of(x, y, c):
    return (x * NY + y) * NC + c


def swap_core():
    return [(d, d ^ 1) for d in range(NX * NY * NC)]


def step_x(k):
    return [
        (dp_of(x, y, c), dp_of((x + k) % NX, y, c))
        for x in range(NX)
        for y in range(NY)
        for c in range(NC)
    ]


def step_y(k):
    return [
        (dp_of(x, y, c), dp_of(x, (y + k) % NY, c))
        for x in range(NX)
        for y in range(NY)
        for c in range(NC)
    ]


def step_z(k):
    return [(z, (z + k) % NZ) for z in range(NZ)]


def dot(left, right, left_dim, right_dim):
    return lax.dot_general(
        left, right, (((left_dim,), (right_dim,)), ((), ())), preferred_element_type=F32
    )


def active_column(halting):
    rows, cols = halting.shape
    active = (halting > UNIT).astype(F32)
    at_row = lax.broadcasted_iota(jnp.int32, (cols, cols), 0)
    at_col = lax.broadcasted_iota(jnp.int32, (cols, cols), 1)
    parts = [
        jnp.sum(jnp.where(at_row == at_col, active[r : r + 1, :], 0.0), axis=1, keepdims=True)
        for r in range(rows)
    ]
    return jnp.concatenate(parts, axis=0)


def neighbours(cells, cols):
    count = cells.shape[0]
    wide = cells.astype(F32)
    col = lax.rem(lax.broadcasted_iota(jnp.int32, (count, 1), 0), cols)
    left = jnp.where(col == 0, 0.0, pltpu.roll(wide, 1, 0))
    right = jnp.where(col == cols - 1, 0.0, pltpu.roll(wide, count - 1, 0))
    return left.astype(BF), right.astype(BF)


def enter_kernel(
    halt_ref, feat_ref, grad_ref, reduce_ref, expand_ref,
    hidden_ref, sign_ref, back_ref, up_ref, down_ref,
):
    cols = halt_ref.shape[2]
    rows = halt_ref.shape[1]
    pre_one = dot(feat_ref[...], reduce_ref[...], 1, 1)
    hidden = jnp.maximum(pre_one, 0.0).astype(BF)
    hidden_ref[...] = hidden
    sign_ref[...] = (pre_one > 0).astype(F32).astype(BF)
    back = (active_column(halt_ref[0]) * dot(grad_ref[...], expand_ref[...], 1, 0)).astype(BF)
    back_ref[...] = back
    up_ref[0 : 2 * cols, :] = hidden[0 : 2 * cols]
    up_ref[2 * cols :, :] = back[0:cols]
    down_ref[0 : 2 * cols, :] = hidden[(rows - 2) * cols :]
    down_ref[2 * cols :, :] = back[(rows - 1) * cols :]


def middle_kernel(
    halt_ref, hidden_ref, back_ref, prev_ref, next_ref, grad_ref, conv_ref,
    keep_ref, send_ref, two_ref, gtwo_ref, columns_ref,
):
    rows, cols = halt_ref.shape[1:]
    own = rows * cols
    width = hidden_ref.shape[1]
    place = lax.axis_index("dp")
    my_x, my_y, my_c = place // (NY * NC), (place // NC) % NY, place % NC

    padded = jnp.concatenate([prev_ref[0 : 2 * cols], hidden_ref[...], next_ref[0 : 2 * cols]], axis=0)
    left, right = neighbours(padded, cols)
    wide = own + 2 * cols
    for a in range(3):
        for b, shifted in enumerate((left, padded, right)):
            tap = 3 * a + b
            columns_ref[:, tap * width : (tap + 1) * width] = shifted[a * cols : a * cols + wide]
    pre_two = dot(columns_ref[...], conv_ref[...], 1, 1)
    back = jnp.concatenate([prev_ref[2 * cols :], back_ref[...], next_ref[2 * cols :]], axis=0)
    grad_two = jnp.where(pre_two > 0, back.astype(F32), 0.0).astype(BF)
    gtwo_ref[...] = grad_two
    active = active_column(halt_ref[0])
    hidden_two = (active * jnp.maximum(pre_two[cols : cols + own], 0.0)).astype(BF)
    two_ref[...] = hidden_two

    shape = (width, width)
    at = lax.broadcasted_iota(jnp.int32, shape, 0)
    per_dp = width // (NX * NY * NC)
    j, y = at % per_dp, (at // per_dp) % NY
    x, c = (at // (per_dp * NY)) % NX, at // (per_dp * NY * NX)
    x, y, c = (x + my_x) % NX, (y + my_y) % NY, (c + my_c) % NC
    wanted = dp_of(x, y, c) * per_dp + j
    shuffle = (lax.broadcasted_iota(jnp.int32, shape, 1) == wanted).astype(F32).astype(BF)
    grad_rows = dot(shuffle, grad_two[cols : cols + own], 1, 1).astype(BF)
    conv_part = dot(grad_rows, columns_ref[cols : cols + own, :], 1, 0).astype(BF)
    block = per_dp * NY
    taps = conv_part.shape[1] // width
    for tap in range(taps):
        for rel in range(NX):
            rows_at = slice(tap * block, (tap + 1) * block)
            lanes = slice(tap * width, (tap + 1) * width)
            keep_ref[rel, rows_at, :] = conv_part[rel * block : (rel + 1) * block, lanes]
            send_ref[rel, rows_at, :] = conv_part[(NX + rel) * block : (NX + rel + 1) * block, lanes]
    expand_part = dot(grad_ref[...], hidden_two, 0, 0).astype(BF)
    start = taps * block
    per_dp = expand_part.shape[0] // (NX * NY * NC)
    for x in range(NX):
        rel_x = (x - my_x + NX) % NX
        for y in range(NY):
            at = pl.multiple_of(start + (y - my_y + NY) % NY * per_dp, per_dp)
            first = dp_of(x, y, 0) * per_dp
            zero, one = (expand_part[first + i * per_dp : first + (i + 1) * per_dp] for i in (0, 1))
            keep_ref[rel_x, pl.ds(at, per_dp), :] = jnp.where(my_c == 0, zero, one)
            send_ref[rel_x, pl.ds(at, per_dp), :] = jnp.where(my_c == 0, one, zero)


def leave_kernel(
    feat_ref, grad_ref, two_ref, gtwo_ref, sign_ref, reduce_ref, conv_ref, expand_ref,
    out_ref, gin_ref, columns_ref, stacked_ref, *, cols,
):
    own = feat_ref.shape[0]
    width = two_ref.shape[1]
    out_ref[...] = (feat_ref[...].astype(F32) + dot(two_ref[...], expand_ref[...], 1, 1)).astype(BF)
    grad_two = gtwo_ref[...]
    left, right = neighbours(grad_two, cols)
    for a in range(3):
        for b, shifted in enumerate((right, grad_two, left)):
            tap = 3 * a + b
            at = slice(tap * width, (tap + 1) * width)
            columns_ref[:, at] = shifted[(2 - a) * cols : (2 - a) * cols + own]
            stacked_ref[at, :] = conv_ref[:, at]
    grad_hidden = dot(columns_ref[...], stacked_ref[...], 1, 0)
    grad_one = (grad_hidden * sign_ref[...].astype(F32)).astype(BF)
    gin_ref[...] = (grad_ref[...].astype(F32) + dot(grad_one, reduce_ref[...], 1, 0)).astype(BF)


def core_kernel(keep_ref, got_ref, own_ref, *send_refs):
    total = keep_ref[...].astype(F32) + got_ref[...].astype(F32)
    own_ref[...] = total[0].astype(own_ref.dtype)
    for k, ref in enumerate(send_refs):
        ref[...] = total[k + 1].astype(BF)


def x_kernel(own_ref, *refs):
    got, out = refs[: NX - 1], refs[NX - 1 :]
    total = own_ref[...].astype(F32)
    for ref in got:
        total = total + ref[...].astype(F32)
    rows_conv, rows_expand, taps = 4, 16, 9
    block = rows_conv * NY
    for y, ref in enumerate(out):
        parts = [
            total[tap * block + y * rows_conv : tap * block + (y + 1) * rows_conv] for tap in range(taps)
        ]
        start = taps * block + y * rows_expand
        parts.append(total[start : start + rows_expand])
        ref[...] = jnp.concatenate(parts, axis=0).astype(ref.dtype)


def y_kernel(own_ref, *refs):
    got, out_ref = refs[:-1], refs[-1]
    total = own_ref[...].astype(F32)
    for ref in got:
        total = total + ref[...].astype(F32)
    out_ref[...] = total.astype(out_ref.dtype)


def z_kernel(own_ref, *refs):
    got, (conv_ref, expand_ref) = refs[:-2], refs[-2:]
    total = own_ref[...].astype(F32)
    for ref in got:
        total = total + ref[...].astype(F32)
    rows_conv, width = conv_ref.shape[0], expand_ref.shape[1]
    taps = conv_ref.shape[1] // width
    for tap in range(taps):
        conv_ref[:, tap * width : (tap + 1) * width] = total[tap * rows_conv : (tap + 1) * rows_conv]
    expand_ref[...] = total[taps * rows_conv :]


def call(kernel, outs, *args, scratch=()):
    return pl.pallas_call(
        kernel,
        out_shape=[jax.ShapeDtypeStruct(shape, dtype) for shape, dtype in outs],
        scratch_shapes=list(scratch),
        compiler_params=VMEM,
    )(*args)


def local(features, halting_map, grad_out, weight_reduce, weight_conv, weight_expand):
    samples, rows, cols, chans = features.shape
    width = weight_reduce.shape[0]
    own = samples * rows * cols
    flat_in = features.reshape(own, chans)
    upstream = grad_out.reshape(own, chans)

    hidden, sign, back, up, down = call(
        enter_kernel,
        [((own, width), BF)] * 3 + [((3 * cols, width), BF)] * 2,
        halting_map, flat_in, upstream, weight_reduce, weight_expand,
    )
    from_prev = lax.ppermute(down, "rows", [(i, i + 1) for i in range(NZ - 1)])
    from_next = lax.ppermute(up, "rows", [(i + 1, i) for i in range(NZ - 1)])

    shard = (4 * weight_conv.shape[1] + 16 * width) // width
    part = (NX, NY * shard, width)
    wide = own + 2 * cols
    keep, send, two, gtwo = call(
        middle_kernel,
        [(part, BF), (part, BF), ((own, width), BF), ((wide, width), BF)],
        halting_map, hidden, back, from_prev, from_next, upstream, weight_conv,
        scratch=[pltpu.VMEM((wide, weight_conv.shape[1]), BF)],
    )

    got = lax.ppermute(send, "dp", swap_core())
    out, grad_in = call(
        functools.partial(leave_kernel, cols=cols),
        [((own, chans), BF)] * 2,
        flat_in, upstream, two, gtwo, sign, weight_reduce, weight_conv, weight_expand,
        scratch=[
            pltpu.VMEM((own, weight_conv.shape[1]), BF),
            pltpu.VMEM((weight_conv.shape[1], width), BF),
        ],
    )
    own_x, *sends = call(core_kernel, [(part[1:], F32)] + [(part[1:], BF)] * (NX - 1), keep, got)
    gots = [lax.ppermute(s, "dp", step_x(k + 1)) for k, s in enumerate(sends)]
    small = (shard, width)
    own_y, *sends = call(x_kernel, [(small, F32)] + [(small, BF)] * (NY - 1), own_x, *gots)
    gots = [lax.ppermute(s, "dp", step_y(k + 1)) for k, s in enumerate(sends)]
    (mine,) = call(y_kernel, [(small, F32)], own_y, *gots)
    gots = [lax.ppermute(mine, "rows", step_z(k)) for k in range(1, NZ)]
    grad_conv, grad_expand = call(
        z_kernel, [((4, weight_conv.shape[1]), F32), ((16, width), F32)], mine, *gots
    )
    return (out.reshape(features.shape), grad_in.reshape(features.shape), grad_conv, grad_expand)


def solution(mesh):
    in_specs = (
        P("dp", "rows", None, None),
        P("dp", "rows", None),
        P("dp", "rows", None, None),
        P(),
        P(),
        P(),
    )
    out_specs = (
        P("dp", "rows", None, None),
        P("dp", "rows", None, None),
        P("dp", None),
        P("dp", None),
    )
    return jax.shard_map(local, mesh=mesh, in_specs=in_specs, out_specs=out_specs, check_vma=False)
```

time: 422 us -> 128 us (0.30)
  the two profiles are of different devices: /device:TPU:16 before, /device:TPU:2 now
where the time goes in v1:
time: 128 us; the launch traced here: 127 us
  starting transfers between devices  79.4 us (62%)
  Pallas kernels  20.8 us (16%)
  waiting for transfers between devices  20 us (16%)
  local copies, waits for them, and re-layouts  5.35 us (4%)
    ppermute x7, starting transfers between devices, local(): gots = [lax.ppermute(mine, 'rows', step_z(k)) for k in range(1, NZ)]  32.3 us
    ppermute x7, starting transfers between devices, local(): gots = [lax.ppermute(s, 'dp', step_y(k + 1)) for k, s in enumerate(sends)]  29.2 us
    pallas_call x7, Pallas kernels, call(): pl.pallas_call(kernel, out_shape=[jax.ShapeDtypeStruct(shape, dtype) for...  20.8 us
    ppermute x3, starting transfers between devices, local(): gots = [lax.ppermute(s, 'dp', step_x(k + 1)) for k, s in enumerate(sends)]  10.5 us
    ppermute x3, waiting for transfers between devices, local(): gots = [lax.ppermute(s, 'dp', step_x(k + 1)) for k, s in enumerate(sends)]  8.08 us
    unnamed x41, local copies, waits for them, and re-layouts  5.35 us
    ppermute x1, waiting for transfers between devices, local(): from_next = lax.ppermute(up, 'rows', [(i + 1, i) for i in range(NZ - 1)])  4.57 us
    ppermute x1, starting transfers between devices, local(): from_prev = lax.ppermute(down, 'rows', [(i, i + 1) for i in range(NZ - 1)])  4.27 us
  transfers between devices with their start and end apart: 20, of which 7 were waited for; matrix products, arithmetic and copies ran while one was open for 0% of the time, Pallas kernels for 3%

profile of v1, /device:TPU:2, one launch (start us, length us, event | category | flops | bytes accessed | tf_op | source)
XLA Modules:
  0.0 126.7 jit_solution(4090852262852687162)
XLA Ops:
  0.6 1.3 %copy.11.halt_ref = s32[1,5,64]{2,1,0:T(8,128)} copy(s32[1,5,64]{2,0,1:T(1,128)} %param.7) | data formatting | bytes 2560 | tf_op args[1]
  1.9 3.0 %shard_map.93 = (bf16[320,256]{1,0:T(8,128)(2,1)}, bf16[320,256]{1,0:T(8,128)(2,1)}, bf16[320,256]{1,0:T(8,128)(2,1)}, bf16[192,256]{1,0:T(8,128)(2,1)}, bf16[192,256]{1,0:T(8,128)(2,1)}) custom-call(s32[1,5,64]{2,1,0:T(8,128)} %copy.11.halt_ref, bf16[320,1024]{1,0:T(8,128)(2,1)} %bitcast.7, bf16[320,1024]{1,0:T(8,128)(2,1)} %bitcast.4, ...), custom_call_target="tpu_custom_call" | custom-call | tf_op jit(solution)/shard_map/pallas_call | solution.py:213
  4.9 4.3 %collective-permute-start = (bf16[192,256]{1,0:T(8,128)(2,1)}, bf16[192,256]{1,0:T(8,128)(2,1)S(1)}, u32[]{:S(2)}, u32[]{:S(2)}) collective-permute-start(bf16[192,256]{1,0:T(8,128)(2,1)} %get-tuple-element.31), channel_id=1, source_target_pairs={{0,1},{1,2},{2,3},{3,4},{4,5},{5,6},{6,7},{8,9},{9,10},{10,11},{11... | collective-permute-start | bytes 294920 | tf_op jit(solution)/shard_map/ppermute | solution.py:233
  9.2 1.3 %collective-permute-start.1 = (bf16[192,256]{1,0:T(8,128)(2,1)}, bf16[192,256]{1,0:T(8,128)(2,1)S(1)}, u32[]{:S(2)}, u32[]{:S(2)}) collective-permute-start(bf16[192,256]{1,0:T(8,128)(2,1)} %get-tuple-element.32), channel_id=1, source_target_pairs={{1,0},{2,1},{3,2},{4,3},{5,4},{6,5},{7,6},{9,8},{10,9},{11,10},{12... | collective-permute-start | bytes 294920 | tf_op jit(solution)/shard_map/ppermute | solution.py:234
  10.5 1.2 collective-permute-done.prev_ref
  11.7 4.6 %collective-permute-done.1.next_ref = bf16[192,256]{1,0:T(8,128)(2,1)S(1)} collective-permute-done((bf16[192,256]{1,0:T(8,128)(2,1)}, bf16[192,256]{1,0:T(8,128)(2,1)S(1)}, u32[]{:S(2)}, u32[]{:S(2)}) %collective-permute-start.1) | collective-permute-done | bytes 98336 | tf_op jit(solution)/shard_map/ppermute | solution.py:234
  16.2 0.6 copy-done.5
  16.9 6.0 %shard_map.94 = (bf16[4,416,256]{2,1,0:T(8,128)(2,1)}, bf16[4,416,256]{2,1,0:T(8,128)(2,1)}, bf16[320,256]{1,0:T(8,128)(2,1)}, bf16[448,256]{1,0:T(8,128)(2,1)}) custom-call(s32[1,5,64]{2,1,0:T(8,128)} %copy.11.halt_ref, bf16[320,256]{1,0:T(8,128)(2,1)} %get-tuple-element.29.hidden_ref, bf16[320,256]{1,0:T(8,128)(2,1)} %get-tuple-element.30.back_ref, ...), custom_call_target="tpu_custom_call" | custom-call | tf_op jit(solution)/shard_map/pallas_call | solution.py:213
  22.9 1.9 %collective-permute-start.2 = (bf16[4,416,256]{2,1,0:T(8,128)(2,1)}, bf16[4,416,256]{2,1,0:T(8,128)(2,1)S(1)}, u32[]{:S(2)}, u32[]{:S(2)}) collective-permute-start(bf16[4,416,256]{2,1,0:T(8,128)(2,1)} %get-tuple-element.39), channel_id=1, source_target_pairs={{0,8},{8,0},{16,24},{24,16},{32,40},{40,32},{48,56},{56,48},{64,72... | collective-permute-start | bytes 2555912 | tf_op jit(solution)/shard_map/ppermute | solution.py:246
  24.8 2.6 %collective-permute-done.2.got_ref = bf16[4,416,256]{2,1,0:T(8,128)(2,1)S(1)} collective-permute-done((bf16[4,416,256]{2,1,0:T(8,128)(2,1)}, bf16[4,416,256]{2,1,0:T(8,128)(2,1)S(1)}, u32[]{:S(2)}, u32[]{:S(2)}) %collective-permute-start.2) | collective-permute-done | bytes 852000 | tf_op jit(solution)/shard_map/ppermute | solution.py:246
  27.4 0.9 copy-done
  28.3 2.4 %shard_map.96 = (f32[416,256]{1,0:T(8,128)}, bf16[416,256]{1,0:T(8,128)(2,1)}, bf16[416,256]{1,0:T(8,128)(2,1)}, bf16[416,256]{1,0:T(8,128)(2,1)}) custom-call(bf16[4,416,256]{2,1,0:T(8,128)(2,1)} %get-tuple-element.38.keep_ref, bf16[4,416,256]{2,1,0:T(8,128)(2,1)} %copy-done), custom_call_target="tpu_custom_call" | custom-call | tf_op jit(solution)/shard_map/pallas_call | solution.py:213
  30.7 3.4 %collective-permute-start.3 = (bf16[416,256]{1,0:T(8,128)(2,1)}, bf16[416,256]{1,0:T(8,128)(2,1)S(1)}, u32[]{:S(2)}, u32[]{:S(2)}) collective-permute-start(bf16[416,256]{1,0:T(8,128)(2,1)} %get-tuple-element.41), channel_id=1, source_target_pairs={{0,128},{8,136},{16,144},{24,152},{32,160},{40,168},{48,176},{56,1... | collective-permute-start | bytes 638984 | tf_op jit(solution)/shard_map/ppermute | solution.py:257
  34.1 5.1 %collective-permute-start.4 = (bf16[416,256]{1,0:T(8,128)(2,1)}, bf16[416,256]{1,0:T(8,128)(2,1)S(1)}, u32[]{:S(2)}, u32[]{:S(2)}) collective-permute-start(bf16[416,256]{1,0:T(8,128)(2,1)} %get-tuple-element.42), channel_id=1, source_target_pairs={{0,256},{8,264},{16,272},{24,280},{32,288},{40,296},{48,304},{56,3... | collective-permute-start | bytes 638984 | tf_op jit(solution)/shard_map/ppermute | solution.py:257
  39.2 2.0 %collective-permute-start.5 = (bf16[416,256]{1,0:T(8,128)(2,1)}, bf16[416,256]{1,0:T(8,128)(2,1)S(1)}, u32[]{:S(2)}, u32[]{:S(2)}) collective-permute-start(bf16[416,256]{1,0:T(8,128)(2,1)} %get-tuple-element.43), channel_id=1, source_target_pairs={{0,384},{8,392},{16,400},{24,408},{32,416},{40,424},{48,432},{56,4... | collective-permute-start | bytes 638984 | tf_op jit(solution)/shard_map/ppermute | solution.py:257
  41.2 0.2 collective-permute-done.3.refs_0_
  41.4 4.4 %collective-permute-done.4.refs_1_ = bf16[416,256]{1,0:T(8,128)(2,1)S(1)} collective-permute-done((bf16[416,256]{1,0:T(8,128)(2,1)}, bf16[416,256]{1,0:T(8,128)(2,1)S(1)}, u32[]{:S(2)}, u32[]{:S(2)}) %collective-permute-start.4) | collective-permute-done | bytes 213024 | tf_op jit(solution)/shard_map/ppermute | solution.py:257
  45.9 3.4 %collective-permute-done.5.refs_2_ = bf16[416,256]{1,0:T(8,128)(2,1)S(1)} collective-permute-done((bf16[416,256]{1,0:T(8,128)(2,1)}, bf16[416,256]{1,0:T(8,128)(2,1)S(1)}, u32[]{:S(2)}, u32[]{:S(2)}) %collective-permute-start.5) | collective-permute-done | bytes 213024 | tf_op jit(solution)/shard_map/ppermute | solution.py:257
  49.3 0.0 copy-done.2
  49.3 0.7 copy-done.3
  50.0 2.0 %shard_map.97 = (f32[52,256]{1,0:T(8,128)}, bf16[52,256]{1,0:T(8,128)(2,1)}, bf16[52,256]{1,0:T(8,128)(2,1)}, bf16[52,256]{1,0:T(8,128)(2,1)}, bf16[52,256]{1,0:...) custom-call(f32[416,256]{1,0:T(8,128)} %get-tuple-element.40.own_ref, ...), custom_call_target="tpu_custom_call" | custom-call | tf_op jit(solution)/shard_map/pallas_call | solution.py:213
  52.0 6.9 %collective-permute-start.10 = (bf16[52,256]{1,0:T(8,128)(2,1)}, bf16[52,256]{1,0:T(8,128)(2,1)S(1)}, u32[]{:S(2)}, u32[]{:S(2)}) collective-permute-start(bf16[52,256]{1,0:T(8,128)(2,1)} %get-tuple-element.49), channel_id=1, source_target_pairs={{0,80},{8,88},{16,96},{24,104},{32,112},{40,120},{48,0},{56,8},{64... | collective-permute-start | bytes 79880 | tf_op jit(solution)/shard_map/ppermute | solution.py:260
  58.9 3.1 %collective-permute-start.11 = (bf16[52,256]{1,0:T(8,128)(2,1)}, bf16[52,256]{1,0:T(8,128)(2,1)S(1)}, u32[]{:S(2)}, u32[]{:S(2)}) collective-permute-start(bf16[52,256]{1,0:T(8,128)(2,1)} %get-tuple-element.50), channel_id=1, source_target_pairs={{0,96},{8,104},{16,112},{24,120},{32,0},{40,8},{48,16},{56,24},{64... | collective-permute-start | bytes 79880 | tf_op jit(solution)/shard_map/ppermute | solution.py:260
  62.0 2.4 %collective-permute-start.12 = (bf16[52,256]{1,0:T(8,128)(2,1)}, bf16[52,256]{1,0:T(8,128)(2,1)S(1)}, u32[]{:S(2)}, u32[]{:S(2)}) collective-permute-start(bf16[52,256]{1,0:T(8,128)(2,1)} %get-tuple-element.51), channel_id=1, source_target_pairs={{0,112},{8,120},{16,0},{24,8},{32,16},{40,24},{48,32},{56,40},{64,... | collective-permute-start | bytes 79880 | tf_op jit(solution)/shard_map/ppermute | solution.py:260
  64.4 3.5 %collective-permute-start.6 = (bf16[52,256]{1,0:T(8,128)(2,1)}, bf16[52,256]{1,0:T(8,128)(2,1)S(1)}, u32[]{:S(2)}, u32[]{:S(2)}) collective-permute-start(bf16[52,256]{1,0:T(8,128)(2,1)} %get-tuple-element.45), channel_id=1, source_target_pairs={{0,16},{8,24},{16,32},{24,40},{32,48},{40,56},{48,64},{56,72},{64,... | collective-permute-start | bytes 79880 | tf_op jit(solution)/shard_map/ppermute | solution.py:260
  67.9 3.6 %collective-permute-start.7 = (bf16[52,256]{1,0:T(8,128)(2,1)}, bf16[52,256]{1,0:T(8,128)(2,1)S(1)}, u32[]{:S(2)}, u32[]{:S(2)}) collective-permute-start(bf16[52,256]{1,0:T(8,128)(2,1)} %get-tuple-element.46), channel_id=1, source_target_pairs={{0,32},{8,40},{16,48},{24,56},{32,64},{40,72},{48,80},{56,88},{64,... | collective-permute-start | bytes 79880 | tf_op jit(solution)/shard_map/ppermute | solution.py:260
  71.5 0.0 collective-permute-done.10.refs_4_
  71.5 0.0 copy-start.13
  71.5 3.4 %collective-permute-start.8 = (bf16[52,256]{1,0:T(8,128)(2,1)}, bf16[52,256]{1,0:T(8,128)(2,1)S(1)}, u32[]{:S(2)}, u32[]{:S(2)}) collective-permute-start(bf16[52,256]{1,0:T(8,128)(2,1)} %get-tuple-element.47), channel_id=1, source_target_pairs={{0,48},{8,56},{16,64},{24,72},{32,80},{40,88},{48,96},{56,104},{64... | collective-permute-start | bytes 79880 | tf_op jit(solution)/shard_map/ppermute | solution.py:260
  74.9 0.0 collective-permute-done.11.refs_5_
  74.9 6.3 %collective-permute-start.9 = (bf16[52,256]{1,0:T(8,128)(2,1)}, bf16[52,256]{1,0:T(8,128)(2,1)S(1)}, u32[]{:S(2)}, u32[]{:S(2)}) collective-permute-start(bf16[52,256]{1,0:T(8,128)(2,1)} %get-tuple-element.48), channel_id=1, source_target_pairs={{0,64},{8,72},{16,80},{24,88},{32,96},{40,104},{48,112},{56,120},{... | collective-permute-start | bytes 79880 | tf_op jit(solution)/shard_map/ppermute | solution.py:260
  81.2 0.0 collective-permute-done.12.refs_6_
  81.2 0.0 copy-start.15
  81.2 0.0 collective-permute-done.6.refs_0_
  81.2 0.0 copy-start.16
  81.3 0.0 collective-permute-done.7.refs_1_
  81.3 0.0 copy-start.17
  81.3 0.0 collective-permute-done.8.refs_2_
  81.3 0.0 copy-start.18
  81.3 3.6 %collective-permute-done.9.refs_3_ = bf16[52,256]{1,0:T(8,128)(2,1)S(1)} collective-permute-done((bf16[52,256]{1,0:T(8,128)(2,1)}, bf16[52,256]{1,0:T(8,128)(2,1)S(1)}, u32[]{:S(2)}, u32[]{:S(2)}) %collective-permute-start.9) | collective-permute-done | bytes 26656 | tf_op jit(solution)/shard_map/ppermute | solution.py:260
  84.9 0.0 copy-done.14
  85.0 0.6 copy-done.19
  85.5 1.5 %shard_map.98.own_ref = f32[52,256]{1,0:T(8,128)} custom-call(f32[52,256]{1,0:T(8,128)} %get-tuple-element.44.own_ref, bf16[52,256]{1,0:T(8,128)(2,1)} %copy-done.16, bf16[52,256]{1,0:T(8,128)(2,1)} %copy-done.17, bf16[52,256]{1,0:T(8,128)(2,1)} %copy-done.18, bf16[52,256]{1,0:T(8,128)(2,1)} %copy-done.19, bf16[52,256]{1,0:T(8,128)(2,1)} %copy-done.13, ...), custom_call_target="tpu_custom_call" | custom-call | tf_op jit(solution)/shard_map/pallas_call | solution.py:213
  87.0 4.3 %collective-permute-start.13 = (f32[52,256]{1,0:T(8,128)}, f32[52,256]{1,0:T(8,128)S(1)}, u32[]{:S(2)}, u32[]{:S(2)}) collective-permute-start(f32[52,256]{1,0:T(8,128)} %shard_map.98.own_ref), channel_id=1, source_target_pairs={{0,1},{1,2},{2,3},{3,4},{4,5},{5,6},{6,7},{7,0},{8,9},{9,10},{10,1... | collective-permute-start | bytes 159752 | tf_op jit(solution)/shard_map/ppermute | solution.py:262
  91.3 8.2 %collective-permute-start.14 = (f32[52,256]{1,0:T(8,128)}, f32[52,256]{1,0:T(8,128)S(1)}, u32[]{:S(2)}, u32[]{:S(2)}) collective-permute-start(f32[52,256]{1,0:T(8,128)} %shard_map.98.own_ref), channel_id=1, source_target_pairs={{0,2},{1,3},{2,4},{3,5},{4,6},{5,7},{6,0},{7,1},{8,10},{9,11},{10,... | collective-permute-start | bytes 159752 | tf_op jit(solution)/shard_map/ppermute | solution.py:262
  99.5 4.0 %collective-permute-start.15 = (f32[52,256]{1,0:T(8,128)}, f32[52,256]{1,0:T(8,128)S(1)}, u32[]{:S(2)}, u32[]{:S(2)}) collective-permute-start(f32[52,256]{1,0:T(8,128)} %shard_map.98.own_ref), channel_id=1, source_target_pairs={{0,3},{1,4},{2,5},{3,6},{4,7},{5,0},{6,1},{7,2},{8,11},{9,12},{10,... | collective-permute-start | bytes 159752 | tf_op jit(solution)/shard_map/ppermute | solution.py:262
  103.5 3.1 %collective-permute-start.16 = (f32[52,256]{1,0:T(8,128)}, f32[52,256]{1,0:T(8,128)S(1)}, u32[]{:S(2)}, u32[]{:S(2)}) collective-permute-start(f32[52,256]{1,0:T(8,128)} %shard_map.98.own_ref), channel_id=1, source_target_pairs={{0,4},{1,5},{2,6},{3,7},{4,0},{5,1},{6,2},{7,3},{8,12},{9,13},{10,... | collective-permute-start | bytes 159752 | tf_op jit(solution)/shard_map/ppermute | solution.py:262
  106.6 5.2 %collective-permute-start.17 = (f32[52,256]{1,0:T(8,128)}, f32[52,256]{1,0:T(8,128)S(1)}, u32[]{:S(2)}, u32[]{:S(2)}) collective-permute-start(f32[52,256]{1,0:T(8,128)} %shard_map.98.own_ref), channel_id=1, source_target_pairs={{0,5},{1,6},{2,7},{3,0},{4,1},{5,2},{6,3},{7,4},{8,13},{9,14},{10,... | collective-permute-start | bytes 159752 | tf_op jit(solution)/shard_map/ppermute | solution.py:262
  111.8 0.0 collective-permute-done.13.refs_0_
  111.8 5.1 %collective-permute-start.18 = (f32[52,256]{1,0:T(8,128)}, f32[52,256]{1,0:T(8,128)S(1)}, u32[]{:S(2)}, u32[]{:S(2)}) collective-permute-start(f32[52,256]{1,0:T(8,128)} %shard_map.98.own_ref), channel_id=1, source_target_pairs={{0,6},{1,7},{2,0},{3,1},{4,2},{5,3},{6,4},{7,5},{8,14},{9,15},{10,... | collective-permute-start | bytes 159752 | tf_op jit(solution)/shard_map/ppermute | solution.py:262
  116.9 0.0 collective-permute-done.14.refs_1_
  117.0 2.5 %collective-permute-start.19 = (f32[52,256]{1,0:T(8,128)}, f32[52,256]{1,0:T(8,128)S(1)}, u32[]{:S(2)}, u32[]{:S(2)}) collective-permute-start(f32[52,256]{1,0:T(8,128)} %shard_map.98.own_ref), channel_id=1, source_target_pairs={{0,7},{1,0},{2,1},{3,2},{4,3},{5,4},{6,5},{7,6},{8,15},{9,8},{10,9... | collective-permute-start | bytes 159752 | tf_op jit(solution)/shard_map/ppermute | solution.py:262
  119.4 4.3 %shard_map.95 = (bf16[320,1024]{1,0:T(8,128)(2,1)}, bf16[320,1024]{1,0:T(8,128)(2,1)}) custom-call(bf16[320,1024]{1,0:T(8,128)(2,1)} %bitcast.8, bf16[320,1024]{1,0:T(8,128)(2,1)} %bitcast.6, bf16[320,256]{1,0:T(8,128)(2,1)} %get-tuple-element.33.two_ref, bf16[448,256]{1,0:T(8,128)(2,1)} %get-tuple-element.34.gtwo_ref, ...), custom_call_target="tpu_custom_call" | custom-call | tf_op jit(solution)/shard_map/pallas_call | solution.py:213
  123.7 0.0 collective-permute-done.15.refs_2_
  123.7 0.0 collective-permute-done.16.refs_3_
  123.7 0.0 collective-permute-done.17.refs_4_
  123.7 0.0 collective-permute-done.18.refs_5_
  123.8 0.0 collective-permute-done.19.refs_6_
  123.8 0.5 copy-done.8
  124.3 0.0 copy-done.9
  124.3 0.0 copy-done.10
  124.4 0.0 copy-done.11
  124.4 0.6 copy-done.12
  125.0 1.7 %shard_map.99 = (f32[4,2304]{1,0:T(4,128)}, f32[16,256]{1,0:T(8,128)}) custom-call(f32[52,256]{1,0:T(8,128)} %shard_map.98.own_ref, f32[52,256]{1,0:T(8,128)} %copy-done.6, f32[52,256]{1,0:T(8,128)} %copy-done.7, f32[52,256]{1,0:T(8,128)} %copy-done.8, f32[52,256]{1,0:T(8,128)} %copy-done.9, f32[52,256]{1,0:T(8,128)} %copy-done.10, f32[52,256]{1,0:T(8,128)} %copy-done.11, ...), custom_call_target="tpu_custom_call" | custom-call | tf_op jit(solution)/shard_map/pallas_call | solution.py:213
  (24 shorter events, 0.0 us)
Async XLA Ops:
  4.9 6.8 %collective-permute-start = (bf16[192,256]{1,0:T(8,128)(2,1)}, bf16[192,256]{1,0:T(8,128)(2,1)S(1)}, u32[]{:S(2)}, u32[]{:S(2)}) collective-permute-start(bf16[192,256]{1,0:T(8,128)(2,1)} %get-tuple-element.31), channel_id=1, source_target_pairs={{0,1},{1,2},{2,3},{3,4},{4,5},{5,6},{6,7},{8,9},{9,10},{10,11},{11... | collective-permute-start | bytes 294920 | tf_op jit(solution)/shard_map/ppermute | solution.py:233
  9.2 7.1 %collective-permute-start.1 = (bf16[192,256]{1,0:T(8,128)(2,1)}, bf16[192,256]{1,0:T(8,128)(2,1)S(1)}, u32[]{:S(2)}, u32[]{:S(2)}) collective-permute-start(bf16[192,256]{1,0:T(8,128)(2,1)} %get-tuple-element.32), channel_id=1, source_target_pairs={{1,0},{2,1},{3,2},{4,3},{5,4},{6,5},{7,6},{9,8},{10,9},{11,10},{12... | collective-permute-start | bytes 294920 | tf_op jit(solution)/shard_map/ppermute | solution.py:234
  11.7 4.6 %copy-start.4 = (bf16[192,256]{1,0:T(8,128)(2,1)}, bf16[192,256]{1,0:T(8,128)(2,1)S(1)}, u32[]{:S(2)}) copy-start(bf16[192,256]{1,0:T(8,128)(2,1)S(1)} %collective-permute-done.prev_ref) | copy-start | bytes 294916
  16.2 0.6 copy-start.5
  22.9 4.5 %collective-permute-start.2 = (bf16[4,416,256]{2,1,0:T(8,128)(2,1)}, bf16[4,416,256]{2,1,0:T(8,128)(2,1)S(1)}, u32[]{:S(2)}, u32[]{:S(2)}) collective-permute-start(bf16[4,416,256]{2,1,0:T(8,128)(2,1)} %get-tuple-element.39), channel_id=1, source_target_pairs={{0,8},{8,0},{16,24},{24,16},{32,40},{40,32},{48,56},{56,48},{64,72... | collective-permute-start | bytes 2555912 | tf_op jit(solution)/shard_map/ppermute | solution.py:246
  27.4 0.9 copy-start
  30.7 10.7 %collective-permute-start.3 = (bf16[416,256]{1,0:T(8,128)(2,1)}, bf16[416,256]{1,0:T(8,128)(2,1)S(1)}, u32[]{:S(2)}, u32[]{:S(2)}) collective-permute-start(bf16[416,256]{1,0:T(8,128)(2,1)} %get-tuple-element.41), channel_id=1, source_target_pairs={{0,128},{8,136},{16,144},{24,152},{32,160},{40,168},{48,176},{56,1... | collective-permute-start | bytes 638984 | tf_op jit(solution)/shard_map/ppermute | solution.py:257
  34.1 11.7 %collective-permute-start.4 = (bf16[416,256]{1,0:T(8,128)(2,1)}, bf16[416,256]{1,0:T(8,128)(2,1)S(1)}, u32[]{:S(2)}, u32[]{:S(2)}) collective-permute-start(bf16[416,256]{1,0:T(8,128)(2,1)} %get-tuple-element.42), channel_id=1, source_target_pairs={{0,256},{8,264},{16,272},{24,280},{32,288},{40,296},{48,304},{56,3... | collective-permute-start | bytes 638984 | tf_op jit(solution)/shard_map/ppermute | solution.py:257
  39.2 10.1 %collective-permute-start.5 = (bf16[416,256]{1,0:T(8,128)(2,1)}, bf16[416,256]{1,0:T(8,128)(2,1)S(1)}, u32[]{:S(2)}, u32[]{:S(2)}) collective-permute-start(bf16[416,256]{1,0:T(8,128)(2,1)} %get-tuple-element.43), channel_id=1, source_target_pairs={{0,384},{8,392},{16,400},{24,408},{32,416},{40,424},{48,432},{56,4... | collective-permute-start | bytes 638984 | tf_op jit(solution)/shard_map/ppermute | solution.py:257
  41.4 7.9 %copy-start.1 = (bf16[416,256]{1,0:T(8,128)(2,1)}, bf16[416,256]{1,0:T(8,128)(2,1)S(1)}, u32[]{:S(2)}) copy-start(bf16[416,256]{1,0:T(8,128)(2,1)S(1)} %collective-permute-done.3.refs_0_) | copy-start | bytes 638980
  45.9 3.4 %copy-start.2 = (bf16[416,256]{1,0:T(8,128)(2,1)}, bf16[416,256]{1,0:T(8,128)(2,1)S(1)}, u32[]{:S(2)}) copy-start(bf16[416,256]{1,0:T(8,128)(2,1)S(1)} %collective-permute-done.4.refs_1_) | copy-start | bytes 638980
  49.3 0.7 copy-start.3
  52.0 19.6 %collective-permute-start.10 = (bf16[52,256]{1,0:T(8,128)(2,1)}, bf16[52,256]{1,0:T(8,128)(2,1)S(1)}, u32[]{:S(2)}, u32[]{:S(2)}) collective-permute-start(bf16[52,256]{1,0:T(8,128)(2,1)} %get-tuple-element.49), channel_id=1, source_target_pairs={{0,80},{8,88},{16,96},{24,104},{32,112},{40,120},{48,0},{56,8},{64... | collective-permute-start | bytes 79880 | tf_op jit(solution)/shard_map/ppermute | solution.py:260
  58.9 16.0 %collective-permute-start.11 = (bf16[52,256]{1,0:T(8,128)(2,1)}, bf16[52,256]{1,0:T(8,128)(2,1)S(1)}, u32[]{:S(2)}, u32[]{:S(2)}) collective-permute-start(bf16[52,256]{1,0:T(8,128)(2,1)} %get-tuple-element.50), channel_id=1, source_target_pairs={{0,96},{8,104},{16,112},{24,120},{32,0},{40,8},{48,16},{56,24},{64... | collective-permute-start | bytes 79880 | tf_op jit(solution)/shard_map/ppermute | solution.py:260
  62.0 19.2 %collective-permute-start.12 = (bf16[52,256]{1,0:T(8,128)(2,1)}, bf16[52,256]{1,0:T(8,128)(2,1)S(1)}, u32[]{:S(2)}, u32[]{:S(2)}) collective-permute-start(bf16[52,256]{1,0:T(8,128)(2,1)} %get-tuple-element.51), channel_id=1, source_target_pairs={{0,112},{8,120},{16,0},{24,8},{32,16},{40,24},{48,32},{56,40},{64,... | collective-permute-start | bytes 79880 | tf_op jit(solution)/shard_map/ppermute | solution.py:260
  64.4 16.8 %collective-permute-start.6 = (bf16[52,256]{1,0:T(8,128)(2,1)}, bf16[52,256]{1,0:T(8,128)(2,1)S(1)}, u32[]{:S(2)}, u32[]{:S(2)}) collective-permute-start(bf16[52,256]{1,0:T(8,128)(2,1)} %get-tuple-element.45), channel_id=1, source_target_pairs={{0,16},{8,24},{16,32},{24,40},{32,48},{40,56},{48,64},{56,72},{64,... | collective-permute-start | bytes 79880 | tf_op jit(solution)/shard_map/ppermute | solution.py:260
  67.9 13.4 %collective-permute-start.7 = (bf16[52,256]{1,0:T(8,128)(2,1)}, bf16[52,256]{1,0:T(8,128)(2,1)S(1)}, u32[]{:S(2)}, u32[]{:S(2)}) collective-permute-start(bf16[52,256]{1,0:T(8,128)(2,1)} %get-tuple-element.46), channel_id=1, source_target_pairs={{0,32},{8,40},{16,48},{24,56},{32,64},{40,72},{48,80},{56,88},{64,... | collective-permute-start | bytes 79880 | tf_op jit(solution)/shard_map/ppermute | solution.py:260
  71.5 13.4 %copy-start.13 = (bf16[52,256]{1,0:T(8,128)(2,1)}, bf16[52,256]{1,0:T(8,128)(2,1)S(1)}, u32[]{:S(2)}) copy-start(bf16[52,256]{1,0:T(8,128)(2,1)S(1)} %collective-permute-done.10.refs_4_) | copy-start | bytes 79876
  71.5 9.7 %collective-permute-start.8 = (bf16[52,256]{1,0:T(8,128)(2,1)}, bf16[52,256]{1,0:T(8,128)(2,1)S(1)}, u32[]{:S(2)}, u32[]{:S(2)}) collective-permute-start(bf16[52,256]{1,0:T(8,128)(2,1)} %get-tuple-element.47), channel_id=1, source_target_pairs={{0,48},{8,56},{16,64},{24,72},{32,80},{40,88},{48,96},{56,104},{64... | collective-permute-start | bytes 79880 | tf_op jit(solution)/shard_map/ppermute | solution.py:260
  74.9 10.0 %copy-start.14 = (bf16[52,256]{1,0:T(8,128)(2,1)}, bf16[52,256]{1,0:T(8,128)(2,1)S(1)}, u32[]{:S(2)}) copy-start(bf16[52,256]{1,0:T(8,128)(2,1)S(1)} %collective-permute-done.11.refs_5_) | copy-start | bytes 79876
  74.9 10.0 %collective-permute-start.9 = (bf16[52,256]{1,0:T(8,128)(2,1)}, bf16[52,256]{1,0:T(8,128)(2,1)S(1)}, u32[]{:S(2)}, u32[]{:S(2)}) collective-permute-start(bf16[52,256]{1,0:T(8,128)(2,1)} %get-tuple-element.48), channel_id=1, source_target_pairs={{0,64},{8,72},{16,80},{24,88},{32,96},{40,104},{48,112},{56,120},{... | collective-permute-start | bytes 79880 | tf_op jit(solution)/shard_map/ppermute | solution.py:260
  81.2 3.7 %copy-start.15 = (bf16[52,256]{1,0:T(8,128)(2,1)}, bf16[52,256]{1,0:T(8,128)(2,1)S(1)}, u32[]{:S(2)}) copy-start(bf16[52,256]{1,0:T(8,128)(2,1)S(1)} %collective-permute-done.12.refs_6_) | copy-start | bytes 79876
  81.2 3.7 %copy-start.16 = (bf16[52,256]{1,0:T(8,128)(2,1)}, bf16[52,256]{1,0:T(8,128)(2,1)S(1)}, u32[]{:S(2)}) copy-start(bf16[52,256]{1,0:T(8,128)(2,1)S(1)} %collective-permute-done.6.refs_0_) | copy-start | bytes 79876
  81.3 3.7 %copy-start.17 = (bf16[52,256]{1,0:T(8,128)(2,1)}, bf16[52,256]{1,0:T(8,128)(2,1)S(1)}, u32[]{:S(2)}) copy-start(bf16[52,256]{1,0:T(8,128)(2,1)S(1)} %collective-permute-done.7.refs_1_) | copy-start | bytes 79876
  81.3 3.7 %copy-start.18 = (bf16[52,256]{1,0:T(8,128)(2,1)}, bf16[52,256]{1,0:T(8,128)(2,1)S(1)}, u32[]{:S(2)}) copy-start(bf16[52,256]{1,0:T(8,128)(2,1)S(1)} %collective-permute-done.8.refs_2_) | copy-start | bytes 79876
  84.9 0.6 copy-start.19
  87.0 24.7 %collective-permute-start.13 = (f32[52,256]{1,0:T(8,128)}, f32[52,256]{1,0:T(8,128)S(1)}, u32[]{:S(2)}, u32[]{:S(2)}) collective-permute-start(f32[52,256]{1,0:T(8,128)} %shard_map.98.own_ref), channel_id=1, source_target_pairs={{0,1},{1,2},{2,3},{3,4},{4,5},{5,6},{6,7},{7,0},{8,9},{9,10},{10,1... | collective-permute-start | bytes 159752 | tf_op jit(solution)/shard_map/ppermute | solution.py:262
  91.3 25.6 %collective-permute-start.14 = (f32[52,256]{1,0:T(8,128)}, f32[52,256]{1,0:T(8,128)S(1)}, u32[]{:S(2)}, u32[]{:S(2)}) collective-permute-start(f32[52,256]{1,0:T(8,128)} %shard_map.98.own_ref), channel_id=1, source_target_pairs={{0,2},{1,3},{2,4},{3,5},{4,6},{5,7},{6,0},{7,1},{8,10},{9,11},{10,... | collective-permute-start | bytes 159752 | tf_op jit(solution)/shard_map/ppermute | solution.py:262
  99.5 24.2 %collective-permute-start.15 = (f32[52,256]{1,0:T(8,128)}, f32[52,256]{1,0:T(8,128)S(1)}, u32[]{:S(2)}, u32[]{:S(2)}) collective-permute-start(f32[52,256]{1,0:T(8,128)} %shard_map.98.own_ref), channel_id=1, source_target_pairs={{0,3},{1,4},{2,5},{3,6},{4,7},{5,0},{6,1},{7,2},{8,11},{9,12},{10,... | collective-permute-start | bytes 159752 | tf_op jit(solution)/shard_map/ppermute | solution.py:262
  103.5 20.2 %collective-permute-start.16 = (f32[52,256]{1,0:T(8,128)}, f32[52,256]{1,0:T(8,128)S(1)}, u32[]{:S(2)}, u32[]{:S(2)}) collective-permute-start(f32[52,256]{1,0:T(8,128)} %shard_map.98.own_ref), channel_id=1, source_target_pairs={{0,4},{1,5},{2,6},{3,7},{4,0},{5,1},{6,2},{7,3},{8,12},{9,13},{10,... | collective-permute-start | bytes 159752 | tf_op jit(solution)/shard_map/ppermute | solution.py:262
  106.6 17.1 %collective-permute-start.17 = (f32[52,256]{1,0:T(8,128)}, f32[52,256]{1,0:T(8,128)S(1)}, u32[]{:S(2)}, u32[]{:S(2)}) collective-permute-start(f32[52,256]{1,0:T(8,128)} %shard_map.98.own_ref), channel_id=1, source_target_pairs={{0,5},{1,6},{2,7},{3,0},{4,1},{5,2},{6,3},{7,4},{8,13},{9,14},{10,... | collective-permute-start | bytes 159752 | tf_op jit(solution)/shard_map/ppermute | solution.py:262
  111.8 11.9 %copy-start.6 = (f32[52,256]{1,0:T(8,128)}, f32[52,256]{1,0:T(8,128)S(1)}, u32[]{:S(2)}) copy-start(f32[52,256]{1,0:T(8,128)S(1)} %collective-permute-done.13.refs_0_) | copy-start | bytes 159748
  111.8 11.9 %collective-permute-start.18 = (f32[52,256]{1,0:T(8,128)}, f32[52,256]{1,0:T(8,128)S(1)}, u32[]{:S(2)}, u32[]{:S(2)}) collective-permute-start(f32[52,256]{1,0:T(8,128)} %shard_map.98.own_ref), channel_id=1, source_target_pairs={{0,6},{1,7},{2,0},{3,1},{4,2},{5,3},{6,4},{7,5},{8,14},{9,15},{10,... | collective-permute-start | bytes 159752 | tf_op jit(solution)/shard_map/ppermute | solution.py:262
  116.9 6.7 %copy-start.7 = (f32[52,256]{1,0:T(8,128)}, f32[52,256]{1,0:T(8,128)S(1)}, u32[]{:S(2)}) copy-start(f32[52,256]{1,0:T(8,128)S(1)} %collective-permute-done.14.refs_1_) | copy-start | bytes 159748
  117.0 6.8 %collective-permute-start.19 = (f32[52,256]{1,0:T(8,128)}, f32[52,256]{1,0:T(8,128)S(1)}, u32[]{:S(2)}, u32[]{:S(2)}) collective-permute-start(f32[52,256]{1,0:T(8,128)} %shard_map.98.own_ref), channel_id=1, source_target_pairs={{0,7},{1,0},{2,1},{3,2},{4,3},{5,4},{6,5},{7,6},{8,15},{9,8},{10,9... | collective-permute-start | bytes 159752 | tf_op jit(solution)/shard_map/ppermute | solution.py:262
  123.7 0.6 copy-start.8
  123.7 0.6 copy-start.9
  123.7 0.6 copy-start.10
  123.8 0.6 copy-start.11
  124.4 0.6 copy-start.12

commit v2 on v1

v2 whole, which is shorter than its diff:
```python
import functools

import jax
import jax.numpy as jnp
from jax import lax
from jax.experimental import pallas as pl
from jax.experimental.pallas import tpu as pltpu
from jax.sharding import Mesh, PartitionSpec as P

UNIT = 5
BF = jnp.bfloat16
F32 = jnp.float32

AXES = ("x", "y_hi", "y_lo", "core", "rows")
NX, NH, NL, NC, NZ = SIZES = (4, 4, 2, 2, 8)
DP = AXES[:4]
VMEM_LIMIT = pltpu.CompilerParams(vmem_limit_bytes=56 * 1024 * 1024)


def dp_of(x, hi, lo, core):
    return ((x * NH + hi) * NL + lo) * NC + core


def dot(left, right, left_dim, right_dim):
    return lax.dot_general(
        left, right, (((left_dim,), (right_dim,)), ((), ())), preferred_element_type=F32
    )


def active_column(halt_ref):
    rows, _, cols = halt_ref.shape
    at_row = lax.broadcasted_iota(jnp.int32, (cols, cols), 0)
    at_col = lax.broadcasted_iota(jnp.int32, (cols, cols), 1)
    parts = [
        jnp.sum(
            jnp.where((at_row == at_col) & (halt_ref[r] > UNIT), 1.0, 0.0), axis=1, keepdims=True
        )
        for r in range(rows)
    ]
    return jnp.concatenate(parts, axis=0)


def neighbours(cells, cols):
    count = cells.shape[0]
    wide = cells.astype(F32)
    col = lax.rem(lax.broadcasted_iota(jnp.int32, (count, 1), 0), cols)
    left = jnp.where(col == 0, 0.0, pltpu.roll(wide, 1, 0))
    right = jnp.where(col == cols - 1, 0.0, pltpu.roll(wide, count - 1, 0))
    return left.astype(BF), right.astype(BF)


def enter_kernel(
    halt_ref, feat_ref, grad_ref, reduce_ref, expand_ref,
    hidden_ref, sign_ref, back_ref, up_ref, down_ref,
):
    rows, _, cols = halt_ref.shape
    pre_one = dot(feat_ref[...], reduce_ref[...], 1, 1)
    hidden = jnp.maximum(pre_one, 0.0).astype(BF)
    hidden_ref[...] = hidden
    sign_ref[...] = (pre_one > 0).astype(F32).astype(BF)
    back = (active_column(halt_ref) * dot(grad_ref[...], expand_ref[...], 1, 0)).astype(BF)
    back_ref[...] = back
    up_ref[0 : 2 * cols, :] = hidden[0 : 2 * cols]
    up_ref[2 * cols :, :] = back[0:cols]
    down_ref[0 : 2 * cols, :] = hidden[(rows - 2) * cols :]
    down_ref[2 * cols :, :] = back[(rows - 1) * cols :]


def middle_kernel(
    halt_ref, hidden_ref, back_ref, prev_ref, next_ref, grad_ref, conv_ref,
    keep_ref, send_ref, two_ref, gtwo_ref, columns_ref,
):
    rows, _, cols = halt_ref.shape
    own = rows * cols
    width = hidden_ref.shape[1]
    core = lax.axis_index("core")

    padded = jnp.concatenate([prev_ref[0 : 2 * cols], hidden_ref[...], next_ref[0 : 2 * cols]], axis=0)
    left, right = neighbours(padded, cols)
    wide = own + 2 * cols
    for a in range(3):
        for b, shifted in enumerate((left, padded, right)):
            tap = 3 * a + b
            columns_ref[:, tap * width : (tap + 1) * width] = shifted[a * cols : a * cols + wide]
    pre_two = dot(columns_ref[...], conv_ref[...], 1, 1)
    back = jnp.concatenate([prev_ref[2 * cols :], back_ref[...], next_ref[2 * cols :]], axis=0)
    grad_two = jnp.where(pre_two > 0, back.astype(F32), 0.0).astype(BF)
    gtwo_ref[...] = grad_two
    active = active_column(halt_ref)
    hidden_two = (active * jnp.maximum(pre_two[cols : cols + own], 0.0)).astype(BF)
    two_ref[...] = hidden_two

    shape = (width, width)
    per_dp = width // (NX * NH * NL * NC)
    at = lax.broadcasted_iota(jnp.int32, shape, 0)
    j, hi, lo = at % per_dp, (at // per_dp) % NH, (at // (per_dp * NH)) % NL
    x, c = (at // (per_dp * NH * NL)) % NX, at // (per_dp * NH * NL * NX)
    wanted = dp_of(x, hi, lo, c ^ core) * per_dp + j
    shuffle = (lax.broadcasted_iota(jnp.int32, shape, 1) == wanted).astype(F32).astype(BF)
    grad_rows = dot(shuffle, grad_two[cols : cols + own], 1, 1).astype(BF)
    conv_part = dot(grad_rows, columns_ref[cols : cols + own, :], 1, 0).astype(BF)
    tall, lanes = per_dp * NH, conv_part.shape[1]
    for group in range(NX * NL):
        keep_ref[group, :, 0:lanes] = conv_part[group * tall : (group + 1) * tall]
        other = NX * NL + group
        send_ref[group, :, 0:lanes] = conv_part[other * tall : (other + 1) * tall]
    expand_part = dot(grad_ref[...], hidden_two, 0, 0).astype(BF)
    per_dp = expand_part.shape[0] // (NX * NH * NL * NC)
    for x in range(NX):
        for lo in range(NL):
            for hi in range(NH):
                first = dp_of(x, hi, lo, 0) * per_dp
                zero, one = (expand_part[first + i * per_dp : first + (i + 1) * per_dp] for i in (0, 1))
                at = slice(lanes + hi * width, lanes + (hi + 1) * width)
                keep_ref[x * NL + lo, :, at] = jnp.where(core == 0, zero, one)
                send_ref[x * NL + lo, :, at] = jnp.where(core == 0, one, zero)


def leave_kernel(
    feat_ref, grad_ref, two_ref, gtwo_ref, sign_ref, reduce_ref, conv_ref, expand_ref,
    out_ref, gin_ref, columns_ref, stacked_ref, *, cols,
):
    own = feat_ref.shape[0]
    width = two_ref.shape[1]
    out_ref[...] = (feat_ref[...].astype(F32) + dot(two_ref[...], expand_ref[...], 1, 1)).astype(BF)
    grad_two = gtwo_ref[...]
    left, right = neighbours(grad_two, cols)
    for a in range(3):
        for b, shifted in enumerate((right, grad_two, left)):
            tap = 3 * a + b
            at = slice(tap * width, (tap + 1) * width)
            columns_ref[:, at] = shifted[(2 - a) * cols : (2 - a) * cols + own]
            stacked_ref[at, :] = conv_ref[:, at]
    grad_hidden = dot(columns_ref[...], stacked_ref[...], 1, 0)
    grad_one = (grad_hidden * sign_ref[...].astype(F32)).astype(BF)
    gin_ref[...] = (grad_ref[...].astype(F32) + dot(grad_one, reduce_ref[...], 1, 0)).astype(BF)


def in_vmem(array):
    return pltpu.with_memory_space_constraint(array, pltpu.VMEM)


def call(kernel, outs, *args, scratch=(), keep=True):
    shape_of = pltpu.VMEM if keep else jax.ShapeDtypeStruct
    return pl.pallas_call(
        kernel,
        out_shape=[shape_of(shape, dtype) for shape, dtype in outs],
        scratch_shapes=list(scratch),
        compiler_params=VMEM_LIMIT,
    )(*[in_vmem(a) for a in args])


def local(features, halting_map, grad_out, weight_reduce, weight_conv, weight_expand):
    samples, rows, cols, chans = features.shape
    width = weight_reduce.shape[0]
    taps = weight_conv.shape[1]
    own = samples * rows * cols
    flat_in = features.reshape(own, chans)
    upstream = grad_out.reshape(own, chans)
    halting = halting_map.reshape(samples * rows, 1, cols)

    hidden, sign, back, up, down = call(
        enter_kernel,
        [((own, width), BF)] * 3 + [((3 * cols, width), BF)] * 2,
        halting, flat_in, upstream, weight_reduce, weight_expand,
    )
    from_prev = lax.ppermute(down, "rows", [(i, i + 1) for i in range(NZ - 1)])
    from_next = lax.ppermute(up, "rows", [(i + 1, i) for i in range(NZ - 1)])

    conv_rows, expand_rows = width // (NX * NH * NL * NC), chans // (NX * NH * NL * NC)
    lanes = taps + NH * width
    part = (NX * NL, NH * conv_rows, lanes)
    wide = own + 2 * cols
    keep, send, two, gtwo = call(
        middle_kernel,
        [(part, BF), (part, BF), ((own, width), BF), ((wide, width), BF)],
        halting, hidden, back, from_prev, from_next, upstream, weight_conv,
        scratch=[pltpu.VMEM((wide, taps), BF)],
    )

    got = lax.ppermute(send, "core", [(0, 1), (1, 0)])
    out, grad_in = call(
        functools.partial(leave_kernel, cols=cols),
        [((own, chans), BF)] * 2,
        flat_in, upstream, two, gtwo, sign, weight_reduce, weight_conv, weight_expand,
        scratch=[pltpu.VMEM((own, taps), BF), pltpu.VMEM((taps, width), BF)],
        keep=False,
    )
    total = (keep.astype(F32) + got.astype(F32)).astype(BF)
    total = lax.all_to_all(total, ("x", "y_lo"), 0, 0, tiled=True).astype(F32).sum(0)
    conv = total[:, :taps].reshape(NH, conv_rows, taps)
    expand = total[:, taps:].reshape(expand_rows // conv_rows, conv_rows, NH, width)
    expand = expand.transpose(2, 1, 0, 3).reshape(NH, conv_rows, expand_rows // conv_rows * width)
    total = jnp.concatenate([conv, expand], axis=2).astype(BF)
    total = lax.all_to_all(total, "y_hi", 0, 0, tiled=True).astype(F32).sum(0).astype(BF)
    total = jnp.broadcast_to(total[None], (NZ,) + total.shape)
    total = lax.all_to_all(total, "rows", 0, 0, tiled=True).astype(F32).sum(0)
    grad_conv = total[:, :taps]
    grad_expand = total[:, taps:].reshape(conv_rows, expand_rows // conv_rows, width)
    grad_expand = grad_expand.transpose(1, 0, 2).reshape(expand_rows, width)
    return (out.reshape(features.shape), grad_in.reshape(features.shape), grad_conv, grad_expand)


def solution(mesh):
    mesh = Mesh(mesh.devices.reshape(SIZES), AXES)
    whole = P(DP, "rows", None, None)
    in_specs = (whole, P(DP, "rows", None), whole, P(), P(), P())
    out_specs = (whole, whole, P(DP, None), P(DP, None))
    return jax.shard_map(local, mesh=mesh, in_specs=in_specs, out_specs=out_specs, check_vma=False)
```

time: 128 us -> 95.3 us (0.74)
  the two profiles are of different devices: /device:TPU:2 before, /device:TPU:8 now
where the time goes in v2:
time: 95.3 us; the launch traced here: 94.1 us
  blocking collectives  32.9 us (35%)
  local copies, waits for them, and re-layouts  19 us (20%)
  starting transfers between devices  16.8 us (18%)
  waiting for transfers between devices  13 us (14%)
  other arithmetic  5.92 us (6%)
  Pallas kernels  5.56 us (6%)
    all_to_all x1, blocking collectives, local(): lax.all_to_all(total, ('x', 'y_lo'), 0, 0, tiled=True).astype(F32).sum(0)  18.6 us
    all_to_all x1, blocking collectives, local(): lax.all_to_all(total, 'y_hi', 0, 0, tiled=True).astype(F32).sum(0)  14.3 us
    all_to_all x1, starting transfers between devices, local(): total = lax.all_to_all(total, 'rows', 0, 0, tiled=True).astype(F32).sum(0)  9.33 us
    unnamed x32, local copies, waits for them, and re-layouts  7.73 us
    pallas_call x3, Pallas kernels, call(): pl.pallas_call(kernel, out_shape=[shape_of(shape, dtype) for shape, dtype...  5.56 us
    all_to_all x1, waiting for transfers between devices, local(): total = lax.all_to_all(total, 'rows', 0, 0, tiled=True).astype(F32).sum(0)  5.13 us
    ppermute x1, waiting for transfers between devices, local(): from_next = lax.ppermute(up, 'rows', [(i + 1, i) for i in range(NZ - 1)])  4.67 us
    ppermute x1, starting transfers between devices, local(): from_prev = lax.ppermute(down, 'rows', [(i, i + 1) for i in range(NZ - 1)])  4.28 us
  transfers between devices with their start and end apart: 4, of which 4 were waited for; matrix products, arithmetic and copies ran while one was open for 0% of the time, Pallas kernels for 2%

profile of v2, /device:TPU:8, one launch (start us, length us, event | category | flops | bytes accessed | tf_op | source)
XLA Modules:
  0.0 94.1 jit_solution(7397461757109584395)
XLA Ops:
  0.6 0.0 copy-start
  0.6 1.1 %copy-done = bf16[1,5,64,1024]{3,2,1,0:T(8,128)(2,1)S(1)} copy-done((bf16[1,5,64,1024]{3,2,1,0:T(8,128)(2,1)S(1)}, bf16[1,5,64,1024]{3,2,1,0:T(8,128)(2,1)}, u32[]{:S(2)}) %copy-start) | copy-done | bytes 655384
  1.7 0.0 copy-start.3
  1.7 1.1 %copy-done.3 = bf16[1,5,64,1024]{3,2,1,0:T(8,128)(2,1)S(1)} copy-done((bf16[1,5,64,1024]{3,2,1,0:T(8,128)(2,1)S(1)}, bf16[1,5,64,1024]{3,2,1,0:T(8,128)(2,1)}, u32[]{:S(2)}) %copy-start.3) | copy-done | bytes 655384
  2.8 0.0 copy-start.5
  2.8 1.0 %copy-done.5 = bf16[256,1024]{1,0:T(8,128)(2,1)S(1)} copy-done((bf16[256,1024]{1,0:T(8,128)(2,1)S(1)}, bf16[256,1024]{1,0:T(8,128)(2,1)}, u32[]{:S(2)}) %copy-start.5) | copy-done | bytes 524312
  3.9 0.0 copy-start.7
  3.9 1.0 %copy-done.7 = bf16[1024,256]{1,0:T(8,128)(2,1)S(1)} copy-done((bf16[1024,256]{1,0:T(8,128)(2,1)S(1)}, bf16[1024,256]{1,0:T(8,128)(2,1)}, u32[]{:S(2)}) %copy-start.7) | copy-done | bytes 524312
  4.9 0.0 copy-start.15
  4.9 0.7 copy-done.15
  5.6 0.0 copy-start.1
  5.6 0.0 copy-start.2
  5.6 0.6 shard_map.93
  6.1 0.0 copy-start.11
  6.2 4.3 %collective-permute-start = (bf16[192,256]{1,0:T(8,128)(2,1)S(1)}, bf16[192,256]{1,0:T(8,128)(2,1)S(1)}, u32[]{:S(2)}, u32[]{:S(2)}) collective-permute-start(bf16[192,256]{1,0:T(8,128)(2,1)S(1)} %get-tuple-element.17), channel_id=1, source_target_pairs={{0,1},{1,2},{2,3},{3,4},{4,5},{5,6},{6,7},{8,9},{9,10},{10,11},{11... | collective-permute-start | bytes 294920 | tf_op jit(solution)/shard_map/ppermute | solution.py:167
  10.4 1.3 %collective-permute-start.1 = (bf16[192,256]{1,0:T(8,128)(2,1)S(1)}, bf16[192,256]{1,0:T(8,128)(2,1)S(1)}, u32[]{:S(2)}, u32[]{:S(2)}) collective-permute-start(bf16[192,256]{1,0:T(8,128)(2,1)S(1)} %get-tuple-element.18), channel_id=1, source_target_pairs={{1,0},{2,1},{3,2},{4,3},{5,4},{6,5},{7,6},{9,8},{10,9},{11,10},{12... | collective-permute-start | bytes 294920 | tf_op jit(solution)/shard_map/ppermute | solution.py:168
  11.7 0.9 collective-permute-done.prev_ref
  12.6 4.7 %collective-permute-done.1.next_ref = bf16[192,256]{1,0:T(8,128)(2,1)S(1)} collective-permute-done((bf16[192,256]{1,0:T(8,128)(2,1)S(1)}, bf16[192,256]{1,0:T(8,128)(2,1)S(1)}, u32[]{:S(2)}, u32[]{:S(2)}) %collective-permute-start.1) | collective-permute-done | bytes 98336 | tf_op jit(solution)/shard_map/ppermute | solution.py:168
  17.3 0.0 copy-done.1
  17.3 0.0 copy-done.2
  17.3 2.9 %shard_map.94 = (bf16[8,16,3328]{2,1,0:T(8,128)(2,1)S(1)}, bf16[8,16,3328]{2,1,0:T(8,128)(2,1)S(1)}, bf16[320,256]{1,0:T(8,128)(2,1)S(1)}, bf16[448,256]{1,0:T(8,128)(2,1)S(1)}) custom-call(s32[5,1,64]{2,1,0:T(1,128)S(1)} %bitcast.13, bf16[320,256]{1,0:T(8,128)(2,1)S(1)} %get-tuple-element.15.hidden_ref, bf16[320,256]{1,0:T(8,128)(2,1)S(1)} %get-tuple-element.16.back_ref, ...), custom_call_target="tpu_custom_call" | custom-call | tf_op jit(solution)/shard_map/pallas_call | solution.py:145
  20.2 0.0 copy-done.11
  20.2 0.0 copy-start.9
  20.2 0.0 copy-start.13
  20.2 1.9 %collective-permute-start.2 = (bf16[8,16,3328]{2,1,0:T(8,128)(2,1)S(1)}, bf16[8,16,3328]{2,1,0:T(8,128)(2,1)S(1)}, u32[]{:S(2)}, u32[]{:S(2)}) collective-permute-start(bf16[8,16,3328]{2,1,0:T(8,128)(2,1)S(1)} %get-tuple-element.25), channel_id=1, source_target_pairs={{0,8},{8,0},{1,9},{9,1},{2,10},{10,2},{3,11},{11,3},{4,12},{12,4},... | collective-permute-start | bytes 2555912 | tf_op jit(solution)/shard_map/ppermute | solution.py:181
  22.2 2.3 %collective-permute-done.2 = bf16[8,16,3328]{2,1,0:T(8,128)(2,1)S(1)} collective-permute-done((bf16[8,16,3328]{2,1,0:T(8,128)(2,1)S(1)}, bf16[8,16,3328]{2,1,0:T(8,128)(2,1)S(1)}, u32[]{:S(2)}, u32[]{:S(2)}) %collective-permute-start.2) | collective-permute-done | bytes 852000 | tf_op jit(solution)/shard_map/ppermute | solution.py:181
  24.5 0.3 add_convert_fusion
  24.8 0.0 copy-done.9
  24.8 0.0 copy-done.13
  24.8 18.6 %all_to_all.15 = bf16[8,16,3328]{2,1,0:T(8,128)(2,1)} all-to-all(bf16[8,16,3328]{2,1,0:T(8,128)(2,1)S(1)} %add_convert_fusion), channel_id=1, replica_groups=mesh['x'=4,'y_hi'=4,'y_lo'=2,'core'=2,'rows'=8] {'x','y_lo'}, dimensions={0} | all-to-all | bytes 1703936 | tf_op jit(solution)/shard_map/all_to_all | solution.py:190
  43.4 0.0 copy-start.4
  43.4 0.0 copy-start.6
  43.4 0.0 copy-start.8
  43.4 2.1 %reduce.1 = bf16[16,3328]{1,0:T(8,128)(2,1)} reduce(bf16[8,16,3328]{2,1,0:T(8,128)(2,1)} %all_to_all.15, bf16[]{:T(256)} %constant.3.clone.1), dimensions={0}, to_apply=%region_0.0.clone | reduce | flops 372736 | bytes 958466 | tf_op jit(solution)/shard_map/reduce_sum | solution.py:190
  45.4 1.5 %slice.18 = bf16[16,2304]{1,0:T(8,128)(2,1)} slice(bf16[16,3328]{1,0:T(8,128)(2,1)} %reduce.1), slice={[0:16], [0:2304]} | slice | bytes 147456 | tf_op jit(solution)/shard_map/slice | solution.py:191
  46.9 1.4 %slice.19 = bf16[16,1024]{1,0:T(8,128)(2,1)} slice(bf16[16,3328]{1,0:T(8,128)(2,1)} %reduce.1), slice={[0:16], [2304:3328]} | slice | bytes 65536 | tf_op jit(solution)/shard_map/slice | solution.py:192
  48.3 1.5 %reshape.47 = bf16[4,4,2304]{2,1,0:T(4,128)(2,1)} reshape(bf16[16,2304]{1,0:T(8,128)(2,1)} %slice.18) | data formatting | bytes 147456 | tf_op jit(solution)/shard_map/reshape | solution.py:191
  49.8 1.4 %reshape.48 = bf16[4,4,4,256]{3,2,1,0:T(4,128)(2,1)} reshape(bf16[16,1024]{1,0:T(8,128)(2,1)} %slice.19) | data formatting | bytes 65536 | tf_op jit(solution)/shard_map/reshape | solution.py:192
  51.2 1.4 %copy.19 = bf16[4,4,4,256]{3,2,1,0:T(4,128)(2,1)} copy(bf16[4,4,4,256]{3,0,1,2:T(4,128)(2,1)} %bitcast.14) | data formatting | bytes 65536 | tf_op jit(solution)/shard_map/transpose | solution.py:193
  52.6 1.4 %reshape.49 = bf16[4,4,1024]{2,1,0:T(4,128)(2,1)} reshape(bf16[4,4,4,256]{3,2,1,0:T(4,128)(2,1)} %copy.19) | data formatting | bytes 65536 | tf_op jit(solution)/shard_map/reshape | solution.py:193
  54.0 1.0 %pad_maximum_fusion = bf16[4,4,3328]{2,1,0:T(4,128)(2,1)S(1)} fusion(bf16[4,4,1024]{2,1,0:T(4,128)(2,1)} %reshape.49, bf16[4,4,2304]{2,1,0:T(4,128)(2,1)} %reshape.47), kind=kLoop, calls=%fused_computation.2 | loop fusion | flops 212992 | bytes 212992 | tf_op jit(solution)/shard_map/concatenate | solution.py:194
  55.0 14.3 %all_to_all.16 = bf16[4,4,3328]{2,1,0:T(4,128)(2,1)} all-to-all(bf16[4,4,3328]{2,1,0:T(4,128)(2,1)S(1)} %pad_maximum_fusion), channel_id=1, replica_groups=mesh['x'=4,'y_hi'=4,'y_lo'=2,'core'=2,'rows'=8] {'y_hi'}, dimensions={0} | all-to-all | bytes 212992 | tf_op jit(solution)/shard_map/all_to_all | solution.py:195
  69.3 1.6 %reduce_sum.31 = bf16[4,3328]{1,0:T(4,128)(2,1)} reduce(bf16[4,4,3328]{2,1,0:T(4,128)(2,1)} %all_to_all.16, bf16[]{:T(256)} %constant.3.clone.1), dimensions={0}, to_apply=%region_1.0 | reduce | flops 39936 | bytes 133122 | tf_op jit(solution)/shard_map/reduce_sum | solution.py:195
  70.9 1.5 %broadcast_in_dim.2 = bf16[8,4,3328]{2,1,0:T(4,128)(2,1)} broadcast(bf16[4,3328]{1,0:T(4,128)(2,1)} %reduce_sum.31), dimensions={1,2} | broadcast | bytes 239616 | tf_op jit(solution)/shard_map/broadcast_in_dim | solution.py:196
  72.4 9.3 %all-to-all-start.2 = ((bf16[8,4,3328]{2,1,0:T(4,128)(2,1)}), bf16[8,4,3328]{2,1,0:T(4,128)(2,1)}, u32[]{:S(2)}, u32[]{:S(2)}) async-start(bf16[8,4,3328]{2,1,0:T(4,128)(2,1)} %broadcast_in_dim.2), calls=%async_computation.2 | async-start | bytes 425984 | tf_op jit(solution)/shard_map/all_to_all | solution.py:197
  81.7 0.0 copy-done.4
  81.7 0.0 copy-done.6
  81.7 0.0 copy-done.8
  81.7 0.0 copy-start.10
  81.7 0.9 copy-done.10
  82.7 0.0 copy-start.12
  82.7 0.9 copy-done.12
  83.6 0.0 copy-start.14
  83.6 0.9 copy-done.14
  84.5 2.1 %shard_map.95 = (bf16[320,1024]{1,0:T(8,128)(2,1)}, bf16[320,1024]{1,0:T(8,128)(2,1)}) custom-call(bf16[320,1024]{1,0:T(8,128)(2,1)S(1)} %bitcast.11, bf16[320,1024]{1,0:T(8,128)(2,1)S(1)} %bitcast.9, bf16[320,256]{1,0:T(8,128)(2,1)S(1)} %copy-done.14, bf16[448,256]{1,0:T(8,128)(2,1)S(1)} %copy-done.10, bf16[320,256]{1,0:T(8,128)(2,1)S(1)} %copy-done.12, ...), custom_call_target="tpu_custom_call" | custom-call | tf_op jit(solution)/shard_map/pallas_call | solution.py:145
  86.6 5.1 %all-to-all-done.2 = bf16[8,4,3328]{2,1,0:T(4,128)(2,1)} async-done(((bf16[8,4,3328]{2,1,0:T(4,128)(2,1)}), bf16[8,4,3328]{2,1,0:T(4,128)(2,1)}, u32[]{:S(2)}, u32[]{:S(2)}) %all-to-all-start.2) | async-done | bytes 213024 | tf_op jit(solution)/shard_map/all_to_all | solution.py:197
  91.8 1.1 %convert_reduce_fusion = f32[4,3328]{1,0:T(4,128)S(1)} fusion(bf16[8,4,3328]{2,1,0:T(4,128)(2,1)} %all-to-all-done.2), kind=kLoop, calls=%fused_computation.1 | loop fusion | flops 199680 | bytes 266240 | tf_op jit(solution)/shard_map/reduce_sum | solution.py:197
  92.9 0.6 slice.20
  93.5 0.6 reshape.51
  (3 shorter events, 0.0 us)
Async XLA Ops:
  0.6 1.1 %copy-start = (bf16[1,5,64,1024]{3,2,1,0:T(8,128)(2,1)S(1)}, bf16[1,5,64,1024]{3,2,1,0:T(8,128)(2,1)}, u32[]{:S(2)}) copy-start(bf16[1,5,64,1024]{3,2,1,0:T(8,128)(2,1)} %param.8) | copy-start | bytes 1966084
  1.7 1.1 %copy-start.3 = (bf16[1,5,64,1024]{3,2,1,0:T(8,128)(2,1)S(1)}, bf16[1,5,64,1024]{3,2,1,0:T(8,128)(2,1)}, u32[]{:S(2)}) copy-start(bf16[1,5,64,1024]{3,2,1,0:T(8,128)(2,1)} %param.6) | copy-start | bytes 1966084
  2.8 1.0 %copy-start.5 = (bf16[256,1024]{1,0:T(8,128)(2,1)S(1)}, bf16[256,1024]{1,0:T(8,128)(2,1)}, u32[]{:S(2)}) copy-start(bf16[256,1024]{1,0:T(8,128)(2,1)} %reduce_ref.3) | copy-start | bytes 1572868
  3.9 1.0 %copy-start.7 = (bf16[1024,256]{1,0:T(8,128)(2,1)S(1)}, bf16[1024,256]{1,0:T(8,128)(2,1)}, u32[]{:S(2)}) copy-start(bf16[1024,256]{1,0:T(8,128)(2,1)} %expand_ref.3) | copy-start | bytes 1572868
  4.9 0.7 copy-start.15
  5.6 11.7 %copy-start.1 = (bf16[1,5,64,1024]{3,2,1,0:T(8,128)(2,1)S(1)}, bf16[1,5,64,1024]{3,2,1,0:T(8,128)(2,1)}, u32[]{:S(2)}) copy-start(bf16[1,5,64,1024]{3,2,1,0:T(8,128)(2,1)} %param.8) | copy-start | bytes 1966084
  5.6 11.7 %copy-start.2 = (bf16[256,2304]{1,0:T(8,128)(2,1)S(1)}, bf16[256,2304]{1,0:T(8,128)(2,1)}, u32[]{:S(2)}) copy-start(bf16[256,2304]{1,0:T(8,128)(2,1)} %conv_ref.3) | copy-start | bytes 3538948
  6.1 14.1 %copy-start.11 = (bf16[320,256]{1,0:T(8,128)(2,1)}, bf16[320,256]{1,0:T(8,128)(2,1)S(1)}, u32[]{:S(2)}) copy-start(bf16[320,256]{1,0:T(8,128)(2,1)S(1)} %get-tuple-element.21.sign_ref) | copy-start | bytes 491524
  6.2 6.5 %collective-permute-start = (bf16[192,256]{1,0:T(8,128)(2,1)S(1)}, bf16[192,256]{1,0:T(8,128)(2,1)S(1)}, u32[]{:S(2)}, u32[]{:S(2)}) collective-permute-start(bf16[192,256]{1,0:T(8,128)(2,1)S(1)} %get-tuple-element.17), channel_id=1, source_target_pairs={{0,1},{1,2},{2,3},{3,4},{4,5},{5,6},{6,7},{8,9},{9,10},{10,11},{11... | collective-permute-start | bytes 294920 | tf_op jit(solution)/shard_map/ppermute | solution.py:167
  10.4 6.9 %collective-permute-start.1 = (bf16[192,256]{1,0:T(8,128)(2,1)S(1)}, bf16[192,256]{1,0:T(8,128)(2,1)S(1)}, u32[]{:S(2)}, u32[]{:S(2)}) collective-permute-start(bf16[192,256]{1,0:T(8,128)(2,1)S(1)} %get-tuple-element.18), channel_id=1, source_target_pairs={{1,0},{2,1},{3,2},{4,3},{5,4},{6,5},{7,6},{9,8},{10,9},{11,10},{12... | collective-permute-start | bytes 294920 | tf_op jit(solution)/shard_map/ppermute | solution.py:168
  20.2 4.6 %copy-start.9 = (bf16[448,256]{1,0:T(8,128)(2,1)}, bf16[448,256]{1,0:T(8,128)(2,1)S(1)}, u32[]{:S(2)}) copy-start(bf16[448,256]{1,0:T(8,128)(2,1)S(1)} %get-tuple-element.20.gtwo_ref) | copy-start | bytes 688132
  20.2 4.6 %copy-start.13 = (bf16[320,256]{1,0:T(8,128)(2,1)}, bf16[320,256]{1,0:T(8,128)(2,1)S(1)}, u32[]{:S(2)}) copy-start(bf16[320,256]{1,0:T(8,128)(2,1)S(1)} %get-tuple-element.19.two_ref) | copy-start | bytes 491524
  20.2 4.3 %collective-permute-start.2 = (bf16[8,16,3328]{2,1,0:T(8,128)(2,1)S(1)}, bf16[8,16,3328]{2,1,0:T(8,128)(2,1)S(1)}, u32[]{:S(2)}, u32[]{:S(2)}) collective-permute-start(bf16[8,16,3328]{2,1,0:T(8,128)(2,1)S(1)} %get-tuple-element.25), channel_id=1, source_target_pairs={{0,8},{8,0},{1,9},{9,1},{2,10},{10,2},{3,11},{11,3},{4,12},{12,4},... | collective-permute-start | bytes 2555912 | tf_op jit(solution)/shard_map/ppermute | solution.py:181
  43.4 38.3 %copy-start.4 = (bf16[1,5,64,1024]{3,2,1,0:T(8,128)(2,1)S(1)}, bf16[1,5,64,1024]{3,2,1,0:T(8,128)(2,1)}, u32[]{:S(2)}) copy-start(bf16[1,5,64,1024]{3,2,1,0:T(8,128)(2,1)} %param.6) | copy-start | bytes 1966084
  43.4 38.3 %copy-start.6 = (bf16[256,1024]{1,0:T(8,128)(2,1)S(1)}, bf16[256,1024]{1,0:T(8,128)(2,1)}, u32[]{:S(2)}) copy-start(bf16[256,1024]{1,0:T(8,128)(2,1)} %reduce_ref.3) | copy-start | bytes 1572868
  43.4 38.3 %copy-start.8 = (bf16[1024,256]{1,0:T(8,128)(2,1)S(1)}, bf16[1024,256]{1,0:T(8,128)(2,1)}, u32[]{:S(2)}) copy-start(bf16[1024,256]{1,0:T(8,128)(2,1)} %expand_ref.3) | copy-start | bytes 1572868
  72.4 19.4 %all-to-all-start.2 = ((bf16[8,4,3328]{2,1,0:T(4,128)(2,1)}), bf16[8,4,3328]{2,1,0:T(4,128)(2,1)}, u32[]{:S(2)}, u32[]{:S(2)}) async-start(bf16[8,4,3328]{2,1,0:T(4,128)(2,1)} %broadcast_in_dim.2), calls=%async_computation.2 | async-start | bytes 425984 | tf_op jit(solution)/shard_map/all_to_all | solution.py:197
  81.7 0.9 %copy-start.10 = (bf16[448,256]{1,0:T(8,128)(2,1)S(1)}, bf16[448,256]{1,0:T(8,128)(2,1)}, u32[]{:S(2)}) copy-start(bf16[448,256]{1,0:T(8,128)(2,1)} %copy-done.9) | copy-start | bytes 688132
  82.7 0.9 copy-start.12
  83.6 0.9 copy-start.14

commit v3 on v2

--- a/solution.py
+++ b/solution.py
@@ -50,19 +50,34 @@
 
 
 def enter_kernel(
+    halt_hbm, feat_hbm, grad_hbm, reduce_hbm, expand_hbm,
     halt_ref, feat_ref, grad_ref, reduce_ref, expand_ref,
-    hidden_ref, sign_ref, back_ref, up_ref, down_ref,
+    hidden_ref, sign_ref, back_ref, up_ref, down_ref, sems,
 ):
+    pairs = (
+        (feat_hbm, feat_ref),
+        (reduce_hbm, reduce_ref),
+        (halt_hbm, halt_ref),
+        (grad_hbm, grad_ref),
+        (expand_hbm, expand_ref),
+    )
+    copies = [pltpu.make_async_copy(src, dst, sems.at[i]) for i, (src, dst) in enumerate(pairs)]
+    for copy in copies:
+        copy.start()
     rows, _, cols = halt_ref.shape
+    copies[0].wait()
+    copies[1].wait()
     pre_one = dot(feat_ref[...], reduce_ref[...], 1, 1)
     hidden = jnp.maximum(pre_one, 0.0).astype(BF)
     hidden_ref[...] = hidden
     sign_ref[...] = (pre_one > 0).astype(F32).astype(BF)
+    up_ref[0 : 2 * cols, :] = hidden[0 : 2 * cols]
+    down_ref[0 : 2 * cols, :] = hidden[(rows - 2) * cols :]
+    for copy in copies[2:]:
+        copy.wait()
     back = (active_column(halt_ref) * dot(grad_ref[...], expand_ref[...], 1, 0)).astype(BF)
     back_ref[...] = back
-    up_ref[0 : 2 * cols, :] = hidden[0 : 2 * cols]
     up_ref[2 * cols :, :] = back[0:cols]
-    down_ref[0 : 2 * cols, :] = hidden[(rows - 2) * cols :]
     down_ref[2 * cols :, :] = back[(rows - 1) * cols :]
 
 
@@ -118,7 +133,7 @@
 
 def leave_kernel(
     feat_ref, grad_ref, two_ref, gtwo_ref, sign_ref, reduce_ref, conv_ref, expand_ref,
-    out_ref, gin_ref, columns_ref, stacked_ref, *, cols,
+    out_ref, gin_ref, done_ref, columns_ref, stacked_ref, *, cols,
 ):
     own = feat_ref.shape[0]
     width = two_ref.shape[1]
@@ -134,19 +149,57 @@
     grad_hidden = dot(columns_ref[...], stacked_ref[...], 1, 0)
     grad_one = (grad_hidden * sign_ref[...].astype(F32)).astype(BF)
     gin_ref[...] = (grad_ref[...].astype(F32) + dot(grad_one, reduce_ref[...], 1, 0)).astype(BF)
+    done_ref[...] = jnp.zeros_like(done_ref)
+
+
+def sum_of(parts_ref):
+    total = parts_ref[0].astype(F32)
+    for i in range(1, parts_ref.shape[0]):
+        total = total + parts_ref[i].astype(F32)
+    return total
+
+
+def core_kernel(keep_ref, got_ref, out_ref):
+    out_ref[...] = (keep_ref[...].astype(F32) + got_ref[...].astype(F32)).astype(BF)
+
+
+def x_kernel(got_ref, done_ref, out_ref, *, taps, width):
+    total = sum_of(got_ref)
+    highs, count, lanes = out_ref.shape
+    for hi in range(highs):
+        out_ref[hi, :, 0:taps] = total[hi * count : (hi + 1) * count, 0:taps].astype(BF)
+        at = slice(taps + hi * width, taps + (hi + 1) * width)
+        for q in range((lanes - taps) // width):
+            to = slice(taps + q * width, taps + (q + 1) * width)
+            out_ref[hi, :, to] = total[q * count : (q + 1) * count, at].astype(BF)
+
+
+def y_kernel(got_ref, out_ref):
+    total = sum_of(got_ref).astype(BF)
+    for z in range(out_ref.shape[0]):
+        out_ref[z] = total
+
+
+def z_kernel(got_ref, conv_ref, expand_ref):
+    total = sum_of(got_ref)
+    count, taps = conv_ref.shape
+    width = expand_ref.shape[1]
+    conv_ref[...] = total[:, 0:taps]
+    for q in range(expand_ref.shape[0] // count):
+        expand_ref[q * count : (q + 1) * count, :] = total[:, taps + q * width : taps + (q + 1) * width]
 
 
 def in_vmem(array):
     return pltpu.with_memory_space_constraint(array, pltpu.VMEM)
 
 
-def call(kernel, outs, *args, scratch=(), keep=True):
-    shape_of = pltpu.VMEM if keep else jax.ShapeDtypeStruct
+def call(kernel, outs, *args, scratch=(), **options):
     return pl.pallas_call(
         kernel,
-        out_shape=[shape_of(shape, dtype) for shape, dtype in outs],
+        out_shape=outs,
         scratch_shapes=list(scratch),
         compiler_params=VMEM_LIMIT,
+        **options,
     )(*[in_vmem(a) for a in args])
 
 
@@ -155,15 +208,22 @@
     width = weight_reduce.shape[0]
     taps = weight_conv.shape[1]
     own = samples * rows * cols
-    flat_in = features.reshape(own, chans)
-    upstream = grad_out.reshape(own, chans)
-    halting = halting_map.reshape(samples * rows, 1, cols)
-
-    hidden, sign, back, up, down = call(
+    inputs = (
+        halting_map.reshape(samples * rows, 1, cols),
+        features.reshape(own, chans),
+        grad_out.reshape(own, chans),
+        weight_reduce,
+        weight_expand,
+    )
+    halting, flat_in, upstream, reduce_in, expand_in, hidden, sign, back, up, down = pl.pallas_call(
         enter_kernel,
-        [((own, width), BF)] * 3 + [((3 * cols, width), BF)] * 2,
-        halting, flat_in, upstream, weight_reduce, weight_expand,
-    )
+        out_shape=[pltpu.VMEM(a.shape, a.dtype) for a in inputs]
+        + [pltpu.VMEM((own, width), BF)] * 3
+        + [pltpu.VMEM((3 * cols, width), BF)] * 2,
+        in_specs=[pl.BlockSpec(memory_space=pl.ANY)] * len(inputs),
+        scratch_shapes=[pltpu.SemaphoreType.DMA((len(inputs),))],
+        compiler_params=VMEM_LIMIT,
+    )(*inputs)
     from_prev = lax.ppermute(down, "rows", [(i, i + 1) for i in range(NZ - 1)])
     from_next = lax.ppermute(up, "rows", [(i + 1, i) for i in range(NZ - 1)])
 
@@ -173,31 +233,32 @@
     wide = own + 2 * cols
     keep, send, two, gtwo = call(
         middle_kernel,
-        [(part, BF), (part, BF), ((own, width), BF), ((wide, width), BF)],
+        [pltpu.VMEM(part, BF), pltpu.VMEM(part, BF), pltpu.VMEM((own, width), BF), pltpu.VMEM((wide, width), BF)],
         halting, hidden, back, from_prev, from_next, upstream, weight_conv,
         scratch=[pltpu.VMEM((wide, taps), BF)],
     )
 
     got = lax.ppermute(send, "core", [(0, 1), (1, 0)])
-    out, grad_in = call(
+    out, grad_in, done = call(
         functools.partial(leave_kernel, cols=cols),
-        [((own, chans), BF)] * 2,
-        flat_in, upstream, two, gtwo, sign, weight_reduce, weight_conv, weight_expand,
+        [jax.ShapeDtypeStruct((own, chans), BF)] * 2 + [pltpu.VMEM((8, 128), F32)],
+        flat_in, upstream, two, gtwo, sign, reduce_in, weight_conv, expand_in,
         scratch=[pltpu.VMEM((own, taps), BF), pltpu.VMEM((taps, width), BF)],
-        keep=False,
-    )
-    total = (keep.astype(F32) + got.astype(F32)).astype(BF)
-    total = lax.all_to_all(total, ("x", "y_lo"), 0, 0, tiled=True).astype(F32).sum(0)
-    conv = total[:, :taps].reshape(NH, conv_rows, taps)
-    expand = total[:, taps:].reshape(expand_rows // conv_rows, conv_rows, NH, width)
-    expand = expand.transpose(2, 1, 0, 3).reshape(NH, conv_rows, expand_rows // conv_rows * width)
-    total = jnp.concatenate([conv, expand], axis=2).astype(BF)
-    total = lax.all_to_all(total, "y_hi", 0, 0, tiled=True).astype(F32).sum(0).astype(BF)
-    total = jnp.broadcast_to(total[None], (NZ,) + total.shape)
-    total = lax.all_to_all(total, "rows", 0, 0, tiled=True).astype(F32).sum(0)
-    grad_conv = total[:, :taps]
-    grad_expand = total[:, taps:].reshape(conv_rows, expand_rows // conv_rows, width)
-    grad_expand = grad_expand.transpose(1, 0, 2).reshape(expand_rows, width)
+    )
+    (total,) = call(core_kernel, [pltpu.VMEM(part, BF)], keep, got)
+    got = lax.all_to_all(total, ("x", "y_lo"), 0, 0, tiled=True)
+    shard = (conv_rows, taps + expand_rows // conv_rows * width)
+    (total,) = call(
+        functools.partial(x_kernel, taps=taps, width=width), [pltpu.VMEM((NH,) + shard, BF)], got, done
+    )
+    got = lax.all_to_all(total, "y_hi", 0, 0, tiled=True)
+    (total,) = call(y_kernel, [pltpu.VMEM((NZ,) + shard, BF)], got)
+    got = lax.all_to_all(total, "rows", 0, 0, tiled=True)
+    grad_conv, grad_expand = call(
+        z_kernel,
+        [jax.ShapeDtypeStruct((conv_rows, taps), F32), jax.ShapeDtypeStruct((expand_rows, width), F32)],
+        got,
+    )
     return (out.reshape(features.shape), grad_in.reshape(features.shape), grad_conv, grad_expand)
 
 

time: 95.3 us -> 78.5 us (0.82)
  local copies, waits for them, and re-layouts: 19 us -> 6.86 us
  other arithmetic: 5.92 us -> 0 us
  Pallas kernels: 5.56 us -> 9.31 us
  starting transfers between devices: 16.8 us -> 13.4 us
  waiting for transfers between devices: 13 us -> 14.9 us
    reshape x5 -> x0, local copies, waits for them, and re-layouts: 4.93 us -> none  [the longest x1 1.53 us: local(): conv = total[:, :taps].reshape(NH, conv_rows, taps)]
    reduce_sum x3 -> x0, other arithmetic: 4.7 us -> none  [the longest x1 2.05 us: local(): lax.all_to_all(total, ('x', 'y_lo'), 0, 0, tiled=True).astype(F32).sum(0)]
    pallas_call x3 -> x7, Pallas kernels: 5.56 us -> 9.31 us  [the longest x6 6.89 us: call(): pl.pallas_call(kernel, out_shape=outs, scratch_shapes=list(scratch), comp...]
    slice x4 -> x0, local copies, waits for them, and re-layouts: 3.5 us -> none  [the longest x1 1.5 us: local(): conv = total[:, :taps].reshape(NH, conv_rows, taps)]
    all_to_all x1, starting transfers between devices: 9.33 us -> 5.93 us  [local(): got = lax.all_to_all(total, ('x', 'y_lo'), 0, 0, tiled=True)]
    all_to_all x1, waiting for transfers between devices: 5.13 us -> 6.96 us  [local(): got = lax.all_to_all(total, ('x', 'y_lo'), 0, 0, tiled=True)]
    broadcast_in_dim x1 -> x0, local copies, waits for them, and re-layouts: 1.49 us -> none  [local(): total = jnp.broadcast_to(total[None], (NZ,) + total.shape)]
    transpose x2 -> x0, local copies, waits for them, and re-layouts: 1.4 us -> none  [the longest x1 1.39 us: local(): expand.transpose(2, 1, 0, 3)]
  transfers between devices with their start and end apart: 4 -> 4, of which waited for: 4 -> 4; matrix products, arithmetic and copies ran while one was open for 0% -> 0% of each run, Pallas kernels for 2% -> 3%
where the time goes in v3:
time: 78.5 us; the launch traced here: 78 us
  blocking collectives  32.9 us (42%)
  waiting for transfers between devices  14.9 us (19%)
  starting transfers between devices  13.4 us (17%)
  Pallas kernels  9.31 us (12%)
  local copies, waits for them, and re-layouts  6.86 us (9%)
    all_to_all x1, blocking collectives, local(): got = lax.all_to_all(total, 'rows', 0, 0, tiled=True)  19.1 us
    all_to_all x1, blocking collectives, local(): got = lax.all_to_all(total, 'y_hi', 0, 0, tiled=True)  13.8 us
    all_to_all x1, waiting for transfers between devices, local(): got = lax.all_to_all(total, ('x', 'y_lo'), 0, 0, tiled=True)  6.96 us
    pallas_call x6, Pallas kernels, call(): pl.pallas_call(kernel, out_shape=outs, scratch_shapes=list(scratch), comp...  6.89 us
    unnamed x18, local copies, waits for them, and re-layouts  6.86 us
    all_to_all x1, starting transfers between devices, local(): got = lax.all_to_all(total, ('x', 'y_lo'), 0, 0, tiled=True)  5.93 us
    ppermute x1, waiting for transfers between devices, local(): from_next = lax.ppermute(up, 'rows', [(i + 1, i) for i in range(NZ - 1)])  4.68 us
    ppermute x1, starting transfers between devices, local(): from_prev = lax.ppermute(down, 'rows', [(i, i + 1) for i in range(NZ - 1)])  4.27 us
  transfers between devices with their start and end apart: 4, of which 4 were waited for; matrix products, arithmetic and copies ran while one was open for 0% of the time, Pallas kernels for 3%

profile of v3, /device:TPU:8, one launch (start us, length us, event | category | flops | bytes accessed | tf_op | source)
XLA Modules:
  0.0 78.0 jit_solution(15849606131581496833)
XLA Ops:
  0.6 0.0 copy-start
  0.6 2.4 %shard_map.93 = (s32[5,1,64]{2,1,0:T(1,128)S(1)}, bf16[320,1024]{1,0:T(8,128)(2,1)S(1)}, bf16[320,1024]{1,0:T(8,128)(2,1)S(1)}, bf16[256,1024]{1,0:T(8,128)(2,1)...) custom-call(s32[5,1,64]{2,1,0:T(1,128)} %bitcast.7, ...), custom_call_target="tpu_custom_call" | custom-call | tf_op jit(solution)/shard_map/pallas_call | solution.py:218
  3.1 0.0 copy-start.1
  3.1 0.8 %copy-done.1 = bf16[256,1024]{1,0:T(8,128)(2,1)} copy-done((bf16[256,1024]{1,0:T(8,128)(2,1)}, bf16[256,1024]{1,0:T(8,128)(2,1)S(1)}, u32[]{:S(2)}) %copy-start.1) | copy-done | bytes 524312
  3.9 0.0 copy-start.3
  3.9 0.8 %copy-done.3 = bf16[1024,256]{1,0:T(8,128)(2,1)} copy-done((bf16[1024,256]{1,0:T(8,128)(2,1)}, bf16[1024,256]{1,0:T(8,128)(2,1)S(1)}, u32[]{:S(2)}) %copy-start.3) | copy-done | bytes 524312
  4.7 4.3 %collective-permute-start = (bf16[192,256]{1,0:T(8,128)(2,1)S(1)}, bf16[192,256]{1,0:T(8,128)(2,1)S(1)}, u32[]{:S(2)}, u32[]{:S(2)}) collective-permute-start(bf16[192,256]{1,0:T(8,128)(2,1)S(1)} %get-tuple-element.28), channel_id=1, source_target_pairs={{0,1},{1,2},{2,3},{3,4},{4,5},{5,6},{6,7},{8,9},{9,10},{10,11},{11... | collective-permute-start | bytes 294920 | tf_op jit(solution)/shard_map/ppermute | solution.py:227
  8.9 1.3 %collective-permute-start.1 = (bf16[192,256]{1,0:T(8,128)(2,1)S(1)}, bf16[192,256]{1,0:T(8,128)(2,1)S(1)}, u32[]{:S(2)}, u32[]{:S(2)}) collective-permute-start(bf16[192,256]{1,0:T(8,128)(2,1)S(1)} %get-tuple-element.29), channel_id=1, source_target_pairs={{1,0},{2,1},{3,2},{4,3},{5,4},{6,5},{7,6},{9,8},{10,9},{11,10},{12... | collective-permute-start | bytes 294920 | tf_op jit(solution)/shard_map/ppermute | solution.py:228
  10.2 0.9 %collective-permute-done.prev_ref = bf16[192,256]{1,0:T(8,128)(2,1)S(1)} collective-permute-done((bf16[192,256]{1,0:T(8,128)(2,1)S(1)}, bf16[192,256]{1,0:T(8,128)(2,1)S(1)}, u32[]{:S(2)}, u32[]{:S(2)}) %collective-permute-start) | collective-permute-done | bytes 98336 | tf_op jit(solution)/shard_map/ppermute | solution.py:227
  11.1 4.7 %collective-permute-done.1.next_ref = bf16[192,256]{1,0:T(8,128)(2,1)S(1)} collective-permute-done((bf16[192,256]{1,0:T(8,128)(2,1)S(1)}, bf16[192,256]{1,0:T(8,128)(2,1)S(1)}, u32[]{:S(2)}, u32[]{:S(2)}) %collective-permute-start.1) | collective-permute-done | bytes 98336 | tf_op jit(solution)/shard_map/ppermute | solution.py:228
  15.8 0.0 copy-done
  15.8 2.9 %shard_map.94 = (bf16[8,16,3328]{2,1,0:T(8,128)(2,1)S(1)}, bf16[8,16,3328]{2,1,0:T(8,128)(2,1)S(1)}, bf16[320,256]{1,0:T(8,128)(2,1)S(1)}, bf16[448,256]{1,0:T(8,128)(2,1)S(1)}) custom-call(s32[5,1,64]{2,1,0:T(1,128)S(1)} %get-tuple-element.25.halt_ref, bf16[320,256]{1,0:T(8,128)(2,1)S(1)} %get-tuple-element.26.hidden_ref, ...), custom_call_target="tpu_custom_call" | custom-call | tf_op jit(solution)/shard_map/pallas_call | solution.py:197
  18.7 0.0 copy-start.5
  18.7 0.7 copy-done.5
  19.4 0.0 copy-start.7
  19.4 0.7 copy-done.7
  20.0 1.9 %collective-permute-start.2 = (bf16[8,16,3328]{2,1,0:T(8,128)(2,1)S(1)}, bf16[8,16,3328]{2,1,0:T(8,128)(2,1)S(1)}, u32[]{:S(2)}, u32[]{:S(2)}) collective-permute-start(bf16[8,16,3328]{2,1,0:T(8,128)(2,1)S(1)} %get-tuple-element.38), channel_id=1, source_target_pairs={{0,8},{8,0},{1,9},{9,1},{2,10},{10,2},{3,11},{11,3},{4,12},{12,4},... | collective-permute-start | bytes 2555912 | tf_op jit(solution)/shard_map/ppermute | solution.py:241
  22.0 2.3 %collective-permute-done.2.got_ref = bf16[8,16,3328]{2,1,0:T(8,128)(2,1)S(1)} collective-permute-done((bf16[8,16,3328]{2,1,0:T(8,128)(2,1)S(1)}, bf16[8,16,3328]{2,1,0:T(8,128)(2,1)S(1)}, u32[]{:S(2)}, u32[]{:S(2)}) %collective-permute-start.2) | collective-permute-done | bytes 852000 | tf_op jit(solution)/shard_map/ppermute | solution.py:241
  24.3 1.1 %shard_map.96 = bf16[8,16,3328]{2,1,0:T(8,128)(2,1)} custom-call(bf16[8,16,3328]{2,1,0:T(8,128)(2,1)S(1)} %get-tuple-element.37.keep_ref, bf16[8,16,3328]{2,1,0:T(8,128)(2,1)S(1)} %collective-permute-done.2.got_ref), custom_call_target="tpu_custom_call" | custom-call | tf_op jit(solution)/shard_map/pallas_call | solution.py:197
  25.4 5.9 %all-to-all-start = ((bf16[8,16,3328]{2,1,0:T(8,128)(2,1)}), bf16[8,16,3328]{2,1,0:T(8,128)(2,1)S(1)}, u32[]{:S(2)}, u32[]{:S(2)}) async-start(bf16[8,16,3328]{2,1,0:T(8,128)(2,1)} %shard_map.96), calls=%async_computation | async-start | bytes 1703936 | tf_op jit(solution)/shard_map/all_to_all | solution.py:249
  31.3 0.0 copy-start.2
  31.3 1.0 %copy-done.2 = bf16[256,1024]{1,0:T(8,128)(2,1)S(1)} copy-done((bf16[256,1024]{1,0:T(8,128)(2,1)S(1)}, bf16[256,1024]{1,0:T(8,128)(2,1)}, u32[]{:S(2)}) %copy-start.2) | copy-done | bytes 524312
  32.4 0.0 copy-start.4
  32.4 1.0 %copy-done.4 = bf16[1024,256]{1,0:T(8,128)(2,1)S(1)} copy-done((bf16[1024,256]{1,0:T(8,128)(2,1)S(1)}, bf16[1024,256]{1,0:T(8,128)(2,1)}, u32[]{:S(2)}) %copy-start.4) | copy-done | bytes 524312
  33.4 0.0 copy-start.6
  33.4 0.9 %copy-done.6 = bf16[448,256]{1,0:T(8,128)(2,1)S(1)} copy-done((bf16[448,256]{1,0:T(8,128)(2,1)S(1)}, bf16[448,256]{1,0:T(8,128)(2,1)}, u32[]{:S(2)}) %copy-start.6) | copy-done | bytes 229400
  34.3 0.0 copy-start.8
  34.3 0.9 %copy-done.8 = bf16[320,256]{1,0:T(8,128)(2,1)S(1)} copy-done((bf16[320,256]{1,0:T(8,128)(2,1)S(1)}, bf16[320,256]{1,0:T(8,128)(2,1)}, u32[]{:S(2)}) %copy-start.8) | copy-done | bytes 163864
  35.3 2.1 %shard_map.95 = (bf16[320,1024]{1,0:T(8,128)(2,1)}, bf16[320,1024]{1,0:T(8,128)(2,1)}, f32[8,128]{1,0:T(8,128)S(1)}) custom-call(bf16[320,1024]{1,0:T(8,128)(2,1)S(1)} %get-tuple-element.23.feat_ref, bf16[320,1024]{1,0:T(8,128)(2,1)S(1)} %get-tuple-element.24.grad_ref, bf16[320,256]{1,0:T(8,128)(2,1)S(1)} %copy-done.8, bf16[448,256]{1,0:T(8,128)(2,1)S(1)} %copy-done.6, ...), custom_call_target="tpu_custom_call" | custom-call | tf_op jit(solution)/shard_map/pallas_call | solution.py:197
  37.4 7.0 %all-to-all-done.got_ref = bf16[8,16,3328]{2,1,0:T(8,128)(2,1)S(1)} async-done(((bf16[8,16,3328]{2,1,0:T(8,128)(2,1)}), bf16[8,16,3328]{2,1,0:T(8,128)(2,1)S(1)}, u32[]{:S(2)}, u32[]{:S(2)}) %all-to-all-start) | async-done | bytes 852000 | tf_op jit(solution)/shard_map/all_to_all | solution.py:249
  44.4 0.1 shard_map.97
  44.5 13.8 %all_to_all.15.got_ref = bf16[4,4,3328]{2,1,0:T(4,128)(2,1)S(1)} all-to-all(bf16[4,4,3328]{2,1,0:T(4,128)(2,1)S(1)} %shard_map.97), channel_id=1, replica_groups=mesh['x'=4,'y_hi'=4,'y_lo'=2,'core'=2,'rows'=8] {'y_hi'}, dimensions={0} | all-to-all | bytes 212992 | tf_op jit(solution)/shard_map/all_to_all | solution.py:254
  58.3 19.1 %all_to_all.16.got_ref = bf16[8,4,3328]{2,1,0:T(4,128)(2,1)S(1)} all-to-all(bf16[8,4,3328]{2,1,0:T(4,128)(2,1)S(1)} %shard_map.98), channel_id=1, replica_groups=mesh['x'=4,'y_hi'=4,'y_lo'=2,'core'=2,'rows'=8] {'rows'}, dimensions={0} | all-to-all | bytes 425984 | tf_op jit(solution)/shard_map/all_to_all | solution.py:256
  77.4 0.6 shard_map.99
  (1 shorter events, 0.0 us)
Async XLA Ops:
  0.6 15.2 %copy-start = (bf16[256,2304]{1,0:T(8,128)(2,1)S(1)}, bf16[256,2304]{1,0:T(8,128)(2,1)}, u32[]{:S(2)}) copy-start(bf16[256,2304]{1,0:T(8,128)(2,1)} %conv_ref.3) | copy-start | bytes 3538948
  3.1 0.8 %copy-start.1 = (bf16[256,1024]{1,0:T(8,128)(2,1)}, bf16[256,1024]{1,0:T(8,128)(2,1)S(1)}, u32[]{:S(2)}) copy-start(bf16[256,1024]{1,0:T(8,128)(2,1)S(1)} %get-tuple-element.33.reduce_ref) | copy-start | bytes 1572868
  3.9 0.8 %copy-start.3 = (bf16[1024,256]{1,0:T(8,128)(2,1)}, bf16[1024,256]{1,0:T(8,128)(2,1)S(1)}, u32[]{:S(2)}) copy-start(bf16[1024,256]{1,0:T(8,128)(2,1)S(1)} %get-tuple-element.34.expand_ref) | copy-start | bytes 1572868
  4.7 6.5 %collective-permute-start = (bf16[192,256]{1,0:T(8,128)(2,1)S(1)}, bf16[192,256]{1,0:T(8,128)(2,1)S(1)}, u32[]{:S(2)}, u32[]{:S(2)}) collective-permute-start(bf16[192,256]{1,0:T(8,128)(2,1)S(1)} %get-tuple-element.28), channel_id=1, source_target_pairs={{0,1},{1,2},{2,3},{3,4},{4,5},{5,6},{6,7},{8,9},{9,10},{10,11},{11... | collective-permute-start | bytes 294920 | tf_op jit(solution)/shard_map/ppermute | solution.py:227
  8.9 6.9 %collective-permute-start.1 = (bf16[192,256]{1,0:T(8,128)(2,1)S(1)}, bf16[192,256]{1,0:T(8,128)(2,1)S(1)}, u32[]{:S(2)}, u32[]{:S(2)}) collective-permute-start(bf16[192,256]{1,0:T(8,128)(2,1)S(1)} %get-tuple-element.29), channel_id=1, source_target_pairs={{1,0},{2,1},{3,2},{4,3},{5,4},{6,5},{7,6},{9,8},{10,9},{11,10},{12... | collective-permute-start | bytes 294920 | tf_op jit(solution)/shard_map/ppermute | solution.py:228
  18.7 0.7 copy-start.5
  19.4 0.7 copy-start.7
  20.0 4.3 %collective-permute-start.2 = (bf16[8,16,3328]{2,1,0:T(8,128)(2,1)S(1)}, bf16[8,16,3328]{2,1,0:T(8,128)(2,1)S(1)}, u32[]{:S(2)}, u32[]{:S(2)}) collective-permute-start(bf16[8,16,3328]{2,1,0:T(8,128)(2,1)S(1)} %get-tuple-element.38), channel_id=1, source_target_pairs={{0,8},{8,0},{1,9},{9,1},{2,10},{10,2},{3,11},{11,3},{4,12},{12,4},... | collective-permute-start | bytes 2555912 | tf_op jit(solution)/shard_map/ppermute | solution.py:241
  25.4 19.0 %all-to-all-start = ((bf16[8,16,3328]{2,1,0:T(8,128)(2,1)}), bf16[8,16,3328]{2,1,0:T(8,128)(2,1)S(1)}, u32[]{:S(2)}, u32[]{:S(2)}) async-start(bf16[8,16,3328]{2,1,0:T(8,128)(2,1)} %shard_map.96), calls=%async_computation | async-start | bytes 1703936 | tf_op jit(solution)/shard_map/all_to_all | solution.py:249
  31.3 1.0 %copy-start.2 = (bf16[256,1024]{1,0:T(8,128)(2,1)S(1)}, bf16[256,1024]{1,0:T(8,128)(2,1)}, u32[]{:S(2)}) copy-start(bf16[256,1024]{1,0:T(8,128)(2,1)} %copy-done.1) | copy-start | bytes 1572868
  32.4 1.0 %copy-start.4 = (bf16[1024,256]{1,0:T(8,128)(2,1)S(1)}, bf16[1024,256]{1,0:T(8,128)(2,1)}, u32[]{:S(2)}) copy-start(bf16[1024,256]{1,0:T(8,128)(2,1)} %copy-done.3) | copy-start | bytes 1572868
  33.4 0.9 %copy-start.6 = (bf16[448,256]{1,0:T(8,128)(2,1)S(1)}, bf16[448,256]{1,0:T(8,128)(2,1)}, u32[]{:S(2)}) copy-start(bf16[448,256]{1,0:T(8,128)(2,1)} %copy-done.5) | copy-start | bytes 688132
  34.3 0.9 %copy-start.8 = (bf16[320,256]{1,0:T(8,128)(2,1)S(1)}, bf16[320,256]{1,0:T(8,128)(2,1)}, u32[]{:S(2)}) copy-start(bf16[320,256]{1,0:T(8,128)(2,1)} %copy-done.7) | copy-start | bytes 491524

commit v4 on v3

--- a/solution.py
+++ b/solution.py
@@ -14,7 +14,7 @@
 AXES = ("x", "y_hi", "y_lo", "core", "rows")
 NX, NH, NL, NC, NZ = SIZES = (4, 4, 2, 2, 8)
 DP = AXES[:4]
-VMEM_LIMIT = pltpu.CompilerParams(vmem_limit_bytes=56 * 1024 * 1024)
+VMEM_LIMIT = pltpu.CompilerParams(vmem_limit_bytes=20 * 1024 * 1024)
 
 
 def dp_of(x, hi, lo, core):
@@ -81,45 +81,76 @@
     down_ref[2 * cols :, :] = back[(rows - 1) * cols :]
 
 
-def middle_kernel(
-    halt_ref, hidden_ref, back_ref, prev_ref, next_ref, grad_ref, conv_ref,
-    keep_ref, send_ref, two_ref, gtwo_ref, columns_ref,
-):
-    rows, _, cols = halt_ref.shape
-    own = rows * cols
-    width = hidden_ref.shape[1]
-    core = lax.axis_index("core")
-
-    padded = jnp.concatenate([prev_ref[0 : 2 * cols], hidden_ref[...], next_ref[0 : 2 * cols]], axis=0)
-    left, right = neighbours(padded, cols)
-    wide = own + 2 * cols
+def fill_columns(columns_ref, first, cells, cols):
+    width = cells.shape[1]
+    count = cells.shape[0] - 2 * cols
+    left, right = neighbours(cells, cols)
     for a in range(3):
-        for b, shifted in enumerate((left, padded, right)):
-            tap = 3 * a + b
-            columns_ref[:, tap * width : (tap + 1) * width] = shifted[a * cols : a * cols + wide]
-    pre_two = dot(columns_ref[...], conv_ref[...], 1, 1)
-    back = jnp.concatenate([prev_ref[2 * cols :], back_ref[...], next_ref[2 * cols :]], axis=0)
-    grad_two = jnp.where(pre_two > 0, back.astype(F32), 0.0).astype(BF)
-    gtwo_ref[...] = grad_two
-    active = active_column(halt_ref)
-    hidden_two = (active * jnp.maximum(pre_two[cols : cols + own], 0.0)).astype(BF)
-    two_ref[...] = hidden_two
-
+        for b, shifted in enumerate((left, cells, right)):
+            at = slice((3 * a + b) * width, (3 * a + b + 1) * width)
+            columns_ref[first : first + count, at] = shifted[a * cols : a * cols + count]
+
+
+def sorting(width):
     shape = (width, width)
     per_dp = width // (NX * NH * NL * NC)
     at = lax.broadcasted_iota(jnp.int32, shape, 0)
     j, hi, lo = at % per_dp, (at // per_dp) % NH, (at // (per_dp * NH)) % NL
     x, c = (at // (per_dp * NH * NL)) % NX, at // (per_dp * NH * NL * NX)
-    wanted = dp_of(x, hi, lo, c ^ core) * per_dp + j
-    shuffle = (lax.broadcasted_iota(jnp.int32, shape, 1) == wanted).astype(F32).astype(BF)
-    grad_rows = dot(shuffle, grad_two[cols : cols + own], 1, 1).astype(BF)
-    conv_part = dot(grad_rows, columns_ref[cols : cols + own, :], 1, 0).astype(BF)
-    tall, lanes = per_dp * NH, conv_part.shape[1]
+    wanted = dp_of(x, hi, lo, c ^ lax.axis_index("core")) * per_dp + j
+    return (lax.broadcasted_iota(jnp.int32, shape, 1) == wanted).astype(F32).astype(BF)
+
+
+def inner_kernel(
+    halt_ref, hidden_ref, back_ref, grad_ref, conv_ref,
+    cpart_ref, epart_ref, two_ref, gtwo_ref, columns_ref,
+):
+    rows, _, cols = halt_ref.shape
+    inner = slice(cols, (rows - 1) * cols)
+    fill_columns(columns_ref, 0, hidden_ref[...], cols)
+    pre_two = dot(columns_ref[...], conv_ref[...], 1, 1)
+    grad_two = jnp.where(pre_two > 0, back_ref[inner, :].astype(F32), 0.0).astype(BF)
+    gtwo_ref[...] = grad_two
+    hidden_two = (active_column(halt_ref)[inner] * jnp.maximum(pre_two, 0.0)).astype(BF)
+    two_ref[...] = hidden_two
+    grad_rows = dot(sorting(grad_two.shape[1]), grad_two, 1, 1).astype(BF)
+    cpart_ref[...] = dot(grad_rows, columns_ref[...], 1, 0)
+    epart_ref[...] = dot(grad_ref[inner, :], hidden_two, 0, 0)
+
+
+def outer_kernel(
+    halt_ref, hidden_ref, back_ref, prev_ref, next_ref, grad_ref, conv_ref, cpart_ref, epart_ref,
+    keep_ref, send_ref, two_ref, gtwo_ref, columns_ref,
+):
+    rows, _, cols = halt_ref.shape
+    width = hidden_ref.shape[1]
+    core = lax.axis_index("core")
+    top, end = slice(0, cols), slice((rows - 1) * cols, rows * cols)
+    halo = 2 * cols
+    above = jnp.concatenate([prev_ref[0:halo], hidden_ref[0:halo]], axis=0)
+    below = jnp.concatenate([hidden_ref[(rows - 2) * cols :], next_ref[0:halo]], axis=0)
+    fill_columns(columns_ref, 0, above, cols)
+    fill_columns(columns_ref, halo, below, cols)
+    pre_two = dot(columns_ref[...], conv_ref[...], 1, 1)
+    back = jnp.concatenate([prev_ref[halo:], back_ref[top, :], back_ref[end, :], next_ref[halo:]], axis=0)
+    grad_two = jnp.where(pre_two > 0, back.astype(F32), 0.0).astype(BF)
+    gtwo_ref[...] = grad_two
+    active = active_column(halt_ref)
+    active = jnp.concatenate([active[top], active[end]], axis=0)
+    own = slice(cols, cols + halo)
+    hidden_two = (active * jnp.maximum(pre_two[own], 0.0)).astype(BF)
+    two_ref[...] = hidden_two
+
+    grad_rows = dot(sorting(width), grad_two[own], 1, 1).astype(BF)
+    conv_part = (cpart_ref[...] + dot(grad_rows, columns_ref[own, :], 1, 0)).astype(BF)
+    per_dp, lanes = width // (NX * NH * NL * NC), conv_part.shape[1]
+    tall = per_dp * NH
     for group in range(NX * NL):
         keep_ref[group, :, 0:lanes] = conv_part[group * tall : (group + 1) * tall]
         other = NX * NL + group
         send_ref[group, :, 0:lanes] = conv_part[other * tall : (other + 1) * tall]
-    expand_part = dot(grad_ref[...], hidden_two, 0, 0).astype(BF)
+    upstream = jnp.concatenate([grad_ref[top, :], grad_ref[end, :]], axis=0)
+    expand_part = (epart_ref[...] + dot(upstream, hidden_two, 0, 0)).astype(BF)
     per_dp = expand_part.shape[0] // (NX * NH * NL * NC)
     for x in range(NX):
         for lo in range(NL):
@@ -132,13 +163,14 @@
 
 
 def leave_kernel(
-    feat_ref, grad_ref, two_ref, gtwo_ref, sign_ref, reduce_ref, conv_ref, expand_ref,
+    feat_ref, grad_ref, two_in_ref, two_ref, gtwo_in_ref, gtwo_ref, sign_ref, reduce_ref, conv_ref, expand_ref,
     out_ref, gin_ref, done_ref, columns_ref, stacked_ref, *, cols,
 ):
     own = feat_ref.shape[0]
     width = two_ref.shape[1]
-    out_ref[...] = (feat_ref[...].astype(F32) + dot(two_ref[...], expand_ref[...], 1, 1)).astype(BF)
-    grad_two = gtwo_ref[...]
+    two = jnp.concatenate([two_ref[0:cols], two_in_ref[...], two_ref[cols:]], axis=0)
+    out_ref[...] = (feat_ref[...].astype(F32) + dot(two, expand_ref[...], 1, 1)).astype(BF)
+    grad_two = jnp.concatenate([gtwo_ref[0 : 2 * cols], gtwo_in_ref[...], gtwo_ref[2 * cols :]], axis=0)
     left, right = neighbours(grad_two, cols)
     for a in range(3):
         for b, shifted in enumerate((right, grad_two, left)):
@@ -223,26 +255,32 @@
         in_specs=[pl.BlockSpec(memory_space=pl.ANY)] * len(inputs),
         scratch_shapes=[pltpu.SemaphoreType.DMA((len(inputs),))],
         compiler_params=VMEM_LIMIT,
-    )(*inputs)
+    )(*[pltpu.with_memory_space_constraint(a, pltpu.MemorySpace.HBM) for a in inputs])
     from_prev = lax.ppermute(down, "rows", [(i, i + 1) for i in range(NZ - 1)])
     from_next = lax.ppermute(up, "rows", [(i + 1, i) for i in range(NZ - 1)])
 
     conv_rows, expand_rows = width // (NX * NH * NL * NC), chans // (NX * NH * NL * NC)
     lanes = taps + NH * width
     part = (NX * NL, NH * conv_rows, lanes)
-    wide = own + 2 * cols
+    inner = (own - 2 * cols, width)
+    conv_part, expand_part, two_in, gtwo_in = call(
+        inner_kernel,
+        [pltpu.VMEM((width, taps), F32), pltpu.VMEM((chans, width), F32), pltpu.VMEM(inner, BF), pltpu.VMEM(inner, BF)],
+        halting, hidden, back, upstream, weight_conv,
+        scratch=[pltpu.VMEM((inner[0], taps), BF)],
+    )
     keep, send, two, gtwo = call(
-        middle_kernel,
-        [pltpu.VMEM(part, BF), pltpu.VMEM(part, BF), pltpu.VMEM((own, width), BF), pltpu.VMEM((wide, width), BF)],
-        halting, hidden, back, from_prev, from_next, upstream, weight_conv,
-        scratch=[pltpu.VMEM((wide, taps), BF)],
+        outer_kernel,
+        [pltpu.VMEM(part, BF), pltpu.VMEM(part, BF), pltpu.VMEM((2 * cols, width), BF), pltpu.VMEM((4 * cols, width), BF)],
+        halting, hidden, back, from_prev, from_next, upstream, weight_conv, conv_part, expand_part,
+        scratch=[pltpu.VMEM((4 * cols, taps), BF)],
     )
 
     got = lax.ppermute(send, "core", [(0, 1), (1, 0)])
     out, grad_in, done = call(
         functools.partial(leave_kernel, cols=cols),
         [jax.ShapeDtypeStruct((own, chans), BF)] * 2 + [pltpu.VMEM((8, 128), F32)],
-        flat_in, upstream, two, gtwo, sign, reduce_in, weight_conv, expand_in,
+        flat_in, upstream, two_in, two, gtwo_in, gtwo, sign, reduce_in, weight_conv, expand_in,
         scratch=[pltpu.VMEM((own, taps), BF), pltpu.VMEM((taps, width), BF)],
     )
     (total,) = call(core_kernel, [pltpu.VMEM(part, BF)], keep, got)

time: 78.5 us -> 75.9 us (0.967)
  waiting for transfers between devices: 14.9 us -> 10.7 us
    all_to_all x1, waiting for transfers between devices: 6.96 us -> 5.29 us  [local(): got = lax.all_to_all(total, ('x', 'y_lo'), 0, 0, tiled=True)]
    ppermute x1, waiting for transfers between devices: 4.68 us -> 3.09 us  [local(): from_next = lax.ppermute(up, 'rows', [(i + 1, i) for i in range(NZ - 1)])]
    ppermute x1, waiting for transfers between devices: 0.89 us -> 0.01 us  [local(): from_prev = lax.ppermute(down, 'rows', [(i, i + 1) for i in range(NZ - 1)])]
    pallas_call x6 -> x7, Pallas kernels: 6.89 us -> 7.61 us  [call(): pl.pallas_call(kernel, out_shape=outs, scratch_shapes=list(scratch), comp...]
    unnamed x18 -> x26, local copies, waits for them, and re-layouts: 6.86 us -> 7.54 us
  transfers between devices with their start and end apart: 4 -> 4, of which waited for: 4 -> 3; matrix products, arithmetic and copies ran while one was open for 0% -> 0% of each run, Pallas kernels for 3% -> 5%
where the time goes in v4:
time: 75.9 us; the launch traced here: 75.3 us
  blocking collectives  32.9 us (43%)
  starting transfers between devices  13.4 us (18%)
  waiting for transfers between devices  10.7 us (14%)
  Pallas kernels  10 us (13%)
  local copies, waits for them, and re-layouts  7.54 us (10%)
  between operations  0.76 us (1%)
    all_to_all x1, blocking collectives, local(): got = lax.all_to_all(total, 'rows', 0, 0, tiled=True)  19.1 us
    all_to_all x1, blocking collectives, local(): got = lax.all_to_all(total, 'y_hi', 0, 0, tiled=True)  13.8 us
    pallas_call x7, Pallas kernels, call(): pl.pallas_call(kernel, out_shape=outs, scratch_shapes=list(scratch), comp...  7.61 us
    unnamed x26, local copies, waits for them, and re-layouts  7.54 us
    all_to_all x1, starting transfers between devices, local(): got = lax.all_to_all(total, ('x', 'y_lo'), 0, 0, tiled=True)  5.93 us
    all_to_all x1, waiting for transfers between devices, local(): got = lax.all_to_all(total, ('x', 'y_lo'), 0, 0, tiled=True)  5.29 us
    ppermute x1, starting transfers between devices, local(): from_prev = lax.ppermute(down, 'rows', [(i, i + 1) for i in range(NZ - 1)])  4.28 us
    ppermute x1, waiting for transfers between devices, local(): from_next = lax.ppermute(up, 'rows', [(i + 1, i) for i in range(NZ - 1)])  3.09 us
  transfers between devices with their start and end apart: 4, of which 3 were waited for; matrix products, arithmetic and copies ran while one was open for 0% of the time, Pallas kernels for 5%

profile of v4, /device:TPU:8, one launch (start us, length us, event | category | flops | bytes accessed | tf_op | source)
XLA Modules:
  0.0 75.3 jit_solution(10063525702772002027)
XLA Ops:
  0.6 0.0 copy-start
  0.6 2.4 %shard_map.93 = (s32[5,1,64]{2,1,0:T(1,128)S(1)}, bf16[320,1024]{1,0:T(8,128)(2,1)S(1)}, bf16[320,1024]{1,0:T(8,128)(2,1)S(1)}, bf16[256,1024]{1,0:T(8,128)(2,1)...) custom-call(s32[5,1,64]{2,1,0:T(1,128)} %bitcast.7, ...), custom_call_target="tpu_custom_call" | custom-call | tf_op jit(solution)/shard_map/pallas_call | solution.py:250
  3.1 0.0 copy-start.1
  3.1 0.0 copy-start.3
  3.1 4.3 %collective-permute-start = (bf16[192,256]{1,0:T(8,128)(2,1)S(1)}, bf16[192,256]{1,0:T(8,128)(2,1)S(1)}, u32[]{:S(2)}, u32[]{:S(2)}) collective-permute-start(bf16[192,256]{1,0:T(8,128)(2,1)S(1)} %get-tuple-element.33), channel_id=1, source_target_pairs={{0,1},{1,2},{2,3},{3,4},{4,5},{5,6},{6,7},{8,9},{9,10},{10,11},{11... | collective-permute-start | bytes 294920 | tf_op jit(solution)/shard_map/ppermute | solution.py:259
  7.4 1.3 %collective-permute-start.1 = (bf16[192,256]{1,0:T(8,128)(2,1)S(1)}, bf16[192,256]{1,0:T(8,128)(2,1)S(1)}, u32[]{:S(2)}, u32[]{:S(2)}) collective-permute-start(bf16[192,256]{1,0:T(8,128)(2,1)S(1)} %get-tuple-element.34), channel_id=1, source_target_pairs={{1,0},{2,1},{3,2},{4,3},{5,4},{6,5},{7,6},{9,8},{10,9},{11,10},{12... | collective-permute-start | bytes 294920 | tf_op jit(solution)/shard_map/ppermute | solution.py:260
  8.7 0.0 copy-done
  8.7 1.8 %shard_map.94 = (f32[256,2304]{1,0:T(8,128)S(1)}, f32[1024,256]{1,0:T(8,128)S(1)}, bf16[192,256]{1,0:T(8,128)(2,1)S(1)}, bf16[192,256]{1,0:T(8,128)(2,1)S(1)}) custom-call(s32[5,1,64]{2,1,0:T(1,128)S(1)} %get-tuple-element.29.halt_ref, bf16[320,256]{1,0:T(8,128)(2,1)S(1)} %get-tuple-element.30.hidden_ref, bf16[320,256]{1,0:T(8,128)(2,1)S(1)} %get-tuple-element.31.back_ref, ...), custom_call_target="tpu_custom_call" | custom-call | tf_op jit(solution)/shard_map/pallas_call | solution.py:229
  10.5 0.0 copy-start.7
  10.5 0.6 copy-done.7
  11.1 0.0 copy-start.9
  11.1 0.0 collective-permute-done.prev_ref
  11.1 3.1 %collective-permute-done.1.next_ref = bf16[192,256]{1,0:T(8,128)(2,1)S(1)} collective-permute-done((bf16[192,256]{1,0:T(8,128)(2,1)S(1)}, bf16[192,256]{1,0:T(8,128)(2,1)S(1)}, u32[]{:S(2)}, u32[]{:S(2)}) %collective-permute-start.1) | collective-permute-done | bytes 98336 | tf_op jit(solution)/shard_map/ppermute | solution.py:260
  14.2 1.8 %shard_map.95 = (bf16[8,16,3328]{2,1,0:T(8,128)(2,1)S(1)}, bf16[8,16,3328]{2,1,0:T(8,128)(2,1)S(1)}, bf16[128,256]{1,0:T(8,128)(2,1)S(1)}, bf16[256,256]{1,0:T(8,128)(2,1)S(1)}) custom-call(s32[5,1,64]{2,1,0:T(1,128)S(1)} %get-tuple-element.29.halt_ref, bf16[320,256]{1,0:T(8,128)(2,1)S(1)} %get-tuple-element.30.hidden_ref, ...), custom_call_target="tpu_custom_call" | custom-call | tf_op jit(solution)/shard_map/pallas_call | solution.py:229
  16.0 0.0 copy-done.1
  16.0 0.0 copy-done.3
  16.0 0.0 copy-done.9
  16.0 0.0 copy-start.5
  16.1 0.6 copy-done.5
  16.7 0.0 copy-start.11
  16.7 0.6 copy-done.11
  17.3 1.9 %collective-permute-start.2 = (bf16[8,16,3328]{2,1,0:T(8,128)(2,1)S(1)}, bf16[8,16,3328]{2,1,0:T(8,128)(2,1)S(1)}, u32[]{:S(2)}, u32[]{:S(2)}) collective-permute-start(bf16[8,16,3328]{2,1,0:T(8,128)(2,1)S(1)} %get-tuple-element.46), channel_id=1, source_target_pairs={{0,8},{8,0},{1,9},{9,1},{2,10},{10,2},{3,11},{11,3},{4,12},{12,4},... | collective-permute-start | bytes 2555912 | tf_op jit(solution)/shard_map/ppermute | solution.py:279
  19.2 2.3 %collective-permute-done.2.got_ref = bf16[8,16,3328]{2,1,0:T(8,128)(2,1)S(1)} collective-permute-done((bf16[8,16,3328]{2,1,0:T(8,128)(2,1)S(1)}, bf16[8,16,3328]{2,1,0:T(8,128)(2,1)S(1)}, u32[]{:S(2)}, u32[]{:S(2)}) %collective-permute-start.2) | collective-permute-done | bytes 852000 | tf_op jit(solution)/shard_map/ppermute | solution.py:279
  21.6 1.1 %shard_map.97 = bf16[8,16,3328]{2,1,0:T(8,128)(2,1)} custom-call(bf16[8,16,3328]{2,1,0:T(8,128)(2,1)S(1)} %get-tuple-element.45.keep_ref, bf16[8,16,3328]{2,1,0:T(8,128)(2,1)S(1)} %collective-permute-done.2.got_ref), custom_call_target="tpu_custom_call" | custom-call | tf_op jit(solution)/shard_map/pallas_call | solution.py:229
  22.7 5.9 %all-to-all-start = ((bf16[8,16,3328]{2,1,0:T(8,128)(2,1)}), bf16[8,16,3328]{2,1,0:T(8,128)(2,1)S(1)}, u32[]{:S(2)}, u32[]{:S(2)}) async-start(bf16[8,16,3328]{2,1,0:T(8,128)(2,1)} %shard_map.97), calls=%async_computation | async-start | bytes 1703936 | tf_op jit(solution)/shard_map/all_to_all | solution.py:287
  28.6 0.0 copy-start.2
  28.6 1.0 %copy-done.2 = bf16[256,1024]{1,0:T(8,128)(2,1)S(1)} copy-done((bf16[256,1024]{1,0:T(8,128)(2,1)S(1)}, bf16[256,1024]{1,0:T(8,128)(2,1)}, u32[]{:S(2)}) %copy-start.2) | copy-done | bytes 524312
  29.7 0.0 copy-start.4
  29.7 1.0 %copy-done.4 = bf16[1024,256]{1,0:T(8,128)(2,1)S(1)} copy-done((bf16[1024,256]{1,0:T(8,128)(2,1)S(1)}, bf16[1024,256]{1,0:T(8,128)(2,1)}, u32[]{:S(2)}) %copy-start.4) | copy-done | bytes 524312
  30.7 0.0 copy-start.6
  30.7 0.9 %copy-done.6 = bf16[256,256]{1,0:T(8,128)(2,1)S(1)} copy-done((bf16[256,256]{1,0:T(8,128)(2,1)S(1)}, bf16[256,256]{1,0:T(8,128)(2,1)}, u32[]{:S(2)}) %copy-start.6) | copy-done | bytes 131096
  31.6 0.0 copy-start.8
  31.6 0.9 %copy-done.8 = bf16[192,256]{1,0:T(8,128)(2,1)S(1)} copy-done((bf16[192,256]{1,0:T(8,128)(2,1)S(1)}, bf16[192,256]{1,0:T(8,128)(2,1)}, u32[]{:S(2)}) %copy-start.8) | copy-done | bytes 98328
  32.5 0.0 copy-start.10
  32.5 0.9 %copy-done.10 = bf16[192,256]{1,0:T(8,128)(2,1)S(1)} copy-done((bf16[192,256]{1,0:T(8,128)(2,1)S(1)}, bf16[192,256]{1,0:T(8,128)(2,1)}, u32[]{:S(2)}) %copy-start.10) | copy-done | bytes 98328
  33.4 0.0 copy-start.12
  33.4 0.8 %copy-done.12 = bf16[128,256]{1,0:T(8,128)(2,1)S(1)} copy-done((bf16[128,256]{1,0:T(8,128)(2,1)S(1)}, bf16[128,256]{1,0:T(8,128)(2,1)}, u32[]{:S(2)}) %copy-start.12) | copy-done | bytes 65560
  34.2 2.1 %shard_map.96 = (bf16[320,1024]{1,0:T(8,128)(2,1)}, bf16[320,1024]{1,0:T(8,128)(2,1)}, f32[8,128]{1,0:T(8,128)S(1)}) custom-call(bf16[320,1024]{1,0:T(8,128)(2,1)S(1)} %get-tuple-element.27.feat_ref, bf16[320,1024]{1,0:T(8,128)(2,1)S(1)} %get-tuple-element.28.grad_ref, bf16[192,256]{1,0:T(8,128)(2,1)S(1)} %copy-done.8, bf16[128,256]{1,0:T(8,128)(2,1)S(1)} %copy-done.12, ...), custom_call_target="tpu_custom_call" | custom-call | tf_op jit(solution)/shard_map/pallas_call | solution.py:229
  36.4 5.3 %all-to-all-done.got_ref = bf16[8,16,3328]{2,1,0:T(8,128)(2,1)S(1)} async-done(((bf16[8,16,3328]{2,1,0:T(8,128)(2,1)}), bf16[8,16,3328]{2,1,0:T(8,128)(2,1)S(1)}, u32[]{:S(2)}, u32[]{:S(2)}) %all-to-all-start) | async-done | bytes 852000 | tf_op jit(solution)/shard_map/all_to_all | solution.py:287
  41.7 0.1 shard_map.98
  41.8 13.8 %all_to_all.15.got_ref = bf16[4,4,3328]{2,1,0:T(4,128)(2,1)S(1)} all-to-all(bf16[4,4,3328]{2,1,0:T(4,128)(2,1)S(1)} %shard_map.98), channel_id=1, replica_groups=mesh['x'=4,'y_hi'=4,'y_lo'=2,'core'=2,'rows'=8] {'y_hi'}, dimensions={0} | all-to-all | bytes 212992 | tf_op jit(solution)/shard_map/all_to_all | solution.py:292
  55.6 19.1 %all_to_all.16.got_ref = bf16[8,4,3328]{2,1,0:T(4,128)(2,1)S(1)} all-to-all(bf16[8,4,3328]{2,1,0:T(4,128)(2,1)S(1)} %shard_map.99), channel_id=1, replica_groups=mesh['x'=4,'y_hi'=4,'y_lo'=2,'core'=2,'rows'=8] {'rows'}, dimensions={0} | all-to-all | bytes 425984 | tf_op jit(solution)/shard_map/all_to_all | solution.py:294
  74.7 0.6 shard_map.100
  (1 shorter events, 0.0 us)
Async XLA Ops:
  0.6 8.0 %copy-start = (bf16[256,2304]{1,0:T(8,128)(2,1)S(1)}, bf16[256,2304]{1,0:T(8,128)(2,1)}, u32[]{:S(2)}) copy-start(bf16[256,2304]{1,0:T(8,128)(2,1)} %conv_ref.5) | copy-start | bytes 3538948
  3.1 13.0 %copy-start.1 = (bf16[256,1024]{1,0:T(8,128)(2,1)}, bf16[256,1024]{1,0:T(8,128)(2,1)S(1)}, u32[]{:S(2)}) copy-start(bf16[256,1024]{1,0:T(8,128)(2,1)S(1)} %get-tuple-element.41.reduce_ref) | copy-start | bytes 1572868
  3.1 13.0 %copy-start.3 = (bf16[1024,256]{1,0:T(8,128)(2,1)}, bf16[1024,256]{1,0:T(8,128)(2,1)S(1)}, u32[]{:S(2)}) copy-start(bf16[1024,256]{1,0:T(8,128)(2,1)S(1)} %get-tuple-element.42.expand_ref) | copy-start | bytes 1572868
  3.1 8.1 %collective-permute-start = (bf16[192,256]{1,0:T(8,128)(2,1)S(1)}, bf16[192,256]{1,0:T(8,128)(2,1)S(1)}, u32[]{:S(2)}, u32[]{:S(2)}) collective-permute-start(bf16[192,256]{1,0:T(8,128)(2,1)S(1)} %get-tuple-element.33), channel_id=1, source_target_pairs={{0,1},{1,2},{2,3},{3,4},{4,5},{5,6},{6,7},{8,9},{9,10},{10,11},{11... | collective-permute-start | bytes 294920 | tf_op jit(solution)/shard_map/ppermute | solution.py:259
  7.4 6.9 %collective-permute-start.1 = (bf16[192,256]{1,0:T(8,128)(2,1)S(1)}, bf16[192,256]{1,0:T(8,128)(2,1)S(1)}, u32[]{:S(2)}, u32[]{:S(2)}) collective-permute-start(bf16[192,256]{1,0:T(8,128)(2,1)S(1)} %get-tuple-element.34), channel_id=1, source_target_pairs={{1,0},{2,1},{3,2},{4,3},{5,4},{6,5},{7,6},{9,8},{10,9},{11,10},{12... | collective-permute-start | bytes 294920 | tf_op jit(solution)/shard_map/ppermute | solution.py:260
  10.5 0.7 copy-start.7
  11.1 4.9 %copy-start.9 = (bf16[192,256]{1,0:T(8,128)(2,1)}, bf16[192,256]{1,0:T(8,128)(2,1)S(1)}, u32[]{:S(2)}) copy-start(bf16[192,256]{1,0:T(8,128)(2,1)S(1)} %get-tuple-element.38.gtwo_in_ref) | copy-start | bytes 294916
  16.0 0.7 copy-start.5
  16.7 0.6 copy-start.11
  17.3 4.3 %collective-permute-start.2 = (bf16[8,16,3328]{2,1,0:T(8,128)(2,1)S(1)}, bf16[8,16,3328]{2,1,0:T(8,128)(2,1)S(1)}, u32[]{:S(2)}, u32[]{:S(2)}) collective-permute-start(bf16[8,16,3328]{2,1,0:T(8,128)(2,1)S(1)} %get-tuple-element.46), channel_id=1, source_target_pairs={{0,8},{8,0},{1,9},{9,1},{2,10},{10,2},{3,11},{11,3},{4,12},{12,4},... | collective-permute-start | bytes 2555912 | tf_op jit(solution)/shard_map/ppermute | solution.py:279
  22.7 19.0 %all-to-all-start = ((bf16[8,16,3328]{2,1,0:T(8,128)(2,1)}), bf16[8,16,3328]{2,1,0:T(8,128)(2,1)S(1)}, u32[]{:S(2)}, u32[]{:S(2)}) async-start(bf16[8,16,3328]{2,1,0:T(8,128)(2,1)} %shard_map.97), calls=%async_computation | async-start | bytes 1703936 | tf_op jit(solution)/shard_map/all_to_all | solution.py:287
  28.6 1.0 %copy-start.2 = (bf16[256,1024]{1,0:T(8,128)(2,1)S(1)}, bf16[256,1024]{1,0:T(8,128)(2,1)}, u32[]{:S(2)}) copy-start(bf16[256,1024]{1,0:T(8,128)(2,1)} %copy-done.1) | copy-start | bytes 1572868
  29.7 1.0 %copy-start.4 = (bf16[1024,256]{1,0:T(8,128)(2,1)S(1)}, bf16[1024,256]{1,0:T(8,128)(2,1)}, u32[]{:S(2)}) copy-start(bf16[1024,256]{1,0:T(8,128)(2,1)} %copy-done.3) | copy-start | bytes 1572868
  30.7 0.9 %copy-start.6 = (bf16[256,256]{1,0:T(8,128)(2,1)S(1)}, bf16[256,256]{1,0:T(8,128)(2,1)}, u32[]{:S(2)}) copy-start(bf16[256,256]{1,0:T(8,128)(2,1)} %copy-done.5) | copy-start | bytes 393220
  31.6 0.9 %copy-start.8 = (bf16[192,256]{1,0:T(8,128)(2,1)S(1)}, bf16[192,256]{1,0:T(8,128)(2,1)}, u32[]{:S(2)}) copy-start(bf16[192,256]{1,0:T(8,128)(2,1)} %copy-done.7) | copy-start | bytes 294916
  32.5 0.9 %copy-start.10 = (bf16[192,256]{1,0:T(8,128)(2,1)S(1)}, bf16[192,256]{1,0:T(8,128)(2,1)}, u32[]{:S(2)}) copy-start(bf16[192,256]{1,0:T(8,128)(2,1)} %copy-done.9) | copy-start | bytes 294916
  33.4 0.8 %copy-start.12 = (bf16[128,256]{1,0:T(8,128)(2,1)S(1)}, bf16[128,256]{1,0:T(8,128)(2,1)}, u32[]{:S(2)}) copy-start(bf16[128,256]{1,0:T(8,128)(2,1)} %copy-done.11) | copy-start | bytes 196612

commit v5 on v4

--- a/solution.py
+++ b/solution.py
@@ -27,15 +27,15 @@
     )
 
 
-def active_column(halt_ref):
-    rows, _, cols = halt_ref.shape
+def active_column(halt_ref, rows):
+    cols = halt_ref.shape[2]
     at_row = lax.broadcasted_iota(jnp.int32, (cols, cols), 0)
     at_col = lax.broadcasted_iota(jnp.int32, (cols, cols), 1)
     parts = [
         jnp.sum(
             jnp.where((at_row == at_col) & (halt_ref[r] > UNIT), 1.0, 0.0), axis=1, keepdims=True
         )
-        for r in range(rows)
+        for r in rows
     ]
     return jnp.concatenate(parts, axis=0)
 
@@ -43,7 +43,7 @@
 def neighbours(cells, cols):
     count = cells.shape[0]
     wide = cells.astype(F32)
-    col = lax.rem(lax.broadcasted_iota(jnp.int32, (count, 1), 0), cols)
+    col = lax.broadcasted_iota(jnp.int32, (count, 1), 0) & (cols - 1)
     left = jnp.where(col == 0, 0.0, pltpu.roll(wide, 1, 0))
     right = jnp.where(col == cols - 1, 0.0, pltpu.roll(wide, count - 1, 0))
     return left.astype(BF), right.astype(BF)
@@ -75,7 +75,7 @@
     down_ref[0 : 2 * cols, :] = hidden[(rows - 2) * cols :]
     for copy in copies[2:]:
         copy.wait()
-    back = (active_column(halt_ref) * dot(grad_ref[...], expand_ref[...], 1, 0)).astype(BF)
+    back = (active_column(halt_ref, range(rows)) * dot(grad_ref[...], expand_ref[...], 1, 0)).astype(BF)
     back_ref[...] = back
     up_ref[2 * cols :, :] = back[0:cols]
     down_ref[2 * cols :, :] = back[(rows - 1) * cols :]
@@ -92,13 +92,12 @@
 
 
 def sorting(width):
-    shape = (width, width)
-    per_dp = width // (NX * NH * NL * NC)
-    at = lax.broadcasted_iota(jnp.int32, shape, 0)
-    j, hi, lo = at % per_dp, (at // per_dp) % NH, (at // (per_dp * NH)) % NL
-    x, c = (at // (per_dp * NH * NL)) % NX, at // (per_dp * NH * NL * NX)
-    wanted = dp_of(x, hi, lo, c ^ lax.axis_index("core")) * per_dp + j
-    return (lax.broadcasted_iota(jnp.int32, shape, 1) == wanted).astype(F32).astype(BF)
+    at = lax.broadcasted_iota(jnp.int32, (width, 1), 0)
+    j, hi, lo = at & 3, (at >> 2) & (NH - 1), (at >> 4) & (NL - 1)
+    x, c = (at >> 5) & (NX - 1), at >> 7
+    wanted = dp_of(x, hi, lo, c ^ lax.axis_index("core")) * 4 + j
+    channel = lax.broadcasted_iota(jnp.int32, (width, width), 1)
+    return (channel == wanted).astype(F32).astype(BF)
 
 
 def inner_kernel(
@@ -111,7 +110,7 @@
     pre_two = dot(columns_ref[...], conv_ref[...], 1, 1)
     grad_two = jnp.where(pre_two > 0, back_ref[inner, :].astype(F32), 0.0).astype(BF)
     gtwo_ref[...] = grad_two
-    hidden_two = (active_column(halt_ref)[inner] * jnp.maximum(pre_two, 0.0)).astype(BF)
+    hidden_two = (active_column(halt_ref, range(1, rows - 1)) * jnp.maximum(pre_two, 0.0)).astype(BF)
     two_ref[...] = hidden_two
     grad_rows = dot(sorting(grad_two.shape[1]), grad_two, 1, 1).astype(BF)
     cpart_ref[...] = dot(grad_rows, columns_ref[...], 1, 0)
@@ -135,20 +134,21 @@
     back = jnp.concatenate([prev_ref[halo:], back_ref[top, :], back_ref[end, :], next_ref[halo:]], axis=0)
     grad_two = jnp.where(pre_two > 0, back.astype(F32), 0.0).astype(BF)
     gtwo_ref[...] = grad_two
-    active = active_column(halt_ref)
-    active = jnp.concatenate([active[top], active[end]], axis=0)
+    active = active_column(halt_ref, (0, rows - 1))
     own = slice(cols, cols + halo)
     hidden_two = (active * jnp.maximum(pre_two[own], 0.0)).astype(BF)
     two_ref[...] = hidden_two
 
     grad_rows = dot(sorting(width), grad_two[own], 1, 1).astype(BF)
     conv_part = (cpart_ref[...] + dot(grad_rows, columns_ref[own, :], 1, 0)).astype(BF)
-    per_dp, lanes = width // (NX * NH * NL * NC), conv_part.shape[1]
-    tall = per_dp * NH
+    tall = width // (NX * NL * NC)
+    taps = conv_part.shape[1] // width
     for group in range(NX * NL):
-        keep_ref[group, :, 0:lanes] = conv_part[group * tall : (group + 1) * tall]
         other = NX * NL + group
-        send_ref[group, :, 0:lanes] = conv_part[other * tall : (other + 1) * tall]
+        for tap in range(taps):
+            to, at = slice(tap * tall, (tap + 1) * tall), slice(tap * width, (tap + 1) * width)
+            keep_ref[group, to, :] = conv_part[group * tall : (group + 1) * tall, at]
+            send_ref[group, to, :] = conv_part[other * tall : (other + 1) * tall, at]
     upstream = jnp.concatenate([grad_ref[top, :], grad_ref[end, :]], axis=0)
     expand_part = (epart_ref[...] + dot(upstream, hidden_two, 0, 0)).astype(BF)
     per_dp = expand_part.shape[0] // (NX * NH * NL * NC)
@@ -157,9 +157,9 @@
             for hi in range(NH):
                 first = dp_of(x, hi, lo, 0) * per_dp
                 zero, one = (expand_part[first + i * per_dp : first + (i + 1) * per_dp] for i in (0, 1))
-                at = slice(lanes + hi * width, lanes + (hi + 1) * width)
-                keep_ref[x * NL + lo, :, at] = jnp.where(core == 0, zero, one)
-                send_ref[x * NL + lo, :, at] = jnp.where(core == 0, one, zero)
+                to = slice(taps * tall + hi * per_dp, taps * tall + (hi + 1) * per_dp)
+                keep_ref[x * NL + lo, to, :] = jnp.where(core == 0, zero, one)
+                send_ref[x * NL + lo, to, :] = jnp.where(core == 0, one, zero)
 
 
 def leave_kernel(
@@ -191,19 +191,22 @@
     return total
 
 
-def core_kernel(keep_ref, got_ref, out_ref):
+def core_kernel(keep_ref, got_ref, done_ref, out_ref):
     out_ref[...] = (keep_ref[...].astype(F32) + got_ref[...].astype(F32)).astype(BF)
 
 
-def x_kernel(got_ref, done_ref, out_ref, *, taps, width):
-    total = sum_of(got_ref)
+def x_kernel(got_ref, out_ref, *, taps):
+    total = sum_of(got_ref).astype(BF)
     highs, count, lanes = out_ref.shape
+    width = total.shape[1]
+    blocks = lanes // width
     for hi in range(highs):
-        out_ref[hi, :, 0:taps] = total[hi * count : (hi + 1) * count, 0:taps].astype(BF)
-        at = slice(taps + hi * width, taps + (hi + 1) * width)
-        for q in range((lanes - taps) // width):
-            to = slice(taps + q * width, taps + (q + 1) * width)
-            out_ref[hi, :, to] = total[q * count : (q + 1) * count, at].astype(BF)
+        for i in range(blocks):
+            if i < taps:
+                first = (i * highs + hi) * count
+            else:
+                first = (taps * highs + hi * (blocks - taps) + i - taps) * count
+            out_ref[hi, :, i * width : (i + 1) * width] = total[first : first + count]
 
 
 def y_kernel(got_ref, out_ref):
@@ -260,8 +263,7 @@
     from_next = lax.ppermute(up, "rows", [(i + 1, i) for i in range(NZ - 1)])
 
     conv_rows, expand_rows = width // (NX * NH * NL * NC), chans // (NX * NH * NL * NC)
-    lanes = taps + NH * width
-    part = (NX * NL, NH * conv_rows, lanes)
+    part = (NX * NL, NH * (conv_rows * taps // width + expand_rows), width)
     inner = (own - 2 * cols, width)
     conv_part, expand_part, two_in, gtwo_in = call(
         inner_kernel,
@@ -283,11 +285,11 @@
         flat_in, upstream, two_in, two, gtwo_in, gtwo, sign, reduce_in, weight_conv, expand_in,
         scratch=[pltpu.VMEM((own, taps), BF), pltpu.VMEM((taps, width), BF)],
     )
-    (total,) = call(core_kernel, [pltpu.VMEM(part, BF)], keep, got)
+    (total,) = call(core_kernel, [pltpu.VMEM(part, BF)], keep, got, done)
     got = lax.all_to_all(total, ("x", "y_lo"), 0, 0, tiled=True)
     shard = (conv_rows, taps + expand_rows // conv_rows * width)
     (total,) = call(
-        functools.partial(x_kernel, taps=taps, width=width), [pltpu.VMEM((NH,) + shard, BF)], got, done
+        functools.partial(x_kernel, taps=taps // width), [pltpu.VMEM((NH,) + shard, BF)], got
     )
     got = lax.all_to_all(total, "y_hi", 0, 0, tiled=True)
     (total,) = call(y_kernel, [pltpu.VMEM((NZ,) + shard, BF)], got)

time: 75.9 us -> 73.5 us (0.968)
  blocking collectives: 32.9 us -> 51.9 us
  local copies, waits for them, and re-layouts: 7.54 us -> 0.01 us
  waiting for transfers between devices: 10.7 us -> 3.95 us
  starting transfers between devices: 13.4 us -> 7.49 us
  Pallas kernels: 10 us -> 9.1 us
    all_to_all x0 -> x1, blocking collectives: none -> 18.4 us  [local(): got = lax.all_to_all(total, ('x', 'y_lo'), 0, 0, tiled=True)]
    unnamed x26 -> x2, local copies, waits for them, and re-layouts: 7.54 us -> 0.01 us
    all_to_all x1 -> x0, starting transfers between devices: 5.93 us -> none  [local(): got = lax.all_to_all(total, ('x', 'y_lo'), 0, 0, tiled=True)]
    all_to_all x1 -> x0, waiting for transfers between devices: 5.29 us -> none  [local(): got = lax.all_to_all(total, ('x', 'y_lo'), 0, 0, tiled=True)]
    ppermute x1, waiting for transfers between devices: 2.34 us -> 0.21 us  [local(): got = lax.ppermute(send, 'core', [(0, 1), (1, 0)])]
    pallas_call x7, Pallas kernels: 7.61 us -> 6.69 us  [call(): pl.pallas_call(kernel, out_shape=outs, scratch_shapes=list(scratch), comp...]
  transfers between devices with their start and end apart: 4 -> 3, of which waited for: 3 -> 2; matrix products, arithmetic and copies ran while one was open for 0% -> 0% of each run, Pallas kernels for 5% -> 5%
where the time goes in v5:
time: 73.5 us; the launch traced here: 73.2 us
  blocking collectives  51.9 us (71%)
  Pallas kernels  9.1 us (12%)
  starting transfers between devices  7.49 us (10%)
  waiting for transfers between devices  3.95 us (5%)
    all_to_all x1, blocking collectives, local(): got = lax.all_to_all(total, 'rows', 0, 0, tiled=True)  19.1 us
    all_to_all x1, blocking collectives, local(): got = lax.all_to_all(total, ('x', 'y_lo'), 0, 0, tiled=True)  18.4 us
    all_to_all x1, blocking collectives, local(): got = lax.all_to_all(total, 'y_hi', 0, 0, tiled=True)  14.4 us
    pallas_call x7, Pallas kernels, call(): pl.pallas_call(kernel, out_shape=outs, scratch_shapes=list(scratch), comp...  6.69 us
    ppermute x1, starting transfers between devices, local(): from_prev = lax.ppermute(down, 'rows', [(i, i + 1) for i in range(NZ - 1)])  4.28 us
    ppermute x1, waiting for transfers between devices, local(): from_next = lax.ppermute(up, 'rows', [(i + 1, i) for i in range(NZ - 1)])  3.75 us
    pallas_call x1, Pallas kernels, local(): pl.pallas_call(enter_kernel, out_shape=[pltpu.VMEM(a.shape, a.dtype) for...  2.41 us
    ppermute x1, starting transfers between devices, local(): got = lax.ppermute(send, 'core', [(0, 1), (1, 0)])  1.92 us
  transfers between devices with their start and end apart: 3, of which 2 were waited for; matrix products, arithmetic and copies ran while one was open for 0% of the time, Pallas kernels for 5%

profile of v5, /device:TPU:8, one launch (start us, length us, event | category | flops | bytes accessed | tf_op | source)
XLA Modules:
  0.0 73.2 jit_solution(5125101354922651131)
XLA Ops:
  0.6 0.0 copy-start
  0.6 2.4 %shard_map.93 = (s32[5,1,64]{2,1,0:T(1,128)S(1)}, bf16[320,1024]{1,0:T(8,128)(2,1)S(1)}, bf16[320,1024]{1,0:T(8,128)(2,1)S(1)}, bf16[256,1024]{1,0:T(8,128)(2,1)...) custom-call(s32[5,1,64]{2,1,0:T(1,128)} %bitcast.7, ...), custom_call_target="tpu_custom_call" | custom-call | tf_op jit(solution)/shard_map/pallas_call | solution.py:253
  3.1 4.3 %collective-permute-start = (bf16[192,256]{1,0:T(8,128)(2,1)S(1)}, bf16[192,256]{1,0:T(8,128)(2,1)S(1)}, u32[]{:S(2)}, u32[]{:S(2)}) collective-permute-start(bf16[192,256]{1,0:T(8,128)(2,1)S(1)} %get-tuple-element.33), channel_id=1, source_target_pairs={{0,1},{1,2},{2,3},{3,4},{4,5},{5,6},{6,7},{8,9},{9,10},{10,11},{11... | collective-permute-start | bytes 294920 | tf_op jit(solution)/shard_map/ppermute | solution.py:262
  7.3 1.3 %collective-permute-start.1 = (bf16[192,256]{1,0:T(8,128)(2,1)S(1)}, bf16[192,256]{1,0:T(8,128)(2,1)S(1)}, u32[]{:S(2)}, u32[]{:S(2)}) collective-permute-start(bf16[192,256]{1,0:T(8,128)(2,1)S(1)} %get-tuple-element.34), channel_id=1, source_target_pairs={{1,0},{2,1},{3,2},{4,3},{5,4},{6,5},{7,6},{9,8},{10,9},{11,10},{12... | collective-permute-start | bytes 294920 | tf_op jit(solution)/shard_map/ppermute | solution.py:263
  8.6 0.0 copy-done
  8.7 1.8 %shard_map.94 = (f32[256,2304]{1,0:T(8,128)S(1)}, f32[1024,256]{1,0:T(8,128)S(1)}, bf16[192,256]{1,0:T(8,128)(2,1)S(1)}, bf16[192,256]{1,0:T(8,128)(2,1)S(1)}) custom-call(s32[5,1,64]{2,1,0:T(1,128)S(1)} %get-tuple-element.29.halt_ref, bf16[320,256]{1,0:T(8,128)(2,1)S(1)} %get-tuple-element.30.hidden_ref, bf16[320,256]{1,0:T(8,128)(2,1)S(1)} %get-tuple-element.31.back_ref, ...), custom_call_target="tpu_custom_call" | custom-call | tf_op jit(solution)/shard_map/pallas_call | solution.py:232
  10.5 0.0 collective-permute-done.prev_ref
  10.5 3.7 %collective-permute-done.1.next_ref = bf16[192,256]{1,0:T(8,128)(2,1)S(1)} collective-permute-done((bf16[192,256]{1,0:T(8,128)(2,1)S(1)}, bf16[192,256]{1,0:T(8,128)(2,1)S(1)}, u32[]{:S(2)}, u32[]{:S(2)}) %collective-permute-start.1) | collective-permute-done | bytes 98336 | tf_op jit(solution)/shard_map/ppermute | solution.py:263
  14.2 1.8 %shard_map.95 = (bf16[8,208,256]{2,1,0:T(8,128)(2,1)S(1)}, bf16[8,208,256]{2,1,0:T(8,128)(2,1)S(1)}, bf16[128,256]{1,0:T(8,128)(2,1)S(1)}, bf16[256,256]{1,0:T(8,128)(2,1)S(1)}) custom-call(s32[5,1,64]{2,1,0:T(1,128)S(1)} %get-tuple-element.29.halt_ref, bf16[320,256]{1,0:T(8,128)(2,1)S(1)} %get-tuple-element.30.hidden_ref, ...), custom_call_target="tpu_custom_call" | custom-call | tf_op jit(solution)/shard_map/pallas_call | solution.py:232
  16.0 1.9 %collective-permute-start.2 = (bf16[8,208,256]{2,1,0:T(8,128)(2,1)S(1)}, bf16[8,208,256]{2,1,0:T(8,128)(2,1)S(1)}, u32[]{:S(2)}, u32[]{:S(2)}) collective-permute-start(bf16[8,208,256]{2,1,0:T(8,128)(2,1)S(1)} %get-tuple-element.46), channel_id=1, source_target_pairs={{0,8},{8,0},{1,9},{9,1},{2,10},{10,2},{3,11},{11,3},{4,12},{12,4},... | collective-permute-start | bytes 2555912 | tf_op jit(solution)/shard_map/ppermute | solution.py:281
  17.9 2.1 %shard_map.96 = (bf16[320,1024]{1,0:T(8,128)(2,1)}, bf16[320,1024]{1,0:T(8,128)(2,1)}, f32[8,128]{1,0:T(8,128)S(1)}) custom-call(bf16[320,1024]{1,0:T(8,128)(2,1)S(1)} %get-tuple-element.27.feat_ref, bf16[320,1024]{1,0:T(8,128)(2,1)S(1)} %get-tuple-element.28.grad_ref, bf16[192,256]{1,0:T(8,128)(2,1)S(1)} %get-tuple-element.32.two_in_ref, ...), custom_call_target="tpu_custom_call" | custom-call | tf_op jit(solution)/shard_map/pallas_call | solution.py:232
  20.1 0.2 collective-permute-done.2.got_ref
  20.3 0.2 shard_map.97
  20.5 18.4 %all_to_all.15.got_ref = bf16[8,208,256]{2,1,0:T(8,128)(2,1)S(1)} all-to-all(bf16[8,208,256]{2,1,0:T(8,128)(2,1)S(1)} %shard_map.97), channel_id=1, replica_groups=mesh['x'=4,'y_hi'=4,'y_lo'=2,'core'=2,'rows'=8] {'x','y_lo'}, dimensions={0} | all-to-all | bytes 1703936 | tf_op jit(solution)/shard_map/all_to_all | solution.py:289
  38.9 0.1 shard_map.98
  39.0 14.4 %all_to_all.16.got_ref = bf16[4,4,3328]{2,1,0:T(4,128)(2,1)S(1)} all-to-all(bf16[4,4,3328]{2,1,0:T(4,128)(2,1)S(1)} %shard_map.98), channel_id=1, replica_groups=mesh['x'=4,'y_hi'=4,'y_lo'=2,'core'=2,'rows'=8] {'y_hi'}, dimensions={0} | all-to-all | bytes 212992 | tf_op jit(solution)/shard_map/all_to_all | solution.py:294
  53.5 19.1 %all_to_all.17.got_ref = bf16[8,4,3328]{2,1,0:T(4,128)(2,1)S(1)} all-to-all(bf16[8,4,3328]{2,1,0:T(4,128)(2,1)S(1)} %shard_map.99), channel_id=1, replica_groups=mesh['x'=4,'y_hi'=4,'y_lo'=2,'core'=2,'rows'=8] {'rows'}, dimensions={0} | all-to-all | bytes 425984 | tf_op jit(solution)/shard_map/all_to_all | solution.py:296
  72.6 0.6 shard_map.100
  (1 shorter events, 0.0 us)
Async XLA Ops:
  0.6 8.0 %copy-start = (bf16[256,2304]{1,0:T(8,128)(2,1)S(1)}, bf16[256,2304]{1,0:T(8,128)(2,1)}, u32[]{:S(2)}) copy-start(bf16[256,2304]{1,0:T(8,128)(2,1)} %conv_ref.5) | copy-start | bytes 3538948
  3.1 7.4 %collective-permute-start = (bf16[192,256]{1,0:T(8,128)(2,1)S(1)}, bf16[192,256]{1,0:T(8,128)(2,1)S(1)}, u32[]{:S(2)}, u32[]{:S(2)}) collective-permute-start(bf16[192,256]{1,0:T(8,128)(2,1)S(1)} %get-tuple-element.33), channel_id=1, source_target_pairs={{0,1},{1,2},{2,3},{3,4},{4,5},{5,6},{6,7},{8,9},{9,10},{10,11},{11... | collective-permute-start | bytes 294920 | tf_op jit(solution)/shard_map/ppermute | solution.py:262
  7.3 6.9 %collective-permute-start.1 = (bf16[192,256]{1,0:T(8,128)(2,1)S(1)}, bf16[192,256]{1,0:T(8,128)(2,1)S(1)}, u32[]{:S(2)}, u32[]{:S(2)}) collective-permute-start(bf16[192,256]{1,0:T(8,128)(2,1)S(1)} %get-tuple-element.34), channel_id=1, source_target_pairs={{1,0},{2,1},{3,2},{4,3},{5,4},{6,5},{7,6},{9,8},{10,9},{11,10},{12... | collective-permute-start | bytes 294920 | tf_op jit(solution)/shard_map/ppermute | solution.py:263
  16.0 4.3 %collective-permute-start.2 = (bf16[8,208,256]{2,1,0:T(8,128)(2,1)S(1)}, bf16[8,208,256]{2,1,0:T(8,128)(2,1)S(1)}, u32[]{:S(2)}, u32[]{:S(2)}) collective-permute-start(bf16[8,208,256]{2,1,0:T(8,128)(2,1)S(1)} %get-tuple-element.46), channel_id=1, source_target_pairs={{0,8},{8,0},{1,9},{9,1},{2,10},{10,2},{3,11},{11,3},{4,12},{12,4},... | collective-permute-start | bytes 2555912 | tf_op jit(solution)/shard_map/ppermute | solution.py:281

commit v6 on v5

--- a/solution.py
+++ b/solution.py
@@ -11,14 +11,43 @@
 BF = jnp.bfloat16
 F32 = jnp.float32
 
-AXES = ("x", "y_hi", "y_lo", "core", "rows")
-NX, NH, NL, NC, NZ = SIZES = (4, 4, 2, 2, 8)
-DP = AXES[:4]
+AXES = ("x_hi", "x_lo", "y_hi", "y_lo", "core", "rows")
+SIZES = (2, 2, 4, 2, 2, 8)
+DP = AXES[:5]
+NX, NY, NC, NZ = 4, 8, 2, 8
+HX, HY, HZ = NX // 2, NY // 2, NZ // 2
 VMEM_LIMIT = pltpu.CompilerParams(vmem_limit_bytes=20 * 1024 * 1024)
 
 
-def dp_of(x, hi, lo, core):
-    return ((x * NH + hi) * NL + lo) * NC + core
+def dp_of(x, y, core):
+    return (x * NY + y) * NC + core
+
+
+def squares():
+    def member(block, parity, size, core):
+        return (2 * block + parity) % size if core == 0 or parity == 1 else (2 * block + 2) % size
+
+    return [
+        [dp_of(member(bx, i, NX, core), member(by, j, NY, core), core) for i in (0, 1) for j in (0, 1)]
+        for core in range(NC)
+        for bx in range(HX)
+        for by in range(HY)
+    ]
+
+
+def rest():
+    return [
+        [
+            dp_of(2 * x_hi + x, 2 * y_hi + y, core) * NZ + 2 * z + low
+            for x_hi in range(HX)
+            for y_hi in range(HY)
+            for low in range(2)
+        ]
+        for x in range(2)
+        for y in range(2)
+        for core in range(NC)
+        for z in range(HZ)
+    ]
 
 
 def dot(left, right, left_dim, right_dim):
@@ -93,9 +122,9 @@
 
 def sorting(width):
     at = lax.broadcasted_iota(jnp.int32, (width, 1), 0)
-    j, hi, lo = at & 3, (at >> 2) & (NH - 1), (at >> 4) & (NL - 1)
-    x, c = (at >> 5) & (NX - 1), at >> 7
-    wanted = dp_of(x, hi, lo, c ^ lax.axis_index("core")) * 4 + j
+    j, y_hi, x_hi = at & 3, (at >> 2) & (HY - 1), (at >> 4) & (HX - 1)
+    y_lo, x_lo, c = (at >> 5) & 1, (at >> 6) & 1, at >> 7
+    wanted = dp_of(2 * x_hi + x_lo, 2 * y_hi + y_lo, c ^ lax.axis_index("core")) * 4 + j
     channel = lax.broadcasted_iota(jnp.int32, (width, width), 1)
     return (channel == wanted).astype(F32).astype(BF)
 
@@ -141,25 +170,26 @@
 
     grad_rows = dot(sorting(width), grad_two[own], 1, 1).astype(BF)
     conv_part = (cpart_ref[...] + dot(grad_rows, columns_ref[own, :], 1, 0)).astype(BF)
-    tall = width // (NX * NL * NC)
+    tall = width // 8
     taps = conv_part.shape[1] // width
-    for group in range(NX * NL):
-        other = NX * NL + group
+    for place in range(4):
+        other = 4 + place
         for tap in range(taps):
             to, at = slice(tap * tall, (tap + 1) * tall), slice(tap * width, (tap + 1) * width)
-            keep_ref[group, to, :] = conv_part[group * tall : (group + 1) * tall, at]
-            send_ref[group, to, :] = conv_part[other * tall : (other + 1) * tall, at]
+            keep_ref[place, to, :] = conv_part[place * tall : (place + 1) * tall, at]
+            send_ref[place, to, :] = conv_part[other * tall : (other + 1) * tall, at]
     upstream = jnp.concatenate([grad_ref[top, :], grad_ref[end, :]], axis=0)
     expand_part = (epart_ref[...] + dot(upstream, hidden_two, 0, 0)).astype(BF)
-    per_dp = expand_part.shape[0] // (NX * NH * NL * NC)
+    per_dp = expand_part.shape[0] // (NX * NY * NC)
     for x in range(NX):
-        for lo in range(NL):
-            for hi in range(NH):
-                first = dp_of(x, hi, lo, 0) * per_dp
-                zero, one = (expand_part[first + i * per_dp : first + (i + 1) * per_dp] for i in (0, 1))
-                to = slice(taps * tall + hi * per_dp, taps * tall + (hi + 1) * per_dp)
-                keep_ref[x * NL + lo, to, :] = jnp.where(core == 0, zero, one)
-                send_ref[x * NL + lo, to, :] = jnp.where(core == 0, one, zero)
+        for y in range(NY):
+            first = dp_of(x, y, 0) * per_dp
+            zero, one = (expand_part[first + i * per_dp : first + (i + 1) * per_dp] for i in (0, 1))
+            mine, theirs = jnp.where(core == 0, zero, one), jnp.where(core == 0, one, zero)
+            start = taps * tall + (x // 2 * HY + y // 2) * per_dp
+            place = x % 2 * 2 + y % 2
+            keep_ref[place, start : start + per_dp, :] = mine
+            send_ref[place, start : start + per_dp, :] = theirs
 
 
 def leave_kernel(
@@ -195,33 +225,42 @@
     out_ref[...] = (keep_ref[...].astype(F32) + got_ref[...].astype(F32)).astype(BF)
 
 
-def x_kernel(got_ref, out_ref, *, taps):
+def square_kernel(got_ref, out_ref, *, taps):
     total = sum_of(got_ref).astype(BF)
-    highs, count, lanes = out_ref.shape
-    width = total.shape[1]
-    blocks = lanes // width
-    for hi in range(highs):
+    parts, count, lanes = out_ref.shape
+    half = total.shape[1] // 2
+    shards, blocks = parts // 2, lanes // half
+    for shard in range(shards):
         for i in range(blocks):
             if i < taps:
-                first = (i * highs + hi) * count
+                first = (i * shards + shard) * count
             else:
-                first = (taps * highs + hi * (blocks - taps) + i - taps) * count
-            out_ref[hi, :, i * width : (i + 1) * width] = total[first : first + count]
-
-
-def y_kernel(got_ref, out_ref):
+                first = (taps * shards + shard * (blocks - taps) + i - taps) * count
+            for low in range(2):
+                block = total[first : first + count, low * half : (low + 1) * half]
+                out_ref[2 * shard + low, :, i * half : (i + 1) * half] = block
+
+
+def plane_kernel(got_ref, out_ref):
     total = sum_of(got_ref).astype(BF)
     for z in range(out_ref.shape[0]):
         out_ref[z] = total
 
 
-def z_kernel(got_ref, conv_ref, expand_ref):
-    total = sum_of(got_ref)
-    count, taps = conv_ref.shape
-    width = expand_ref.shape[1]
-    conv_ref[...] = total[:, 0:taps]
-    for q in range(expand_ref.shape[0] // count):
-        expand_ref[q * count : (q + 1) * count, :] = total[:, taps + q * width : taps + (q + 1) * width]
+def rows_kernel(got_ref, conv_ref, expand_ref):
+    count, width = conv_ref.shape[0], expand_ref.shape[1]
+    half, taps = width // 2, conv_ref.shape[1] // width
+    for low in range(2):
+        total = got_ref[low].astype(F32)
+        for z in range(low + 2, NZ, 2):
+            total = total + got_ref[z].astype(F32)
+        for i in range(got_ref.shape[2] // half):
+            block = total[:, i * half : (i + 1) * half]
+            if i < taps:
+                conv_ref[:, i * width + low * half : i * width + (low + 1) * half] = block
+            else:
+                first = (i - taps) * count
+                expand_ref[first : first + count, low * half : (low + 1) * half] = block
 
 
 def in_vmem(array):
@@ -262,8 +301,10 @@
     from_prev = lax.ppermute(down, "rows", [(i, i + 1) for i in range(NZ - 1)])
     from_next = lax.ppermute(up, "rows", [(i + 1, i) for i in range(NZ - 1)])
 
-    conv_rows, expand_rows = width // (NX * NH * NL * NC), chans // (NX * NH * NL * NC)
-    part = (NX * NL, NH * (conv_rows * taps // width + expand_rows), width)
+    devices = NX * NY * NC
+    conv_rows, expand_rows = width // devices, chans // devices
+    shard_rows = conv_rows * taps // width + expand_rows
+    part = (4, HX * HY * shard_rows, width)
     inner = (own - 2 * cols, width)
     conv_part, expand_part, two_in, gtwo_in = call(
         inner_kernel,
@@ -286,16 +327,16 @@
         scratch=[pltpu.VMEM((own, taps), BF), pltpu.VMEM((taps, width), BF)],
     )
     (total,) = call(core_kernel, [pltpu.VMEM(part, BF)], keep, got, done)
-    got = lax.all_to_all(total, ("x", "y_lo"), 0, 0, tiled=True)
-    shard = (conv_rows, taps + expand_rows // conv_rows * width)
+    got = lax.all_to_all(total, DP, 0, 0, axis_index_groups=squares(), tiled=True)
+    shard = (conv_rows, shard_rows // conv_rows * width // 2)
     (total,) = call(
-        functools.partial(x_kernel, taps=taps // width), [pltpu.VMEM((NH,) + shard, BF)], got
-    )
-    got = lax.all_to_all(total, "y_hi", 0, 0, tiled=True)
-    (total,) = call(y_kernel, [pltpu.VMEM((NZ,) + shard, BF)], got)
+        functools.partial(square_kernel, taps=taps // width), [pltpu.VMEM((2 * HX * HY,) + shard, BF)], got
+    )
+    got = lax.all_to_all(total, AXES, 0, 0, axis_index_groups=rest(), tiled=True)
+    (total,) = call(plane_kernel, [pltpu.VMEM((NZ,) + shard, BF)], got)
     got = lax.all_to_all(total, "rows", 0, 0, tiled=True)
     grad_conv, grad_expand = call(
-        z_kernel,
+        rows_kernel,
         [jax.ShapeDtypeStruct((conv_rows, taps), F32), jax.ShapeDtypeStruct((expand_rows, width), F32)],
         got,
     )

time: 73.5 us -> 73 us (level)
    all_to_all x1, blocking collectives: 19.1 us -> 16.7 us  [local(): got = lax.all_to_all(total, 'rows', 0, 0, tiled=True)]
    all_to_all x2, blocking collectives: 32.9 us -> 34.7 us  [the longest x1 22 us: local(): lax.all_to_all(total, AXES, 0, 0, axis_index_groups=rest(), tiled=True)]
where the time goes in v6:
time: 73 us; the launch traced here: 72.7 us
  blocking collectives  51.4 us (70%)
  Pallas kernels  9.14 us (13%)
  starting transfers between devices  7.49 us (10%)
  waiting for transfers between devices  3.96 us (5%)
    all_to_all x1, blocking collectives, local(): lax.all_to_all(total, AXES, 0, 0, axis_index_groups=rest(), tiled=True)  22 us
    all_to_all x1, blocking collectives, local(): got = lax.all_to_all(total, 'rows', 0, 0, tiled=True)  16.7 us
    all_to_all x1, blocking collectives, local(): lax.all_to_all(total, DP, 0, 0, axis_index_groups=squares(), tiled=True)  12.6 us
    pallas_call x7, Pallas kernels, call(): pl.pallas_call(kernel, out_shape=outs, scratch_shapes=list(scratch), comp...  6.73 us
    ppermute x1, starting transfers between devices, local(): from_prev = lax.ppermute(down, 'rows', [(i, i + 1) for i in range(NZ - 1)])  4.28 us
    ppermute x1, waiting for transfers between devices, local(): from_next = lax.ppermute(up, 'rows', [(i + 1, i) for i in range(NZ - 1)])  3.75 us
    pallas_call x1, Pallas kernels, local(): pl.pallas_call(enter_kernel, out_shape=[pltpu.VMEM(a.shape, a.dtype) for...  2.41 us
    ppermute x1, starting transfers between devices, local(): got = lax.ppermute(send, 'core', [(0, 1), (1, 0)])  1.92 us
  transfers between devices with their start and end apart: 3, of which 2 were waited for; matrix products, arithmetic and copies ran while one was open for 0% of the time, Pallas kernels for 5%

profile of v6, /device:TPU:8, one launch (start us, length us, event | category | flops | bytes accessed | tf_op | source)
XLA Modules:
  0.0 72.7 jit_solution(5109834533065020132)
XLA Ops:
  0.6 0.0 copy-start
  0.6 2.4 %shard_map.93 = (s32[5,1,64]{2,1,0:T(1,128)S(1)}, bf16[320,1024]{1,0:T(8,128)(2,1)S(1)}, bf16[320,1024]{1,0:T(8,128)(2,1)S(1)}, bf16[256,1024]{1,0:T(8,128)(2,1)...) custom-call(s32[5,1,64]{2,1,0:T(1,128)} %bitcast.7, ...), custom_call_target="tpu_custom_call" | custom-call | tf_op jit(solution)/shard_map/pallas_call | solution.py:292
  3.1 4.3 %collective-permute-start = (bf16[192,256]{1,0:T(8,128)(2,1)S(1)}, bf16[192,256]{1,0:T(8,128)(2,1)S(1)}, u32[]{:S(2)}, u32[]{:S(2)}) collective-permute-start(bf16[192,256]{1,0:T(8,128)(2,1)S(1)} %get-tuple-element.33), channel_id=1, source_target_pairs={{0,1},{1,2},{2,3},{3,4},{4,5},{5,6},{6,7},{8,9},{9,10},{10,11},{11... | collective-permute-start | bytes 294920 | tf_op jit(solution)/shard_map/ppermute | solution.py:301
  7.3 1.3 %collective-permute-start.1 = (bf16[192,256]{1,0:T(8,128)(2,1)S(1)}, bf16[192,256]{1,0:T(8,128)(2,1)S(1)}, u32[]{:S(2)}, u32[]{:S(2)}) collective-permute-start(bf16[192,256]{1,0:T(8,128)(2,1)S(1)} %get-tuple-element.34), channel_id=1, source_target_pairs={{1,0},{2,1},{3,2},{4,3},{5,4},{6,5},{7,6},{9,8},{10,9},{11,10},{12... | collective-permute-start | bytes 294920 | tf_op jit(solution)/shard_map/ppermute | solution.py:302
  8.6 0.0 copy-done
  8.7 1.8 %shard_map.94 = (f32[256,2304]{1,0:T(8,128)S(1)}, f32[1024,256]{1,0:T(8,128)S(1)}, bf16[192,256]{1,0:T(8,128)(2,1)S(1)}, bf16[192,256]{1,0:T(8,128)(2,1)S(1)}) custom-call(s32[5,1,64]{2,1,0:T(1,128)S(1)} %get-tuple-element.29.halt_ref, bf16[320,256]{1,0:T(8,128)(2,1)S(1)} %get-tuple-element.30.hidden_ref, bf16[320,256]{1,0:T(8,128)(2,1)S(1)} %get-tuple-element.31.back_ref, ...), custom_call_target="tpu_custom_call" | custom-call | tf_op jit(solution)/shard_map/pallas_call | solution.py:271
  10.5 0.0 collective-permute-done.prev_ref
  10.5 3.7 %collective-permute-done.1.next_ref = bf16[192,256]{1,0:T(8,128)(2,1)S(1)} collective-permute-done((bf16[192,256]{1,0:T(8,128)(2,1)S(1)}, bf16[192,256]{1,0:T(8,128)(2,1)S(1)}, u32[]{:S(2)}, u32[]{:S(2)}) %collective-permute-start.1) | collective-permute-done | bytes 98336 | tf_op jit(solution)/shard_map/ppermute | solution.py:302
  14.2 1.8 %shard_map.95 = (bf16[4,416,256]{2,1,0:T(8,128)(2,1)S(1)}, bf16[4,416,256]{2,1,0:T(8,128)(2,1)S(1)}, bf16[128,256]{1,0:T(8,128)(2,1)S(1)}, bf16[256,256]{1,0:T(8,128)(2,1)S(1)}) custom-call(s32[5,1,64]{2,1,0:T(1,128)S(1)} %get-tuple-element.29.halt_ref, bf16[320,256]{1,0:T(8,128)(2,1)S(1)} %get-tuple-element.30.hidden_ref, ...), custom_call_target="tpu_custom_call" | custom-call | tf_op jit(solution)/shard_map/pallas_call | solution.py:271
  16.0 1.9 %collective-permute-start.2 = (bf16[4,416,256]{2,1,0:T(8,128)(2,1)S(1)}, bf16[4,416,256]{2,1,0:T(8,128)(2,1)S(1)}, u32[]{:S(2)}, u32[]{:S(2)}) collective-permute-start(bf16[4,416,256]{2,1,0:T(8,128)(2,1)S(1)} %get-tuple-element.46), channel_id=1, source_target_pairs={{0,8},{8,0},{1,9},{9,1},{2,10},{10,2},{3,11},{11,3},{4,12},{12,4},... | collective-permute-start | bytes 2555912 | tf_op jit(solution)/shard_map/ppermute | solution.py:322
  17.9 2.1 %shard_map.96 = (bf16[320,1024]{1,0:T(8,128)(2,1)}, bf16[320,1024]{1,0:T(8,128)(2,1)}, f32[8,128]{1,0:T(8,128)S(1)}) custom-call(bf16[320,1024]{1,0:T(8,128)(2,1)S(1)} %get-tuple-element.27.feat_ref, bf16[320,1024]{1,0:T(8,128)(2,1)S(1)} %get-tuple-element.28.grad_ref, bf16[192,256]{1,0:T(8,128)(2,1)S(1)} %get-tuple-element.32.two_in_ref, ...), custom_call_target="tpu_custom_call" | custom-call | tf_op jit(solution)/shard_map/pallas_call | solution.py:271
  20.1 0.2 collective-permute-done.2.got_ref
  20.3 0.2 shard_map.97
  20.5 12.6 %all_to_all.15.got_ref = bf16[4,416,256]{2,1,0:T(8,128)(2,1)S(1)} all-to-all(bf16[4,416,256]{2,1,0:T(8,128)(2,1)S(1)} %shard_map.97), channel_id=1, replica_groups={{0,16,128,144},{32,48,160,176},{64,80,192,208},{96,112,224,240},{256,27..., dimensions={0} | all-to-all | bytes 1703936 | tf_op jit(solution)/shard_map/all_to_all | solution.py:330
  33.1 0.1 shard_map.98
  33.3 22.0 %all_to_all.16.got_ref = bf16[16,4,1664]{2,1,0:T(4,128)(2,1)S(1)} all-to-all(bf16[16,4,1664]{2,1,0:T(4,128)(2,1)S(1)} %shard_map.98), channel_id=1, replica_groups={{0,1,32,33,64,65,96,97,256,257,288,289,320,321,352,353},{2,3,34,35,66,6..., dimensions={0} | all-to-all | bytes 425984 | tf_op jit(solution)/shard_map/all_to_all | solution.py:335
  55.3 16.7 %all_to_all.17.got_ref = bf16[8,4,1664]{2,1,0:T(4,128)(2,1)S(1)} all-to-all(bf16[8,4,1664]{2,1,0:T(4,128)(2,1)S(1)} %shard_map.99), channel_id=1, replica_groups=mesh['x_hi'=2,'x_lo'=2,'y_hi'=4,'y_lo'=2,'core'=2,'rows'=8] {'rows'}, dimensions={0} | all-to-all | bytes 212992 | tf_op jit(solution)/shard_map/all_to_all | solution.py:337
  72.1 0.6 shard_map.100
  (1 shorter events, 0.0 us)
Async XLA Ops:
  0.6 8.0 %copy-start = (bf16[256,2304]{1,0:T(8,128)(2,1)S(1)}, bf16[256,2304]{1,0:T(8,128)(2,1)}, u32[]{:S(2)}) copy-start(bf16[256,2304]{1,0:T(8,128)(2,1)} %conv_ref.5) | copy-start | bytes 3538948
  3.1 7.4 %collective-permute-start = (bf16[192,256]{1,0:T(8,128)(2,1)S(1)}, bf16[192,256]{1,0:T(8,128)(2,1)S(1)}, u32[]{:S(2)}, u32[]{:S(2)}) collective-permute-start(bf16[192,256]{1,0:T(8,128)(2,1)S(1)} %get-tuple-element.33), channel_id=1, source_target_pairs={{0,1},{1,2},{2,3},{3,4},{4,5},{5,6},{6,7},{8,9},{9,10},{10,11},{11... | collective-permute-start | bytes 294920 | tf_op jit(solution)/shard_map/ppermute | solution.py:301
  7.3 6.9 %collective-permute-start.1 = (bf16[192,256]{1,0:T(8,128)(2,1)S(1)}, bf16[192,256]{1,0:T(8,128)(2,1)S(1)}, u32[]{:S(2)}, u32[]{:S(2)}) collective-permute-start(bf16[192,256]{1,0:T(8,128)(2,1)S(1)} %get-tuple-element.34), channel_id=1, source_target_pairs={{1,0},{2,1},{3,2},{4,3},{5,4},{6,5},{7,6},{9,8},{10,9},{11,10},{12... | collective-permute-start | bytes 294920 | tf_op jit(solution)/shard_map/ppermute | solution.py:302
  16.0 4.3 %collective-permute-start.2 = (bf16[4,416,256]{2,1,0:T(8,128)(2,1)S(1)}, bf16[4,416,256]{2,1,0:T(8,128)(2,1)S(1)}, u32[]{:S(2)}, u32[]{:S(2)}) collective-permute-start(bf16[4,416,256]{2,1,0:T(8,128)(2,1)S(1)} %get-tuple-element.46), channel_id=1, source_target_pairs={{0,8},{8,0},{1,9},{9,1},{2,10},{10,2},{3,11},{11,3},{4,12},{12,4},... | collective-permute-start | bytes 2555912 | tf_op jit(solution)/shard_map/ppermute | solution.py:322

commit v7 on v6

--- a/solution.py
+++ b/solution.py
@@ -23,31 +23,33 @@
     return (x * NY + y) * NC + core
 
 
-def squares():
-    def member(block, parity, size, core):
-        return (2 * block + parity) % size if core == 0 or parity == 1 else (2 * block + 2) % size
-
-    return [
-        [dp_of(member(bx, i, NX, core), member(by, j, NY, core), core) for i in (0, 1) for j in (0, 1)]
-        for core in range(NC)
-        for bx in range(HX)
-        for by in range(HY)
-    ]
-
-
-def rest():
-    return [
-        [
-            dp_of(2 * x_hi + x, 2 * y_hi + y, core) * NZ + 2 * z + low
-            for x_hi in range(HX)
-            for y_hi in range(HY)
-            for low in range(2)
-        ]
-        for x in range(2)
-        for y in range(2)
-        for core in range(NC)
-        for z in range(HZ)
-    ]
+def near_groups():
+    along_x = [
+        [dp_of(x, y, 0) * NZ + z for x in range(NX)]
+        for y in range(NY)
+        for z in range(NZ)
+    ]
+    squares = [
+        [dp_of(x, 2 * y_hi + i, 1) * NZ + 2 * z_hi + k for i in (0, 1) for k in (0, 1)]
+        for x in range(NX)
+        for y_hi in range(HY)
+        for z_hi in range(HZ)
+    ]
+    return along_x + squares
+
+
+def far_groups():
+    columns = [
+        [dp_of(x, y, 0) * NZ + 2 * z_hi + k for y in range(NY) for k in (0, 1)]
+        for x in range(NX)
+        for z_hi in range(HZ)
+    ]
+    planes = [
+        [dp_of(x, 2 * y_hi + i, 1) * NZ + z for x in range(NX) for y_hi in range(HY)]
+        for i in (0, 1)
+        for z in range(NZ)
+    ]
+    return columns + planes
 
 
 def dot(left, right, left_dim, right_dim):
@@ -104,10 +106,11 @@
     down_ref[0 : 2 * cols, :] = hidden[(rows - 2) * cols :]
     for copy in copies[2:]:
         copy.wait()
-    back = (active_column(halt_ref, range(rows)) * dot(grad_ref[...], expand_ref[...], 1, 0)).astype(BF)
+    edges = jnp.concatenate([grad_ref[0:cols, :], grad_ref[(rows - 1) * cols :, :]], axis=0)
+    back = (active_column(halt_ref, (0, rows - 1)) * dot(edges, expand_ref[...], 1, 0)).astype(BF)
     back_ref[...] = back
     up_ref[2 * cols :, :] = back[0:cols]
-    down_ref[2 * cols :, :] = back[(rows - 1) * cols :]
+    down_ref[2 * cols :, :] = back[cols:]
 
 
 def fill_columns(columns_ref, first, cells, cols):
@@ -122,22 +125,24 @@
 
 def sorting(width):
     at = lax.broadcasted_iota(jnp.int32, (width, 1), 0)
-    j, y_hi, x_hi = at & 3, (at >> 2) & (HY - 1), (at >> 4) & (HX - 1)
-    y_lo, x_lo, c = (at >> 5) & 1, (at >> 6) & 1, at >> 7
-    wanted = dp_of(2 * x_hi + x_lo, 2 * y_hi + y_lo, c ^ lax.axis_index("core")) * 4 + j
+    j, place, c = at & 3, (at >> 2) & (NX * NY - 1), at >> 7
+    x, y = place >> 3, place & (NY - 1)
+    other_x, other_y = (place >> 2) & (NX - 1), 2 * (place & (HY - 1)) + (place >> 4)
+    wanted = jnp.where(c == 0, dp_of(x, y, 0), dp_of(other_x, other_y, 1)) * 4 + j
     channel = lax.broadcasted_iota(jnp.int32, (width, width), 1)
     return (channel == wanted).astype(F32).astype(BF)
 
 
 def inner_kernel(
-    halt_ref, hidden_ref, back_ref, grad_ref, conv_ref,
+    halt_ref, hidden_ref, grad_ref, expand_ref, conv_ref,
     cpart_ref, epart_ref, two_ref, gtwo_ref, columns_ref,
 ):
     rows, _, cols = halt_ref.shape
     inner = slice(cols, (rows - 1) * cols)
     fill_columns(columns_ref, 0, hidden_ref[...], cols)
     pre_two = dot(columns_ref[...], conv_ref[...], 1, 1)
-    grad_two = jnp.where(pre_two > 0, back_ref[inner, :].astype(F32), 0.0).astype(BF)
+    back = active_column(halt_ref, range(1, rows - 1)) * dot(grad_ref[inner, :], expand_ref[...], 1, 0)
+    grad_two = jnp.where(pre_two > 0, back, 0.0).astype(BF)
     gtwo_ref[...] = grad_two
     hidden_two = (active_column(halt_ref, range(1, rows - 1)) * jnp.maximum(pre_two, 0.0)).astype(BF)
     two_ref[...] = hidden_two
@@ -160,7 +165,7 @@
     fill_columns(columns_ref, 0, above, cols)
     fill_columns(columns_ref, halo, below, cols)
     pre_two = dot(columns_ref[...], conv_ref[...], 1, 1)
-    back = jnp.concatenate([prev_ref[halo:], back_ref[top, :], back_ref[end, :], next_ref[halo:]], axis=0)
+    back = jnp.concatenate([prev_ref[halo:], back_ref[...], next_ref[halo:]], axis=0)
     grad_two = jnp.where(pre_two > 0, back.astype(F32), 0.0).astype(BF)
     gtwo_ref[...] = grad_two
     active = active_column(halt_ref, (0, rows - 1))
@@ -170,26 +175,33 @@
 
     grad_rows = dot(sorting(width), grad_two[own], 1, 1).astype(BF)
     conv_part = (cpart_ref[...] + dot(grad_rows, columns_ref[own, :], 1, 0)).astype(BF)
-    tall = width // 8
-    taps = conv_part.shape[1] // width
-    for place in range(4):
-        other = 4 + place
-        for tap in range(taps):
-            to, at = slice(tap * tall, (tap + 1) * tall), slice(tap * width, (tap + 1) * width)
-            keep_ref[place, to, :] = conv_part[place * tall : (place + 1) * tall, at]
-            send_ref[place, to, :] = conv_part[other * tall : (other + 1) * tall, at]
     upstream = jnp.concatenate([grad_ref[top, :], grad_ref[end, :]], axis=0)
     expand_part = (epart_ref[...] + dot(upstream, hidden_two, 0, 0)).astype(BF)
+
+    def write(group, rows, low, zero, one):
+        at = slice(low * half, (low + 1) * half)
+        keep_ref[group, rows, at] = jnp.where(core == 0, zero, one)
+        send_ref[group, rows, at] = jnp.where(core == 0, one, zero)
+
+    tall, taps, half = width // 8, conv_part.shape[1] // width, width // 2
     per_dp = expand_part.shape[0] // (NX * NY * NC)
-    for x in range(NX):
-        for y in range(NY):
-            first = dp_of(x, y, 0) * per_dp
-            zero, one = (expand_part[first + i * per_dp : first + (i + 1) * per_dp] for i in (0, 1))
-            mine, theirs = jnp.where(core == 0, zero, one), jnp.where(core == 0, one, zero)
-            start = taps * tall + (x // 2 * HY + y // 2) * per_dp
-            place = x % 2 * 2 + y % 2
-            keep_ref[place, start : start + per_dp, :] = mine
-            send_ref[place, start : start + per_dp, :] = theirs
+    for group in range(4):
+        y_lo, part = group // 2, group % 2
+        for low in range(2):
+            zero = conv_part[group * tall : (group + 1) * tall]
+            first = (4 + 2 * y_lo + low) * tall
+            one = conv_part[first : first + tall]
+            for tap in range(taps):
+                lanes = tap * width + low * half, tap * width + part * half
+                rows = slice(tap * tall, (tap + 1) * tall)
+                write(group, rows, low, zero[:, lanes[0] : lanes[0] + half], one[:, lanes[1] : lanes[1] + half])
+            for shard in range(NY):
+                first = dp_of(group, shard, 0) * per_dp
+                zero_part = expand_part[first : first + per_dp, low * half : (low + 1) * half]
+                first = dp_of(2 * low + shard // HY, 2 * (shard % HY) + y_lo, 1) * per_dp
+                one_part = expand_part[first : first + per_dp, part * half : (part + 1) * half]
+                start = taps * tall + shard * per_dp
+                write(group, slice(start, start + per_dp), low, zero_part, one_part)
 
 
 def leave_kernel(
@@ -225,20 +237,22 @@
     out_ref[...] = (keep_ref[...].astype(F32) + got_ref[...].astype(F32)).astype(BF)
 
 
-def square_kernel(got_ref, out_ref, *, taps):
+def near_kernel(got_ref, out_ref, *, taps):
     total = sum_of(got_ref).astype(BF)
+    core = lax.axis_index("core")
     parts, count, lanes = out_ref.shape
     half = total.shape[1] // 2
     shards, blocks = parts // 2, lanes // half
     for shard in range(shards):
-        for i in range(blocks):
-            if i < taps:
-                first = (i * shards + shard) * count
-            else:
-                first = (taps * shards + shard * (blocks - taps) + i - taps) * count
-            for low in range(2):
+        for low in range(2):
+            to = jnp.where(core == 0, 2 * shard + low, shards * low + shard)
+            for i in range(blocks):
+                if i < taps:
+                    first = (i * shards + shard) * count
+                else:
+                    first = (taps * shards + shard * (blocks - taps) + i - taps) * count
                 block = total[first : first + count, low * half : (low + 1) * half]
-                out_ref[2 * shard + low, :, i * half : (i + 1) * half] = block
+                out_ref[to, :, i * half : (i + 1) * half] = block
 
 
 def plane_kernel(got_ref, out_ref):
@@ -292,7 +306,8 @@
     halting, flat_in, upstream, reduce_in, expand_in, hidden, sign, back, up, down = pl.pallas_call(
         enter_kernel,
         out_shape=[pltpu.VMEM(a.shape, a.dtype) for a in inputs]
-        + [pltpu.VMEM((own, width), BF)] * 3
+        + [pltpu.VMEM((own, width), BF)] * 2
+        + [pltpu.VMEM((2 * cols, width), BF)]
         + [pltpu.VMEM((3 * cols, width), BF)] * 2,
         in_specs=[pl.BlockSpec(memory_space=pl.ANY)] * len(inputs),
         scratch_shapes=[pltpu.SemaphoreType.DMA((len(inputs),))],
@@ -309,7 +324,7 @@
     conv_part, expand_part, two_in, gtwo_in = call(
         inner_kernel,
         [pltpu.VMEM((width, taps), F32), pltpu.VMEM((chans, width), F32), pltpu.VMEM(inner, BF), pltpu.VMEM(inner, BF)],
-        halting, hidden, back, upstream, weight_conv,
+        halting, hidden, upstream, expand_in, weight_conv,
         scratch=[pltpu.VMEM((inner[0], taps), BF)],
     )
     keep, send, two, gtwo = call(
@@ -327,12 +342,12 @@
         scratch=[pltpu.VMEM((own, taps), BF), pltpu.VMEM((taps, width), BF)],
     )
     (total,) = call(core_kernel, [pltpu.VMEM(part, BF)], keep, got, done)
-    got = lax.all_to_all(total, DP, 0, 0, axis_index_groups=squares(), tiled=True)
+    got = lax.all_to_all(total, AXES, 0, 0, axis_index_groups=near_groups(), tiled=True)
     shard = (conv_rows, shard_rows // conv_rows * width // 2)
     (total,) = call(
-        functools.partial(square_kernel, taps=taps // width), [pltpu.VMEM((2 * HX * HY,) + shard, BF)], got
-    )
-    got = lax.all_to_all(total, AXES, 0, 0, axis_index_groups=rest(), tiled=True)
+        functools.partial(near_kernel, taps=taps // width), [pltpu.VMEM((2 * HX * HY,) + shard, BF)], got
+    )
+    got = lax.all_to_all(total, AXES, 0, 0, axis_index_groups=far_groups(), tiled=True)
     (total,) = call(plane_kernel, [pltpu.VMEM((NZ,) + shard, BF)], got)
     got = lax.all_to_all(total, "rows", 0, 0, tiled=True)
     grad_conv, grad_expand = call(

time: 73 us -> 71.2 us (0.975)
  blocking collectives: 51.4 us -> 49.6 us
    all_to_all x2, blocking collectives: 34.7 us -> 32 us  [the longest x1 18 us: local(): lax.all_to_all(total, AXES, 0, 0, axis_index_groups=far_groups(), tiled=T...]
    all_to_all x1, blocking collectives: 16.7 us -> 17.7 us  [local(): got = lax.all_to_all(total, 'rows', 0, 0, tiled=True)]
where the time goes in v7:
time: 71.2 us; the launch traced here: 70.7 us
  blocking collectives  49.6 us (70%)
  Pallas kernels  8.8 us (12%)
  starting transfers between devices  7.49 us (11%)
  waiting for transfers between devices  4.03 us (6%)
    all_to_all x1, blocking collectives, local(): lax.all_to_all(total, AXES, 0, 0, axis_index_groups=far_groups(), tiled=T...  18 us
    all_to_all x1, blocking collectives, local(): got = lax.all_to_all(total, 'rows', 0, 0, tiled=True)  17.7 us
    all_to_all x1, blocking collectives, local(): lax.all_to_all(total, AXES, 0, 0, axis_index_groups=near_groups(), tiled=...  13.9 us
    pallas_call x7, Pallas kernels, call(): pl.pallas_call(kernel, out_shape=outs, scratch_shapes=list(scratch), comp...  6.68 us
    ppermute x1, starting transfers between devices, local(): from_prev = lax.ppermute(down, 'rows', [(i, i + 1) for i in range(NZ - 1)])  4.28 us
    ppermute x1, waiting for transfers between devices, local(): from_next = lax.ppermute(up, 'rows', [(i + 1, i) for i in range(NZ - 1)])  3.82 us
    pallas_call x1, Pallas kernels, local(): pl.pallas_call(enter_kernel, out_shape=[pltpu.VMEM(a.shape, a.dtype) for...  2.12 us
    ppermute x1, starting transfers between devices, local(): got = lax.ppermute(send, 'core', [(0, 1), (1, 0)])  1.92 us
  transfers between devices with their start and end apart: 3, of which 2 were waited for; matrix products, arithmetic and copies ran while one was open for 0% of the time, Pallas kernels for 5%

profile of v7, /device:TPU:8, one launch (start us, length us, event | category | flops | bytes accessed | tf_op | source)
XLA Modules:
  0.0 70.7 jit_solution(135789495832392994)
XLA Ops:
  0.6 0.0 copy-start
  0.6 2.1 %shard_map.93 = (s32[5,1,64]{2,1,0:T(1,128)S(1)}, bf16[320,1024]{1,0:T(8,128)(2,1)S(1)}, bf16[320,1024]{1,0:T(8,128)(2,1)S(1)}, bf16[256,1024]{1,0:T(8,128)(2,1)...) custom-call(s32[5,1,64]{2,1,0:T(1,128)} %bitcast.7, ...), custom_call_target="tpu_custom_call" | custom-call | tf_op jit(solution)/shard_map/pallas_call | solution.py:306
  2.8 4.3 %collective-permute-start = (bf16[192,256]{1,0:T(8,128)(2,1)S(1)}, bf16[192,256]{1,0:T(8,128)(2,1)S(1)}, u32[]{:S(2)}, u32[]{:S(2)}) collective-permute-start(bf16[192,256]{1,0:T(8,128)(2,1)S(1)} %get-tuple-element.34), channel_id=1, source_target_pairs={{0,1},{1,2},{2,3},{3,4},{4,5},{5,6},{6,7},{8,9},{9,10},{10,11},{11... | collective-permute-start | bytes 294920 | tf_op jit(solution)/shard_map/ppermute | solution.py:316
  7.1 1.3 %collective-permute-start.1 = (bf16[192,256]{1,0:T(8,128)(2,1)S(1)}, bf16[192,256]{1,0:T(8,128)(2,1)S(1)}, u32[]{:S(2)}, u32[]{:S(2)}) collective-permute-start(bf16[192,256]{1,0:T(8,128)(2,1)S(1)} %get-tuple-element.35), channel_id=1, source_target_pairs={{1,0},{2,1},{3,2},{4,3},{5,4},{6,5},{7,6},{9,8},{10,9},{11,10},{12... | collective-permute-start | bytes 294920 | tf_op jit(solution)/shard_map/ppermute | solution.py:317
  8.4 0.0 copy-done
  8.4 1.7 %shard_map.94 = (f32[256,2304]{1,0:T(8,128)S(1)}, f32[1024,256]{1,0:T(8,128)S(1)}, bf16[192,256]{1,0:T(8,128)(2,1)S(1)}, bf16[192,256]{1,0:T(8,128)(2,1)S(1)}) custom-call(s32[5,1,64]{2,1,0:T(1,128)S(1)} %get-tuple-element.29.halt_ref, bf16[320,256]{1,0:T(8,128)(2,1)S(1)} %get-tuple-element.30.hidden_ref, bf16[320,1024]{1,0:T(8,128)(2,1)S(1)} %get-tuple-element.28.grad_ref, ...), custom_call_target="tpu_custom_call" | custom-call | tf_op jit(solution)/shard_map/pallas_call | solution.py:285
  10.1 0.0 collective-permute-done.prev_ref
  10.1 3.8 %collective-permute-done.1.next_ref = bf16[192,256]{1,0:T(8,128)(2,1)S(1)} collective-permute-done((bf16[192,256]{1,0:T(8,128)(2,1)S(1)}, bf16[192,256]{1,0:T(8,128)(2,1)S(1)}, u32[]{:S(2)}, u32[]{:S(2)}) %collective-permute-start.1) | collective-permute-done | bytes 98336 | tf_op jit(solution)/shard_map/ppermute | solution.py:317
  13.9 1.8 %shard_map.95 = (bf16[4,416,256]{2,1,0:T(8,128)(2,1)S(1)}, bf16[4,416,256]{2,1,0:T(8,128)(2,1)S(1)}, bf16[128,256]{1,0:T(8,128)(2,1)S(1)}, bf16[256,256]{1,0:T(8,128)(2,1)S(1)}) custom-call(s32[5,1,64]{2,1,0:T(1,128)S(1)} %get-tuple-element.29.halt_ref, bf16[320,256]{1,0:T(8,128)(2,1)S(1)} %get-tuple-element.30.hidden_ref, ...), custom_call_target="tpu_custom_call" | custom-call | tf_op jit(solution)/shard_map/pallas_call | solution.py:285
  15.7 1.9 %collective-permute-start.2 = (bf16[4,416,256]{2,1,0:T(8,128)(2,1)S(1)}, bf16[4,416,256]{2,1,0:T(8,128)(2,1)S(1)}, u32[]{:S(2)}, u32[]{:S(2)}) collective-permute-start(bf16[4,416,256]{2,1,0:T(8,128)(2,1)S(1)} %get-tuple-element.46), channel_id=1, source_target_pairs={{0,8},{8,0},{1,9},{9,1},{2,10},{10,2},{3,11},{11,3},{4,12},{12,4},... | collective-permute-start | bytes 2555912 | tf_op jit(solution)/shard_map/ppermute | solution.py:337
  17.7 2.1 %shard_map.96 = (bf16[320,1024]{1,0:T(8,128)(2,1)}, bf16[320,1024]{1,0:T(8,128)(2,1)}, f32[8,128]{1,0:T(8,128)S(1)}) custom-call(bf16[320,1024]{1,0:T(8,128)(2,1)S(1)} %get-tuple-element.27.feat_ref, bf16[320,1024]{1,0:T(8,128)(2,1)S(1)} %get-tuple-element.28.grad_ref, bf16[192,256]{1,0:T(8,128)(2,1)S(1)} %get-tuple-element.32.two_in_ref, ...), custom_call_target="tpu_custom_call" | custom-call | tf_op jit(solution)/shard_map/pallas_call | solution.py:285
  19.8 0.2 collective-permute-done.2.got_ref
  20.0 0.2 shard_map.97
  20.2 13.9 %all_to_all.15.got_ref = bf16[4,416,256]{2,1,0:T(8,128)(2,1)S(1)} all-to-all(bf16[4,416,256]{2,1,0:T(8,128)(2,1)S(1)} %shard_map.97), channel_id=1, replica_groups={{0,128,256,384},{1,129,257,385},{2,130,258,386},{3,131,259,387},{4,132,..., dimensions={0} | all-to-all | bytes 1703936 | tf_op jit(solution)/shard_map/all_to_all | solution.py:345
  34.1 0.2 shard_map.98
  34.3 18.0 %all_to_all.16.got_ref = bf16[16,4,1664]{2,1,0:T(4,128)(2,1)S(1)} all-to-all(bf16[16,4,1664]{2,1,0:T(4,128)(2,1)S(1)} %shard_map.98), channel_id=1, replica_groups={{0,1,16,17,32,33,48,49,64,65,80,81,96,97,112,113},{2,3,18,19,34,35,50,5..., dimensions={0} | all-to-all | bytes 425984 | tf_op jit(solution)/shard_map/all_to_all | solution.py:350
  52.4 17.7 %all_to_all.17.got_ref = bf16[8,4,1664]{2,1,0:T(4,128)(2,1)S(1)} all-to-all(bf16[8,4,1664]{2,1,0:T(4,128)(2,1)S(1)} %shard_map.99), channel_id=1, replica_groups=mesh['x_hi'=2,'x_lo'=2,'y_hi'=4,'y_lo'=2,'core'=2,'rows'=8] {'rows'}, dimensions={0} | all-to-all | bytes 212992 | tf_op jit(solution)/shard_map/all_to_all | solution.py:352
  70.0 0.6 shard_map.100
  (1 shorter events, 0.0 us)
Async XLA Ops:
  0.6 7.7 %copy-start = (bf16[256,2304]{1,0:T(8,128)(2,1)S(1)}, bf16[256,2304]{1,0:T(8,128)(2,1)}, u32[]{:S(2)}) copy-start(bf16[256,2304]{1,0:T(8,128)(2,1)} %conv_ref.5) | copy-start | bytes 3538948
  2.8 7.3 %collective-permute-start = (bf16[192,256]{1,0:T(8,128)(2,1)S(1)}, bf16[192,256]{1,0:T(8,128)(2,1)S(1)}, u32[]{:S(2)}, u32[]{:S(2)}) collective-permute-start(bf16[192,256]{1,0:T(8,128)(2,1)S(1)} %get-tuple-element.34), channel_id=1, source_target_pairs={{0,1},{1,2},{2,3},{3,4},{4,5},{5,6},{6,7},{8,9},{9,10},{10,11},{11... | collective-permute-start | bytes 294920 | tf_op jit(solution)/shard_map/ppermute | solution.py:316
  7.1 6.9 %collective-permute-start.1 = (bf16[192,256]{1,0:T(8,128)(2,1)S(1)}, bf16[192,256]{1,0:T(8,128)(2,1)S(1)}, u32[]{:S(2)}, u32[]{:S(2)}) collective-permute-start(bf16[192,256]{1,0:T(8,128)(2,1)S(1)} %get-tuple-element.35), channel_id=1, source_target_pairs={{1,0},{2,1},{3,2},{4,3},{5,4},{6,5},{7,6},{9,8},{10,9},{11,10},{12... | collective-permute-start | bytes 294920 | tf_op jit(solution)/shard_map/ppermute | solution.py:317
  15.7 4.3 %collective-permute-start.2 = (bf16[4,416,256]{2,1,0:T(8,128)(2,1)S(1)}, bf16[4,416,256]{2,1,0:T(8,128)(2,1)S(1)}, u32[]{:S(2)}, u32[]{:S(2)}) collective-permute-start(bf16[4,416,256]{2,1,0:T(8,128)(2,1)S(1)} %get-tuple-element.46), channel_id=1, source_target_pairs={{0,8},{8,0},{1,9},{9,1},{2,10},{10,2},{3,11},{11,3},{4,12},{12,4},... | collective-permute-start | bytes 2555912 | tf_op jit(solution)/shard_map/ppermute | solution.py:337

commit v8 on v7

--- a/solution.py
+++ b/solution.py
@@ -25,12 +25,12 @@
 
 def near_groups():
     along_x = [
-        [dp_of(x, y, 0) * NZ + z for x in range(NX)]
+        [dp_of(x, y, 1) * NZ + z for x in range(NX)]
         for y in range(NY)
         for z in range(NZ)
     ]
     squares = [
-        [dp_of(x, 2 * y_hi + i, 1) * NZ + 2 * z_hi + k for i in (0, 1) for k in (0, 1)]
+        [dp_of(x, 2 * y_hi + i, 0) * NZ + 2 * z_hi + k for i in (0, 1) for k in (0, 1)]
         for x in range(NX)
         for y_hi in range(HY)
         for z_hi in range(HZ)
@@ -40,12 +40,12 @@
 
 def far_groups():
     columns = [
-        [dp_of(x, y, 0) * NZ + 2 * z_hi + k for y in range(NY) for k in (0, 1)]
+        [dp_of(x, y, 1) * NZ + 2 * z_hi + k for y in range(NY) for k in (0, 1)]
         for x in range(NX)
         for z_hi in range(HZ)
     ]
     planes = [
-        [dp_of(x, 2 * y_hi + i, 1) * NZ + z for x in range(NX) for y_hi in range(HY)]
+        [dp_of(x, 2 * y_hi + i, 0) * NZ + z for x in range(NX) for y_hi in range(HY)]
         for i in (0, 1)
         for z in range(NZ)
     ]
@@ -128,7 +128,7 @@
     j, place, c = at & 3, (at >> 2) & (NX * NY - 1), at >> 7
     x, y = place >> 3, place & (NY - 1)
     other_x, other_y = (place >> 2) & (NX - 1), 2 * (place & (HY - 1)) + (place >> 4)
-    wanted = jnp.where(c == 0, dp_of(x, y, 0), dp_of(other_x, other_y, 1)) * 4 + j
+    wanted = jnp.where(c == 1, dp_of(x, y, 1), dp_of(other_x, other_y, 0)) * 4 + j
     channel = lax.broadcasted_iota(jnp.int32, (width, width), 1)
     return (channel == wanted).astype(F32).astype(BF)
 
@@ -178,30 +178,30 @@
     upstream = jnp.concatenate([grad_ref[top, :], grad_ref[end, :]], axis=0)
     expand_part = (epart_ref[...] + dot(upstream, hidden_two, 0, 0)).astype(BF)
 
-    def write(group, rows, low, zero, one):
+    def write(group, rows, low, along, square):
         at = slice(low * half, (low + 1) * half)
-        keep_ref[group, rows, at] = jnp.where(core == 0, zero, one)
-        send_ref[group, rows, at] = jnp.where(core == 0, one, zero)
+        keep_ref[group, rows, at] = jnp.where(core == 1, along, square)
+        send_ref[group, rows, at] = jnp.where(core == 1, square, along)
 
     tall, taps, half = width // 8, conv_part.shape[1] // width, width // 2
     per_dp = expand_part.shape[0] // (NX * NY * NC)
     for group in range(4):
         y_lo, part = group // 2, group % 2
         for low in range(2):
-            zero = conv_part[group * tall : (group + 1) * tall]
-            first = (4 + 2 * y_lo + low) * tall
-            one = conv_part[first : first + tall]
+            along = conv_part[(4 + group) * tall : (5 + group) * tall]
+            first = (2 * y_lo + low) * tall
+            square = conv_part[first : first + tall]
             for tap in range(taps):
                 lanes = tap * width + low * half, tap * width + part * half
                 rows = slice(tap * tall, (tap + 1) * tall)
-                write(group, rows, low, zero[:, lanes[0] : lanes[0] + half], one[:, lanes[1] : lanes[1] + half])
+                write(group, rows, low, along[:, lanes[0] : lanes[0] + half], square[:, lanes[1] : lanes[1] + half])
             for shard in range(NY):
-                first = dp_of(group, shard, 0) * per_dp
-                zero_part = expand_part[first : first + per_dp, low * half : (low + 1) * half]
-                first = dp_of(2 * low + shard // HY, 2 * (shard % HY) + y_lo, 1) * per_dp
-                one_part = expand_part[first : first + per_dp, part * half : (part + 1) * half]
+                first = dp_of(group, shard, 1) * per_dp
+                along_part = expand_part[first : first + per_dp, low * half : (low + 1) * half]
+                first = dp_of(2 * low + shard // HY, 2 * (shard % HY) + y_lo, 0) * per_dp
+                square_part = expand_part[first : first + per_dp, part * half : (part + 1) * half]
                 start = taps * tall + shard * per_dp
-                write(group, slice(start, start + per_dp), low, zero_part, one_part)
+                write(group, slice(start, start + per_dp), low, along_part, square_part)
 
 
 def leave_kernel(
@@ -238,21 +238,21 @@
 
 
 def near_kernel(got_ref, out_ref, *, taps):
-    total = sum_of(got_ref).astype(BF)
+    total = sum_of(got_ref)
     core = lax.axis_index("core")
     parts, count, lanes = out_ref.shape
     half = total.shape[1] // 2
     shards, blocks = parts // 2, lanes // half
     for shard in range(shards):
         for low in range(2):
-            to = jnp.where(core == 0, 2 * shard + low, shards * low + shard)
+            to = jnp.where(core == 1, 2 * shard + low, shards * low + shard)
             for i in range(blocks):
                 if i < taps:
                     first = (i * shards + shard) * count
                 else:
                     first = (taps * shards + shard * (blocks - taps) + i - taps) * count
                 block = total[first : first + count, low * half : (low + 1) * half]
-                out_ref[to, :, i * half : (i + 1) * half] = block
+                out_ref[to, :, i * half : (i + 1) * half] = block.astype(BF)
 
 
 def plane_kernel(got_ref, out_ref):

time: 71.2 us -> 71 us (level)
    all_to_all x1, blocking collectives: 18 us -> 20.2 us  [local(): lax.all_to_all(total, AXES, 0, 0, axis_index_groups=far_groups(), tiled=T...]
    all_to_all x1, blocking collectives: 13.9 us -> 12.7 us  [local(): lax.all_to_all(total, AXES, 0, 0, axis_index_groups=near_groups(), tiled=...]
    all_to_all x1, blocking collectives: 17.7 us -> 16.7 us  [local(): got = lax.all_to_all(total, 'rows', 0, 0, tiled=True)]
where the time goes in v8:
time: 71 us; the launch traced here: 70.7 us
  blocking collectives  49.6 us (70%)
  Pallas kernels  8.8 us (12%)
  starting transfers between devices  7.49 us (11%)
  waiting for transfers between devices  4.04 us (6%)
  between operations  0.71 us (1%)
    all_to_all x1, blocking collectives, local(): lax.all_to_all(total, AXES, 0, 0, axis_index_groups=far_groups(), tiled=T...  20.2 us
    all_to_all x1, blocking collectives, local(): got = lax.all_to_all(total, 'rows', 0, 0, tiled=True)  16.7 us
    all_to_all x1, blocking collectives, local(): lax.all_to_all(total, AXES, 0, 0, axis_index_groups=near_groups(), tiled=...  12.7 us
    pallas_call x7, Pallas kernels, call(): pl.pallas_call(kernel, out_shape=outs, scratch_shapes=list(scratch), comp...  6.68 us
    ppermute x1, starting transfers between devices, local(): from_prev = lax.ppermute(down, 'rows', [(i, i + 1) for i in range(NZ - 1)])  4.28 us
    ppermute x1, waiting for transfers between devices, local(): from_next = lax.ppermute(up, 'rows', [(i + 1, i) for i in range(NZ - 1)])  3.83 us
    pallas_call x1, Pallas kernels, local(): pl.pallas_call(enter_kernel, out_shape=[pltpu.VMEM(a.shape, a.dtype) for...  2.12 us
    ppermute x1, starting transfers between devices, local(): got = lax.ppermute(send, 'core', [(0, 1), (1, 0)])  1.92 us
  transfers between devices with their start and end apart: 3, of which 2 were waited for; matrix products, arithmetic and copies ran while one was open for 0% of the time, Pallas kernels for 5%

profile of v8, /device:TPU:8, one launch (start us, length us, event | category | flops | bytes accessed | tf_op | source)
XLA Modules:
  0.0 70.7 jit_solution(14899679664446758793)
XLA Ops:
  0.6 0.0 copy-start
  0.6 2.1 %shard_map.93 = (s32[5,1,64]{2,1,0:T(1,128)S(1)}, bf16[320,1024]{1,0:T(8,128)(2,1)S(1)}, bf16[320,1024]{1,0:T(8,128)(2,1)S(1)}, bf16[256,1024]{1,0:T(8,128)(2,1)...) custom-call(s32[5,1,64]{2,1,0:T(1,128)} %bitcast.7, ...), custom_call_target="tpu_custom_call" | custom-call | tf_op jit(solution)/shard_map/pallas_call | solution.py:306
  2.8 4.3 %collective-permute-start = (bf16[192,256]{1,0:T(8,128)(2,1)S(1)}, bf16[192,256]{1,0:T(8,128)(2,1)S(1)}, u32[]{:S(2)}, u32[]{:S(2)}) collective-permute-start(bf16[192,256]{1,0:T(8,128)(2,1)S(1)} %get-tuple-element.34), channel_id=1, source_target_pairs={{0,1},{1,2},{2,3},{3,4},{4,5},{5,6},{6,7},{8,9},{9,10},{10,11},{11... | collective-permute-start | bytes 294920 | tf_op jit(solution)/shard_map/ppermute | solution.py:316
  7.1 1.3 %collective-permute-start.1 = (bf16[192,256]{1,0:T(8,128)(2,1)S(1)}, bf16[192,256]{1,0:T(8,128)(2,1)S(1)}, u32[]{:S(2)}, u32[]{:S(2)}) collective-permute-start(bf16[192,256]{1,0:T(8,128)(2,1)S(1)} %get-tuple-element.35), channel_id=1, source_target_pairs={{1,0},{2,1},{3,2},{4,3},{5,4},{6,5},{7,6},{9,8},{10,9},{11,10},{12... | collective-permute-start | bytes 294920 | tf_op jit(solution)/shard_map/ppermute | solution.py:317
  8.4 0.0 copy-done
  8.4 1.7 %shard_map.94 = (f32[256,2304]{1,0:T(8,128)S(1)}, f32[1024,256]{1,0:T(8,128)S(1)}, bf16[192,256]{1,0:T(8,128)(2,1)S(1)}, bf16[192,256]{1,0:T(8,128)(2,1)S(1)}) custom-call(s32[5,1,64]{2,1,0:T(1,128)S(1)} %get-tuple-element.29.halt_ref, bf16[320,256]{1,0:T(8,128)(2,1)S(1)} %get-tuple-element.30.hidden_ref, bf16[320,1024]{1,0:T(8,128)(2,1)S(1)} %get-tuple-element.28.grad_ref, ...), custom_call_target="tpu_custom_call" | custom-call | tf_op jit(solution)/shard_map/pallas_call | solution.py:285
  10.1 0.0 collective-permute-done.prev_ref
  10.1 3.8 %collective-permute-done.1.next_ref = bf16[192,256]{1,0:T(8,128)(2,1)S(1)} collective-permute-done((bf16[192,256]{1,0:T(8,128)(2,1)S(1)}, bf16[192,256]{1,0:T(8,128)(2,1)S(1)}, u32[]{:S(2)}, u32[]{:S(2)}) %collective-permute-start.1) | collective-permute-done | bytes 98336 | tf_op jit(solution)/shard_map/ppermute | solution.py:317
  13.9 1.8 %shard_map.95 = (bf16[4,416,256]{2,1,0:T(8,128)(2,1)S(1)}, bf16[4,416,256]{2,1,0:T(8,128)(2,1)S(1)}, bf16[128,256]{1,0:T(8,128)(2,1)S(1)}, bf16[256,256]{1,0:T(8,128)(2,1)S(1)}) custom-call(s32[5,1,64]{2,1,0:T(1,128)S(1)} %get-tuple-element.29.halt_ref, bf16[320,256]{1,0:T(8,128)(2,1)S(1)} %get-tuple-element.30.hidden_ref, ...), custom_call_target="tpu_custom_call" | custom-call | tf_op jit(solution)/shard_map/pallas_call | solution.py:285
  15.7 1.9 %collective-permute-start.2 = (bf16[4,416,256]{2,1,0:T(8,128)(2,1)S(1)}, bf16[4,416,256]{2,1,0:T(8,128)(2,1)S(1)}, u32[]{:S(2)}, u32[]{:S(2)}) collective-permute-start(bf16[4,416,256]{2,1,0:T(8,128)(2,1)S(1)} %get-tuple-element.46), channel_id=1, source_target_pairs={{0,8},{8,0},{1,9},{9,1},{2,10},{10,2},{3,11},{11,3},{4,12},{12,4},... | collective-permute-start | bytes 2555912 | tf_op jit(solution)/shard_map/ppermute | solution.py:337
  17.6 2.1 %shard_map.96 = (bf16[320,1024]{1,0:T(8,128)(2,1)}, bf16[320,1024]{1,0:T(8,128)(2,1)}, f32[8,128]{1,0:T(8,128)S(1)}) custom-call(bf16[320,1024]{1,0:T(8,128)(2,1)S(1)} %get-tuple-element.27.feat_ref, bf16[320,1024]{1,0:T(8,128)(2,1)S(1)} %get-tuple-element.28.grad_ref, bf16[192,256]{1,0:T(8,128)(2,1)S(1)} %get-tuple-element.32.two_in_ref, ...), custom_call_target="tpu_custom_call" | custom-call | tf_op jit(solution)/shard_map/pallas_call | solution.py:285
  19.8 0.2 collective-permute-done.2.got_ref
  20.0 0.2 shard_map.97
  20.2 12.7 %all_to_all.15.got_ref = bf16[4,416,256]{2,1,0:T(8,128)(2,1)S(1)} all-to-all(bf16[4,416,256]{2,1,0:T(8,128)(2,1)S(1)} %shard_map.97), channel_id=1, replica_groups={{8,136,264,392},{9,137,265,393},{10,138,266,394},{11,139,267,395},{12,1..., dimensions={0} | all-to-all | bytes 1703936 | tf_op jit(solution)/shard_map/all_to_all | solution.py:345
  32.9 0.2 shard_map.98
  33.0 20.2 %all_to_all.16.got_ref = bf16[16,4,1664]{2,1,0:T(4,128)(2,1)S(1)} all-to-all(bf16[16,4,1664]{2,1,0:T(4,128)(2,1)S(1)} %shard_map.98), channel_id=1, replica_groups={{8,9,24,25,40,41,56,57,72,73,88,89,104,105,120,121},{10,11,26,27,42,43,..., dimensions={0} | all-to-all | bytes 425984 | tf_op jit(solution)/shard_map/all_to_all | solution.py:350
  53.3 16.7 %all_to_all.17.got_ref = bf16[8,4,1664]{2,1,0:T(4,128)(2,1)S(1)} all-to-all(bf16[8,4,1664]{2,1,0:T(4,128)(2,1)S(1)} %shard_map.99), channel_id=1, replica_groups=mesh['x_hi'=2,'x_lo'=2,'y_hi'=4,'y_lo'=2,'core'=2,'rows'=8] {'rows'}, dimensions={0} | all-to-all | bytes 212992 | tf_op jit(solution)/shard_map/all_to_all | solution.py:352
  70.1 0.6 shard_map.100
  (1 shorter events, 0.0 us)
Async XLA Ops:
  0.6 7.7 %copy-start = (bf16[256,2304]{1,0:T(8,128)(2,1)S(1)}, bf16[256,2304]{1,0:T(8,128)(2,1)}, u32[]{:S(2)}) copy-start(bf16[256,2304]{1,0:T(8,128)(2,1)} %conv_ref.5) | copy-start | bytes 3538948
  2.8 7.3 %collective-permute-start = (bf16[192,256]{1,0:T(8,128)(2,1)S(1)}, bf16[192,256]{1,0:T(8,128)(2,1)S(1)}, u32[]{:S(2)}, u32[]{:S(2)}) collective-permute-start(bf16[192,256]{1,0:T(8,128)(2,1)S(1)} %get-tuple-element.34), channel_id=1, source_target_pairs={{0,1},{1,2},{2,3},{3,4},{4,5},{5,6},{6,7},{8,9},{9,10},{10,11},{11... | collective-permute-start | bytes 294920 | tf_op jit(solution)/shard_map/ppermute | solution.py:316
  7.1 6.9 %collective-permute-start.1 = (bf16[192,256]{1,0:T(8,128)(2,1)S(1)}, bf16[192,256]{1,0:T(8,128)(2,1)S(1)}, u32[]{:S(2)}, u32[]{:S(2)}) collective-permute-start(bf16[192,256]{1,0:T(8,128)(2,1)S(1)} %get-tuple-element.35), channel_id=1, source_target_pairs={{1,0},{2,1},{3,2},{4,3},{5,4},{6,5},{7,6},{9,8},{10,9},{11,10},{12... | collective-permute-start | bytes 294920 | tf_op jit(solution)/shard_map/ppermute | solution.py:317
  15.7 4.3 %collective-permute-start.2 = (bf16[4,416,256]{2,1,0:T(8,128)(2,1)S(1)}, bf16[4,416,256]{2,1,0:T(8,128)(2,1)S(1)}, u32[]{:S(2)}, u32[]{:S(2)}) collective-permute-start(bf16[4,416,256]{2,1,0:T(8,128)(2,1)S(1)} %get-tuple-element.46), channel_id=1, source_target_pairs={{0,8},{8,0},{1,9},{9,1},{2,10},{10,2},{3,11},{11,3},{4,12},{12,4},... | collective-permute-start | bytes 2555912 | tf_op jit(solution)/shard_map/ppermute | solution.py:337

commit v9 on v8

--- a/solution.py
+++ b/solution.py
@@ -152,7 +152,7 @@
 
 
 def outer_kernel(
-    halt_ref, hidden_ref, back_ref, prev_ref, next_ref, grad_ref, conv_ref, cpart_ref, epart_ref,
+    halt_ref, hidden_ref, back_ref, next_ref, prev_ref, grad_ref, conv_ref, cpart_ref, epart_ref,
     keep_ref, send_ref, two_ref, gtwo_ref, columns_ref,
 ):
     rows, _, cols = halt_ref.shape
@@ -313,8 +313,8 @@
         scratch_shapes=[pltpu.SemaphoreType.DMA((len(inputs),))],
         compiler_params=VMEM_LIMIT,
     )(*[pltpu.with_memory_space_constraint(a, pltpu.MemorySpace.HBM) for a in inputs])
+    from_next = lax.ppermute(up, "rows", [(i + 1, i) for i in range(NZ - 1)])
     from_prev = lax.ppermute(down, "rows", [(i, i + 1) for i in range(NZ - 1)])
-    from_next = lax.ppermute(up, "rows", [(i + 1, i) for i in range(NZ - 1)])
 
     devices = NX * NY * NC
     conv_rows, expand_rows = width // devices, chans // devices
@@ -330,7 +330,7 @@
     keep, send, two, gtwo = call(
         outer_kernel,
         [pltpu.VMEM(part, BF), pltpu.VMEM(part, BF), pltpu.VMEM((2 * cols, width), BF), pltpu.VMEM((4 * cols, width), BF)],
-        halting, hidden, back, from_prev, from_next, upstream, weight_conv, conv_part, expand_part,
+        halting, hidden, back, from_next, from_prev, upstream, weight_conv, conv_part, expand_part,
         scratch=[pltpu.VMEM((4 * cols, taps), BF)],
     )
 

time: 71 us -> 70.5 us (level)
  waiting for transfers between devices: 4.04 us -> 0.64 us
  blocking collectives: 49.6 us -> 51.9 us
    all_to_all x1, blocking collectives: 12.7 us -> 16.7 us  [local(): lax.all_to_all(total, AXES, 0, 0, axis_index_groups=near_groups(), tiled=...]
    all_to_all x1, blocking collectives: 20.2 us -> 16.2 us  [local(): lax.all_to_all(total, AXES, 0, 0, axis_index_groups=far_groups(), tiled=T...]
    ppermute x1, waiting for transfers between devices: 3.83 us -> 0.01 us  [local(): from_next = lax.ppermute(up, 'rows', [(i + 1, i) for i in range(NZ - 1)])]
    all_to_all x1, blocking collectives: 16.7 us -> 18.9 us  [local(): got = lax.all_to_all(total, 'rows', 0, 0, tiled=True)]
  transfers between devices with their start and end apart: 3 -> 3, of which waited for: 2 -> 2; matrix products, arithmetic and copies ran while one was open for 0% -> 0% of each run, Pallas kernels for 5% -> 6%
where the time goes in v9:
time: 70.5 us; the launch traced here: 70.2 us
  blocking collectives  51.9 us (74%)
  Pallas kernels  8.82 us (13%)
  starting transfers between devices  8.12 us (12%)
  between operations  0.71 us (1%)
    all_to_all x1, blocking collectives, local(): got = lax.all_to_all(total, 'rows', 0, 0, tiled=True)  18.9 us
    all_to_all x1, blocking collectives, local(): lax.all_to_all(total, AXES, 0, 0, axis_index_groups=near_groups(), tiled=...  16.7 us
    all_to_all x1, blocking collectives, local(): lax.all_to_all(total, AXES, 0, 0, axis_index_groups=far_groups(), tiled=T...  16.2 us
    pallas_call x7, Pallas kernels, call(): pl.pallas_call(kernel, out_shape=outs, scratch_shapes=list(scratch), comp...  6.7 us
    ppermute x1, starting transfers between devices, local(): from_prev = lax.ppermute(down, 'rows', [(i, i + 1) for i in range(NZ - 1)])  4.91 us
    pallas_call x1, Pallas kernels, local(): pl.pallas_call(enter_kernel, out_shape=[pltpu.VMEM(a.shape, a.dtype) for...  2.12 us
    ppermute x1, starting transfers between devices, local(): got = lax.ppermute(send, 'core', [(0, 1), (1, 0)])  1.92 us
  transfers between devices with their start and end apart: 3, of which 2 were waited for; matrix products, arithmetic and copies ran while one was open for 0% of the time, Pallas kernels for 6%

profile of v9, /device:TPU:8, one launch (start us, length us, event | category | flops | bytes accessed | tf_op | source)
XLA Modules:
  0.0 70.2 jit_solution(634788272305704087)
XLA Ops:
  0.6 0.0 copy-start
  0.6 2.1 %shard_map.93 = (s32[5,1,64]{2,1,0:T(1,128)S(1)}, bf16[320,1024]{1,0:T(8,128)(2,1)S(1)}, bf16[320,1024]{1,0:T(8,128)(2,1)S(1)}, bf16[256,1024]{1,0:T(8,128)(2,1)...) custom-call(s32[5,1,64]{2,1,0:T(1,128)} %bitcast.7, ...), custom_call_target="tpu_custom_call" | custom-call | tf_op jit(solution)/shard_map/pallas_call | solution.py:306
  2.8 1.3 %collective-permute-start = (bf16[192,256]{1,0:T(8,128)(2,1)S(1)}, bf16[192,256]{1,0:T(8,128)(2,1)S(1)}, u32[]{:S(2)}, u32[]{:S(2)}) collective-permute-start(bf16[192,256]{1,0:T(8,128)(2,1)S(1)} %get-tuple-element.34), channel_id=1, source_target_pairs={{1,0},{2,1},{3,2},{4,3},{5,4},{6,5},{7,6},{9,8},{10,9},{11,10},{12... | collective-permute-start | bytes 294920 | tf_op jit(solution)/shard_map/ppermute | solution.py:316
  4.1 4.9 %collective-permute-start.1 = (bf16[192,256]{1,0:T(8,128)(2,1)S(1)}, bf16[192,256]{1,0:T(8,128)(2,1)S(1)}, u32[]{:S(2)}, u32[]{:S(2)}) collective-permute-start(bf16[192,256]{1,0:T(8,128)(2,1)S(1)} %get-tuple-element.35), channel_id=1, source_target_pairs={{0,1},{1,2},{2,3},{3,4},{4,5},{5,6},{6,7},{8,9},{9,10},{10,11},{11... | collective-permute-start | bytes 294920 | tf_op jit(solution)/shard_map/ppermute | solution.py:317
  9.0 0.0 copy-done
  9.0 1.7 %shard_map.94 = (f32[256,2304]{1,0:T(8,128)S(1)}, f32[1024,256]{1,0:T(8,128)S(1)}, bf16[192,256]{1,0:T(8,128)(2,1)S(1)}, bf16[192,256]{1,0:T(8,128)(2,1)S(1)}) custom-call(s32[5,1,64]{2,1,0:T(1,128)S(1)} %get-tuple-element.29.halt_ref, bf16[320,256]{1,0:T(8,128)(2,1)S(1)} %get-tuple-element.30.hidden_ref, bf16[320,1024]{1,0:T(8,128)(2,1)S(1)} %get-tuple-element.28.grad_ref, ...), custom_call_target="tpu_custom_call" | custom-call | tf_op jit(solution)/shard_map/pallas_call | solution.py:285
  10.7 0.0 collective-permute-done.next_ref
  10.8 0.4 collective-permute-done.1.prev_ref
  11.2 1.8 %shard_map.95 = (bf16[4,416,256]{2,1,0:T(8,128)(2,1)S(1)}, bf16[4,416,256]{2,1,0:T(8,128)(2,1)S(1)}, bf16[128,256]{1,0:T(8,128)(2,1)S(1)}, bf16[256,256]{1,0:T(8,128)(2,1)S(1)}) custom-call(s32[5,1,64]{2,1,0:T(1,128)S(1)} %get-tuple-element.29.halt_ref, bf16[320,256]{1,0:T(8,128)(2,1)S(1)} %get-tuple-element.30.hidden_ref, ...), custom_call_target="tpu_custom_call" | custom-call | tf_op jit(solution)/shard_map/pallas_call | solution.py:285
  13.0 1.9 %collective-permute-start.2 = (bf16[4,416,256]{2,1,0:T(8,128)(2,1)S(1)}, bf16[4,416,256]{2,1,0:T(8,128)(2,1)S(1)}, u32[]{:S(2)}, u32[]{:S(2)}) collective-permute-start(bf16[4,416,256]{2,1,0:T(8,128)(2,1)S(1)} %get-tuple-element.46), channel_id=1, source_target_pairs={{0,8},{8,0},{1,9},{9,1},{2,10},{10,2},{3,11},{11,3},{4,12},{12,4},... | collective-permute-start | bytes 2555912 | tf_op jit(solution)/shard_map/ppermute | solution.py:337
  14.9 2.1 %shard_map.96 = (bf16[320,1024]{1,0:T(8,128)(2,1)}, bf16[320,1024]{1,0:T(8,128)(2,1)}, f32[8,128]{1,0:T(8,128)S(1)}) custom-call(bf16[320,1024]{1,0:T(8,128)(2,1)S(1)} %get-tuple-element.27.feat_ref, bf16[320,1024]{1,0:T(8,128)(2,1)S(1)} %get-tuple-element.28.grad_ref, bf16[192,256]{1,0:T(8,128)(2,1)S(1)} %get-tuple-element.32.two_in_ref, ...), custom_call_target="tpu_custom_call" | custom-call | tf_op jit(solution)/shard_map/pallas_call | solution.py:285
  17.0 0.2 collective-permute-done.2.got_ref
  17.2 0.2 shard_map.97
  17.4 16.7 %all_to_all.15.got_ref = bf16[4,416,256]{2,1,0:T(8,128)(2,1)S(1)} all-to-all(bf16[4,416,256]{2,1,0:T(8,128)(2,1)S(1)} %shard_map.97), channel_id=1, replica_groups={{8,136,264,392},{9,137,265,393},{10,138,266,394},{11,139,267,395},{12,1..., dimensions={0} | all-to-all | bytes 1703936 | tf_op jit(solution)/shard_map/all_to_all | solution.py:345
  34.1 0.2 shard_map.98
  34.3 16.2 %all_to_all.16.got_ref = bf16[16,4,1664]{2,1,0:T(4,128)(2,1)S(1)} all-to-all(bf16[16,4,1664]{2,1,0:T(4,128)(2,1)S(1)} %shard_map.98), channel_id=1, replica_groups={{8,9,24,25,40,41,56,57,72,73,88,89,104,105,120,121},{10,11,26,27,42,43,..., dimensions={0} | all-to-all | bytes 425984 | tf_op jit(solution)/shard_map/all_to_all | solution.py:350
  50.6 18.9 %all_to_all.17.got_ref = bf16[8,4,1664]{2,1,0:T(4,128)(2,1)S(1)} all-to-all(bf16[8,4,1664]{2,1,0:T(4,128)(2,1)S(1)} %shard_map.99), channel_id=1, replica_groups=mesh['x_hi'=2,'x_lo'=2,'y_hi'=4,'y_lo'=2,'core'=2,'rows'=8] {'rows'}, dimensions={0} | all-to-all | bytes 212992 | tf_op jit(solution)/shard_map/all_to_all | solution.py:352
  69.5 0.6 shard_map.100
  (1 shorter events, 0.0 us)
Async XLA Ops:
  0.6 8.4 %copy-start = (bf16[256,2304]{1,0:T(8,128)(2,1)S(1)}, bf16[256,2304]{1,0:T(8,128)(2,1)}, u32[]{:S(2)}) copy-start(bf16[256,2304]{1,0:T(8,128)(2,1)} %conv_ref.5) | copy-start | bytes 3538948
  2.8 8.0 %collective-permute-start = (bf16[192,256]{1,0:T(8,128)(2,1)S(1)}, bf16[192,256]{1,0:T(8,128)(2,1)S(1)}, u32[]{:S(2)}, u32[]{:S(2)}) collective-permute-start(bf16[192,256]{1,0:T(8,128)(2,1)S(1)} %get-tuple-element.34), channel_id=1, source_target_pairs={{1,0},{2,1},{3,2},{4,3},{5,4},{6,5},{7,6},{9,8},{10,9},{11,10},{12... | collective-permute-start | bytes 294920 | tf_op jit(solution)/shard_map/ppermute | solution.py:316
  4.1 7.1 %collective-permute-start.1 = (bf16[192,256]{1,0:T(8,128)(2,1)S(1)}, bf16[192,256]{1,0:T(8,128)(2,1)S(1)}, u32[]{:S(2)}, u32[]{:S(2)}) collective-permute-start(bf16[192,256]{1,0:T(8,128)(2,1)S(1)} %get-tuple-element.35), channel_id=1, source_target_pairs={{0,1},{1,2},{2,3},{3,4},{4,5},{5,6},{6,7},{8,9},{9,10},{10,11},{11... | collective-permute-start | bytes 294920 | tf_op jit(solution)/shard_map/ppermute | solution.py:317
  13.0 4.3 %collective-permute-start.2 = (bf16[4,416,256]{2,1,0:T(8,128)(2,1)S(1)}, bf16[4,416,256]{2,1,0:T(8,128)(2,1)S(1)}, u32[]{:S(2)}, u32[]{:S(2)}) collective-permute-start(bf16[4,416,256]{2,1,0:T(8,128)(2,1)S(1)} %get-tuple-element.46), channel_id=1, source_target_pairs={{0,8},{8,0},{1,9},{9,1},{2,10},{10,2},{3,11},{11,3},{4,12},{12,4},... | collective-permute-start | bytes 2555912 | tf_op jit(solution)/shard_map/ppermute | solution.py:337

commit v10 on v9

--- a/solution.py
+++ b/solution.py
@@ -206,12 +206,14 @@
 
 def leave_kernel(
     feat_ref, grad_ref, two_in_ref, two_ref, gtwo_in_ref, gtwo_ref, sign_ref, reduce_ref, conv_ref, expand_ref,
-    out_ref, gin_ref, done_ref, columns_ref, stacked_ref, *, cols,
+    out_ref, gin_ref, done_ref, columns_ref, stacked_ref, out_buf, gin_buf, sems, *, cols,
 ):
     own = feat_ref.shape[0]
     width = two_ref.shape[1]
     two = jnp.concatenate([two_ref[0:cols], two_in_ref[...], two_ref[cols:]], axis=0)
-    out_ref[...] = (feat_ref[...].astype(F32) + dot(two, expand_ref[...], 1, 1)).astype(BF)
+    out_buf[...] = (feat_ref[...].astype(F32) + dot(two, expand_ref[...], 1, 1)).astype(BF)
+    copies = [pltpu.make_async_copy(out_buf, out_ref, sems.at[0])]
+    copies[0].start()
     grad_two = jnp.concatenate([gtwo_ref[0 : 2 * cols], gtwo_in_ref[...], gtwo_ref[2 * cols :]], axis=0)
     left, right = neighbours(grad_two, cols)
     for a in range(3):
@@ -222,8 +224,16 @@
             stacked_ref[at, :] = conv_ref[:, at]
     grad_hidden = dot(columns_ref[...], stacked_ref[...], 1, 0)
     grad_one = (grad_hidden * sign_ref[...].astype(F32)).astype(BF)
-    gin_ref[...] = (grad_ref[...].astype(F32) + dot(grad_one, reduce_ref[...], 1, 0)).astype(BF)
+    half = own // 2
+    for i in range(2):
+        at = pl.ds(i * half, half)
+        back = dot(grad_one[i * half : (i + 1) * half], reduce_ref[...], 1, 0)
+        gin_buf[at, :] = (grad_ref[at, :].astype(F32) + back).astype(BF)
+        copies.append(pltpu.make_async_copy(gin_buf.at[at], gin_ref.at[at], sems.at[1 + i]))
+        copies[-1].start()
     done_ref[...] = jnp.zeros_like(done_ref)
+    for copy in copies:
+        copy.wait()
 
 
 def sum_of(parts_ref):
@@ -339,7 +349,14 @@
         functools.partial(leave_kernel, cols=cols),
         [jax.ShapeDtypeStruct((own, chans), BF)] * 2 + [pltpu.VMEM((8, 128), F32)],
         flat_in, upstream, two_in, two, gtwo_in, gtwo, sign, reduce_in, weight_conv, expand_in,
-        scratch=[pltpu.VMEM((own, taps), BF), pltpu.VMEM((taps, width), BF)],
+        scratch=[
+            pltpu.VMEM((own, taps), BF),
+            pltpu.VMEM((taps, width), BF),
+            pltpu.VMEM((own, chans), BF),
+            pltpu.VMEM((own, chans), BF),
+            pltpu.SemaphoreType.DMA((3,)),
+        ],
+        out_specs=[pl.BlockSpec(memory_space=pl.ANY)] * 2 + [pl.BlockSpec(memory_space=pltpu.VMEM)],
     )
     (total,) = call(core_kernel, [pltpu.VMEM(part, BF)], keep, got, done)
     got = lax.all_to_all(total, AXES, 0, 0, axis_index_groups=near_groups(), tiled=True)

time: 70.5 us -> 70.5 us (level)
  transfers between devices with their start and end apart: 3 -> 3, of which waited for: 2 -> 2; matrix products, arithmetic and copies ran while one was open for 0% -> 0% of each run, Pallas kernels for 6% -> 5%
where the time goes in v10:
time: 70.5 us; the launch traced here: 70.2 us
  blocking collectives  51.9 us (74%)
  Pallas kernels  8.73 us (12%)
  starting transfers between devices  8.12 us (12%)
  waiting for transfers between devices  0.72 us (1%)
  between operations  0.72 us (1%)
    all_to_all x1, blocking collectives, local(): got = lax.all_to_all(total, 'rows', 0, 0, tiled=True)  18.9 us
    all_to_all x1, blocking collectives, local(): lax.all_to_all(total, AXES, 0, 0, axis_index_groups=near_groups(), tiled=...  16.7 us
    all_to_all x1, blocking collectives, local(): lax.all_to_all(total, AXES, 0, 0, axis_index_groups=far_groups(), tiled=T...  16.2 us
    pallas_call x7, Pallas kernels, call(): pl.pallas_call(kernel, out_shape=outs, scratch_shapes=list(scratch), comp...  6.61 us
    ppermute x1, starting transfers between devices, local(): from_prev = lax.ppermute(down, 'rows', [(i, i + 1) for i in range(NZ - 1)])  4.91 us
    pallas_call x1, Pallas kernels, local(): pl.pallas_call(enter_kernel, out_shape=[pltpu.VMEM(a.shape, a.dtype) for...  2.12 us
    ppermute x1, starting transfers between devices, local(): got = lax.ppermute(send, 'core', [(0, 1), (1, 0)])  1.92 us
  transfers between devices with their start and end apart: 3, of which 2 were waited for; matrix products, arithmetic and copies ran while one was open for 0% of the time, Pallas kernels for 5%

profile of v10, /device:TPU:8, one launch (start us, length us, event | category | flops | bytes accessed | tf_op | source)
XLA Modules:
  0.0 70.2 jit_solution(18050330315679268949)
XLA Ops:
  0.6 0.0 copy-start
  0.6 2.1 %shard_map.93 = (s32[5,1,64]{2,1,0:T(1,128)S(1)}, bf16[320,1024]{1,0:T(8,128)(2,1)S(1)}, bf16[320,1024]{1,0:T(8,128)(2,1)S(1)}, bf16[256,1024]{1,0:T(8,128)(2,1)...) custom-call(s32[5,1,64]{2,1,0:T(1,128)} %bitcast.7, ...), custom_call_target="tpu_custom_call" | custom-call | tf_op jit(solution)/shard_map/pallas_call | solution.py:316
  2.8 1.3 %collective-permute-start = (bf16[192,256]{1,0:T(8,128)(2,1)S(1)}, bf16[192,256]{1,0:T(8,128)(2,1)S(1)}, u32[]{:S(2)}, u32[]{:S(2)}) collective-permute-start(bf16[192,256]{1,0:T(8,128)(2,1)S(1)} %get-tuple-element.34), channel_id=1, source_target_pairs={{1,0},{2,1},{3,2},{4,3},{5,4},{6,5},{7,6},{9,8},{10,9},{11,10},{12... | collective-permute-start | bytes 294920 | tf_op jit(solution)/shard_map/ppermute | solution.py:326
  4.1 4.9 %collective-permute-start.1 = (bf16[192,256]{1,0:T(8,128)(2,1)S(1)}, bf16[192,256]{1,0:T(8,128)(2,1)S(1)}, u32[]{:S(2)}, u32[]{:S(2)}) collective-permute-start(bf16[192,256]{1,0:T(8,128)(2,1)S(1)} %get-tuple-element.35), channel_id=1, source_target_pairs={{0,1},{1,2},{2,3},{3,4},{4,5},{5,6},{6,7},{8,9},{9,10},{10,11},{11... | collective-permute-start | bytes 294920 | tf_op jit(solution)/shard_map/ppermute | solution.py:327
  9.0 0.0 copy-done
  9.0 1.7 %shard_map.94 = (f32[256,2304]{1,0:T(8,128)S(1)}, f32[1024,256]{1,0:T(8,128)S(1)}, bf16[192,256]{1,0:T(8,128)(2,1)S(1)}, bf16[192,256]{1,0:T(8,128)(2,1)S(1)}) custom-call(s32[5,1,64]{2,1,0:T(1,128)S(1)} %get-tuple-element.29.halt_ref, bf16[320,256]{1,0:T(8,128)(2,1)S(1)} %get-tuple-element.30.hidden_ref, bf16[320,1024]{1,0:T(8,128)(2,1)S(1)} %get-tuple-element.28.grad_ref, ...), custom_call_target="tpu_custom_call" | custom-call | tf_op jit(solution)/shard_map/pallas_call | solution.py:295
  10.7 0.0 collective-permute-done.next_ref
  10.8 0.4 collective-permute-done.1.prev_ref
  11.2 1.8 %shard_map.95 = (bf16[4,416,256]{2,1,0:T(8,128)(2,1)S(1)}, bf16[4,416,256]{2,1,0:T(8,128)(2,1)S(1)}, bf16[128,256]{1,0:T(8,128)(2,1)S(1)}, bf16[256,256]{1,0:T(8,128)(2,1)S(1)}) custom-call(s32[5,1,64]{2,1,0:T(1,128)S(1)} %get-tuple-element.29.halt_ref, bf16[320,256]{1,0:T(8,128)(2,1)S(1)} %get-tuple-element.30.hidden_ref, ...), custom_call_target="tpu_custom_call" | custom-call | tf_op jit(solution)/shard_map/pallas_call | solution.py:295
  13.0 1.9 %collective-permute-start.2 = (bf16[4,416,256]{2,1,0:T(8,128)(2,1)S(1)}, bf16[4,416,256]{2,1,0:T(8,128)(2,1)S(1)}, u32[]{:S(2)}, u32[]{:S(2)}) collective-permute-start(bf16[4,416,256]{2,1,0:T(8,128)(2,1)S(1)} %get-tuple-element.46), channel_id=1, source_target_pairs={{0,8},{8,0},{1,9},{9,1},{2,10},{10,2},{3,11},{11,3},{4,12},{12,4},... | collective-permute-start | bytes 2555912 | tf_op jit(solution)/shard_map/ppermute | solution.py:347
  14.9 2.0 %shard_map.96 = (bf16[320,1024]{1,0:T(8,128)(2,1)}, bf16[320,1024]{1,0:T(8,128)(2,1)}, f32[8,128]{1,0:T(8,128)S(1)}) custom-call(bf16[320,1024]{1,0:T(8,128)(2,1)S(1)} %get-tuple-element.27.feat_ref, bf16[320,1024]{1,0:T(8,128)(2,1)S(1)} %get-tuple-element.28.grad_ref, bf16[192,256]{1,0:T(8,128)(2,1)S(1)} %get-tuple-element.32.two_in_ref, ...), custom_call_target="tpu_custom_call" | custom-call | tf_op jit(solution)/shard_map/pallas_call | solution.py:295
  17.0 0.3 collective-permute-done.2.got_ref
  17.2 0.2 shard_map.97
  17.4 16.7 %all_to_all.15.got_ref = bf16[4,416,256]{2,1,0:T(8,128)(2,1)S(1)} all-to-all(bf16[4,416,256]{2,1,0:T(8,128)(2,1)S(1)} %shard_map.97), channel_id=1, replica_groups={{8,136,264,392},{9,137,265,393},{10,138,266,394},{11,139,267,395},{12,1..., dimensions={0} | all-to-all | bytes 1703936 | tf_op jit(solution)/shard_map/all_to_all | solution.py:362
  34.1 0.2 shard_map.98
  34.3 16.2 %all_to_all.16.got_ref = bf16[16,4,1664]{2,1,0:T(4,128)(2,1)S(1)} all-to-all(bf16[16,4,1664]{2,1,0:T(4,128)(2,1)S(1)} %shard_map.98), channel_id=1, replica_groups={{8,9,24,25,40,41,56,57,72,73,88,89,104,105,120,121},{10,11,26,27,42,43,..., dimensions={0} | all-to-all | bytes 425984 | tf_op jit(solution)/shard_map/all_to_all | solution.py:367
  50.6 18.9 %all_to_all.17.got_ref = bf16[8,4,1664]{2,1,0:T(4,128)(2,1)S(1)} all-to-all(bf16[8,4,1664]{2,1,0:T(4,128)(2,1)S(1)} %shard_map.99), channel_id=1, replica_groups=mesh['x_hi'=2,'x_lo'=2,'y_hi'=4,'y_lo'=2,'core'=2,'rows'=8] {'rows'}, dimensions={0} | all-to-all | bytes 212992 | tf_op jit(solution)/shard_map/all_to_all | solution.py:369
  69.5 0.6 shard_map.100
  (1 shorter events, 0.0 us)
Async XLA Ops:
  0.6 8.4 %copy-start = (bf16[256,2304]{1,0:T(8,128)(2,1)S(1)}, bf16[256,2304]{1,0:T(8,128)(2,1)}, u32[]{:S(2)}) copy-start(bf16[256,2304]{1,0:T(8,128)(2,1)} %conv_ref.5) | copy-start | bytes 3538948
  2.8 8.0 %collective-permute-start = (bf16[192,256]{1,0:T(8,128)(2,1)S(1)}, bf16[192,256]{1,0:T(8,128)(2,1)S(1)}, u32[]{:S(2)}, u32[]{:S(2)}) collective-permute-start(bf16[192,256]{1,0:T(8,128)(2,1)S(1)} %get-tuple-element.34), channel_id=1, source_target_pairs={{1,0},{2,1},{3,2},{4,3},{5,4},{6,5},{7,6},{9,8},{10,9},{11,10},{12... | collective-permute-start | bytes 294920 | tf_op jit(solution)/shard_map/ppermute | solution.py:326
  4.1 7.1 %collective-permute-start.1 = (bf16[192,256]{1,0:T(8,128)(2,1)S(1)}, bf16[192,256]{1,0:T(8,128)(2,1)S(1)}, u32[]{:S(2)}, u32[]{:S(2)}) collective-permute-start(bf16[192,256]{1,0:T(8,128)(2,1)S(1)} %get-tuple-element.35), channel_id=1, source_target_pairs={{0,1},{1,2},{2,3},{3,4},{4,5},{5,6},{6,7},{8,9},{9,10},{10,11},{11... | collective-permute-start | bytes 294920 | tf_op jit(solution)/shard_map/ppermute | solution.py:327
  13.0 4.3 %collective-permute-start.2 = (bf16[4,416,256]{2,1,0:T(8,128)(2,1)S(1)}, bf16[4,416,256]{2,1,0:T(8,128)(2,1)S(1)}, u32[]{:S(2)}, u32[]{:S(2)}) collective-permute-start(bf16[4,416,256]{2,1,0:T(8,128)(2,1)S(1)} %get-tuple-element.46), channel_id=1, source_target_pairs={{0,8},{8,0},{1,9},{9,1},{2,10},{10,2},{3,11},{11,3},{4,12},{12,4},... | collective-permute-start | bytes 2555912 | tf_op jit(solution)/shard_map/ppermute | solution.py:347

commit v11 on v9

--- a/solution.py
+++ b/solution.py
@@ -134,48 +134,48 @@
 
 
 def inner_kernel(
-    halt_ref, hidden_ref, grad_ref, expand_ref, conv_ref,
+    halt_ref, hidden_ref, back_ref, next_ref, grad_ref, expand_ref, conv_ref,
     cpart_ref, epart_ref, two_ref, gtwo_ref, columns_ref,
 ):
     rows, _, cols = halt_ref.shape
-    inner = slice(cols, (rows - 1) * cols)
-    fill_columns(columns_ref, 0, hidden_ref[...], cols)
+    mine, middle = slice(cols, rows * cols), (rows - 2) * cols
+    own = slice(0, (rows - 1) * cols)
+    fill_columns(columns_ref, 0, jnp.concatenate([hidden_ref[...], next_ref[0 : 2 * cols]], axis=0), cols)
     pre_two = dot(columns_ref[...], conv_ref[...], 1, 1)
-    back = active_column(halt_ref, range(1, rows - 1)) * dot(grad_ref[inner, :], expand_ref[...], 1, 0)
-    grad_two = jnp.where(pre_two > 0, back, 0.0).astype(BF)
+    active = active_column(halt_ref, range(1, rows))
+    back = (active[0:middle] * dot(grad_ref[cols : cols + middle, :], expand_ref[...], 1, 0)).astype(BF)
+    back = jnp.concatenate([back, back_ref[cols:], next_ref[2 * cols :]], axis=0)
+    grad_two = jnp.where(pre_two > 0, back.astype(F32), 0.0).astype(BF)
     gtwo_ref[...] = grad_two
-    hidden_two = (active_column(halt_ref, range(1, rows - 1)) * jnp.maximum(pre_two, 0.0)).astype(BF)
+    hidden_two = (active * jnp.maximum(pre_two[own], 0.0)).astype(BF)
     two_ref[...] = hidden_two
-    grad_rows = dot(sorting(grad_two.shape[1]), grad_two, 1, 1).astype(BF)
-    cpart_ref[...] = dot(grad_rows, columns_ref[...], 1, 0)
-    epart_ref[...] = dot(grad_ref[inner, :], hidden_two, 0, 0)
+    grad_rows = dot(sorting(grad_two.shape[1]), grad_two[own], 1, 1).astype(BF)
+    cpart_ref[...] = dot(grad_rows, columns_ref[own, :], 1, 0)
+    epart_ref[...] = dot(grad_ref[mine, :], hidden_two, 0, 0)
 
 
 def outer_kernel(
-    halt_ref, hidden_ref, back_ref, next_ref, prev_ref, grad_ref, conv_ref, cpart_ref, epart_ref,
+    halt_ref, hidden_ref, back_ref, prev_ref, grad_ref, conv_ref, cpart_ref, epart_ref,
     keep_ref, send_ref, two_ref, gtwo_ref, columns_ref,
 ):
-    rows, _, cols = halt_ref.shape
+    cols = halt_ref.shape[2]
     width = hidden_ref.shape[1]
     core = lax.axis_index("core")
-    top, end = slice(0, cols), slice((rows - 1) * cols, rows * cols)
     halo = 2 * cols
     above = jnp.concatenate([prev_ref[0:halo], hidden_ref[0:halo]], axis=0)
-    below = jnp.concatenate([hidden_ref[(rows - 2) * cols :], next_ref[0:halo]], axis=0)
     fill_columns(columns_ref, 0, above, cols)
-    fill_columns(columns_ref, halo, below, cols)
     pre_two = dot(columns_ref[...], conv_ref[...], 1, 1)
-    back = jnp.concatenate([prev_ref[halo:], back_ref[...], next_ref[halo:]], axis=0)
+    back = jnp.concatenate([prev_ref[halo:], back_ref[0:cols]], axis=0)
     grad_two = jnp.where(pre_two > 0, back.astype(F32), 0.0).astype(BF)
     gtwo_ref[...] = grad_two
-    active = active_column(halt_ref, (0, rows - 1))
-    own = slice(cols, cols + halo)
+    active = active_column(halt_ref, (0,))
+    own = slice(cols, halo)
     hidden_two = (active * jnp.maximum(pre_two[own], 0.0)).astype(BF)
     two_ref[...] = hidden_two
 
     grad_rows = dot(sorting(width), grad_two[own], 1, 1).astype(BF)
     conv_part = (cpart_ref[...] + dot(grad_rows, columns_ref[own, :], 1, 0)).astype(BF)
-    upstream = jnp.concatenate([grad_ref[top, :], grad_ref[end, :]], axis=0)
+    upstream = grad_ref[0:cols, :]
     expand_part = (epart_ref[...] + dot(upstream, hidden_two, 0, 0)).astype(BF)
 
     def write(group, rows, low, along, square):
@@ -210,9 +210,9 @@
 ):
     own = feat_ref.shape[0]
     width = two_ref.shape[1]
-    two = jnp.concatenate([two_ref[0:cols], two_in_ref[...], two_ref[cols:]], axis=0)
+    two = jnp.concatenate([two_ref[...], two_in_ref[...]], axis=0)
     out_ref[...] = (feat_ref[...].astype(F32) + dot(two, expand_ref[...], 1, 1)).astype(BF)
-    grad_two = jnp.concatenate([gtwo_ref[0 : 2 * cols], gtwo_in_ref[...], gtwo_ref[2 * cols :]], axis=0)
+    grad_two = jnp.concatenate([gtwo_ref[...], gtwo_in_ref[...]], axis=0)
     left, right = neighbours(grad_two, cols)
     for a in range(3):
         for b, shifted in enumerate((right, grad_two, left)):
@@ -320,18 +320,17 @@
     conv_rows, expand_rows = width // devices, chans // devices
     shard_rows = conv_rows * taps // width + expand_rows
     part = (4, HX * HY * shard_rows, width)
-    inner = (own - 2 * cols, width)
     conv_part, expand_part, two_in, gtwo_in = call(
         inner_kernel,
-        [pltpu.VMEM((width, taps), F32), pltpu.VMEM((chans, width), F32), pltpu.VMEM(inner, BF), pltpu.VMEM(inner, BF)],
-        halting, hidden, upstream, expand_in, weight_conv,
-        scratch=[pltpu.VMEM((inner[0], taps), BF)],
+        [pltpu.VMEM((width, taps), F32), pltpu.VMEM((chans, width), F32), pltpu.VMEM((own - cols, width), BF), pltpu.VMEM((own, width), BF)],
+        halting, hidden, back, from_next, upstream, expand_in, weight_conv,
+        scratch=[pltpu.VMEM((own, taps), BF)],
     )
     keep, send, two, gtwo = call(
         outer_kernel,
-        [pltpu.VMEM(part, BF), pltpu.VMEM(part, BF), pltpu.VMEM((2 * cols, width), BF), pltpu.VMEM((4 * cols, width), BF)],
-        halting, hidden, back, from_next, from_prev, upstream, weight_conv, conv_part, expand_part,
-        scratch=[pltpu.VMEM((4 * cols, taps), BF)],
+        [pltpu.VMEM(part, BF), pltpu.VMEM(part, BF), pltpu.VMEM((cols, width), BF), pltpu.VMEM((2 * cols, width), BF)],
+        halting, hidden, back, from_prev, upstream, weight_conv, conv_part, expand_part,
+        scratch=[pltpu.VMEM((2 * cols, taps), BF)],
     )
 
     got = lax.ppermute(send, "core", [(0, 1), (1, 0)])

time: 70.5 us -> 70.4 us (level)
    ppermute x1, waiting for transfers between devices: 0.01 us -> 0.85 us  [local(): from_next = lax.ppermute(up, 'rows', [(i + 1, i) for i in range(NZ - 1)])]
where the time goes in v11:
time: 70.4 us; the launch traced here: 70.2 us
  blocking collectives  51.3 us (73%)
  Pallas kernels  9.02 us (13%)
  starting transfers between devices  8.12 us (12%)
  waiting for transfers between devices  1.06 us (2%)
    all_to_all x1, blocking collectives, local(): got = lax.all_to_all(total, 'rows', 0, 0, tiled=True)  18.3 us
    all_to_all x1, blocking collectives, local(): lax.all_to_all(total, AXES, 0, 0, axis_index_groups=far_groups(), tiled=T...  16.8 us
    all_to_all x1, blocking collectives, local(): lax.all_to_all(total, AXES, 0, 0, axis_index_groups=near_groups(), tiled=...  16.1 us
    pallas_call x7, Pallas kernels, call(): pl.pallas_call(kernel, out_shape=outs, scratch_shapes=list(scratch), comp...  6.89 us
    ppermute x1, starting transfers between devices, local(): from_prev = lax.ppermute(down, 'rows', [(i, i + 1) for i in range(NZ - 1)])  4.91 us
    pallas_call x1, Pallas kernels, local(): pl.pallas_call(enter_kernel, out_shape=[pltpu.VMEM(a.shape, a.dtype) for...  2.12 us
    ppermute x1, starting transfers between devices, local(): got = lax.ppermute(send, 'core', [(0, 1), (1, 0)])  1.92 us
  transfers between devices with their start and end apart: 3, of which 2 were waited for; matrix products, arithmetic and copies ran while one was open for 0% of the time, Pallas kernels for 6%

profile of v11, /device:TPU:8, one launch (start us, length us, event | category | flops | bytes accessed | tf_op | source)
XLA Modules:
  0.0 70.2 jit_solution(6112492234921925599)
XLA Ops:
  0.6 0.0 copy-start
  0.6 2.1 %shard_map.93 = (s32[5,1,64]{2,1,0:T(1,128)S(1)}, bf16[320,1024]{1,0:T(8,128)(2,1)S(1)}, bf16[320,1024]{1,0:T(8,128)(2,1)S(1)}, bf16[256,1024]{1,0:T(8,128)(2,1)...) custom-call(s32[5,1,64]{2,1,0:T(1,128)} %bitcast.7, ...), custom_call_target="tpu_custom_call" | custom-call | tf_op jit(solution)/shard_map/pallas_call | solution.py:306
  2.8 1.3 %collective-permute-start = (bf16[192,256]{1,0:T(8,128)(2,1)S(1)}, bf16[192,256]{1,0:T(8,128)(2,1)S(1)}, u32[]{:S(2)}, u32[]{:S(2)}) collective-permute-start(bf16[192,256]{1,0:T(8,128)(2,1)S(1)} %get-tuple-element.32), channel_id=1, source_target_pairs={{1,0},{2,1},{3,2},{4,3},{5,4},{6,5},{7,6},{9,8},{10,9},{11,10},{12... | collective-permute-start | bytes 294920 | tf_op jit(solution)/shard_map/ppermute | solution.py:316
  4.1 4.9 %collective-permute-start.1 = (bf16[192,256]{1,0:T(8,128)(2,1)S(1)}, bf16[192,256]{1,0:T(8,128)(2,1)S(1)}, u32[]{:S(2)}, u32[]{:S(2)}) collective-permute-start(bf16[192,256]{1,0:T(8,128)(2,1)S(1)} %get-tuple-element.35), channel_id=1, source_target_pairs={{0,1},{1,2},{2,3},{3,4},{4,5},{5,6},{6,7},{8,9},{9,10},{10,11},{11... | collective-permute-start | bytes 294920 | tf_op jit(solution)/shard_map/ppermute | solution.py:317
  9.0 0.8 %collective-permute-done.next_ref = bf16[192,256]{1,0:T(8,128)(2,1)S(1)} collective-permute-done((bf16[192,256]{1,0:T(8,128)(2,1)S(1)}, bf16[192,256]{1,0:T(8,128)(2,1)S(1)}, u32[]{:S(2)}, u32[]{:S(2)}) %collective-permute-start) | collective-permute-done | bytes 98336 | tf_op jit(solution)/shard_map/ppermute | solution.py:316
  9.8 0.0 copy-done
  9.8 1.9 %shard_map.94 = (f32[256,2304]{1,0:T(8,128)S(1)}, f32[1024,256]{1,0:T(8,128)S(1)}, bf16[256,256]{1,0:T(8,128)(2,1)S(1)}, bf16[320,256]{1,0:T(8,128)(2,1)S(1)}) custom-call(s32[5,1,64]{2,1,0:T(1,128)S(1)} %get-tuple-element.29.halt_ref, bf16[320,256]{1,0:T(8,128)(2,1)S(1)} %get-tuple-element.30.hidden_ref, bf16[128,256]{1,0:T(8,128)(2,1)S(1)} %get-tuple-element.31.back_ref, ...), custom_call_target="tpu_custom_call" | custom-call | tf_op jit(solution)/shard_map/pallas_call | solution.py:285
  11.8 0.0 collective-permute-done.1.prev_ref
  11.8 1.8 %shard_map.95 = (bf16[4,416,256]{2,1,0:T(8,128)(2,1)S(1)}, bf16[4,416,256]{2,1,0:T(8,128)(2,1)S(1)}, bf16[64,256]{1,0:T(8,128)(2,1)S(1)}, bf16[128,256]{1,0:T(8,128)(2,1)S(1)}) custom-call(s32[5,1,64]{2,1,0:T(1,128)S(1)} %get-tuple-element.29.halt_ref, bf16[320,256]{1,0:T(8,128)(2,1)S(1)} %get-tuple-element.30.hidden_ref, ...), custom_call_target="tpu_custom_call" | custom-call | tf_op jit(solution)/shard_map/pallas_call | solution.py:285
  13.6 1.9 %collective-permute-start.2 = (bf16[4,416,256]{2,1,0:T(8,128)(2,1)S(1)}, bf16[4,416,256]{2,1,0:T(8,128)(2,1)S(1)}, u32[]{:S(2)}, u32[]{:S(2)}) collective-permute-start(bf16[4,416,256]{2,1,0:T(8,128)(2,1)S(1)} %get-tuple-element.46), channel_id=1, source_target_pairs={{0,8},{8,0},{1,9},{9,1},{2,10},{10,2},{3,11},{11,3},{4,12},{12,4},... | collective-permute-start | bytes 2555912 | tf_op jit(solution)/shard_map/ppermute | solution.py:336
  15.5 2.1 %shard_map.96 = (bf16[320,1024]{1,0:T(8,128)(2,1)}, bf16[320,1024]{1,0:T(8,128)(2,1)}, f32[8,128]{1,0:T(8,128)S(1)}) custom-call(bf16[320,1024]{1,0:T(8,128)(2,1)S(1)} %get-tuple-element.27.feat_ref, bf16[320,1024]{1,0:T(8,128)(2,1)S(1)} %get-tuple-element.28.grad_ref, bf16[256,256]{1,0:T(8,128)(2,1)S(1)} %get-tuple-element.34.two_in_ref, ...), custom_call_target="tpu_custom_call" | custom-call | tf_op jit(solution)/shard_map/pallas_call | solution.py:285
  17.6 0.2 collective-permute-done.2.got_ref
  17.8 0.2 shard_map.97
  18.0 16.1 %all_to_all.15.got_ref = bf16[4,416,256]{2,1,0:T(8,128)(2,1)S(1)} all-to-all(bf16[4,416,256]{2,1,0:T(8,128)(2,1)S(1)} %shard_map.97), channel_id=1, replica_groups={{8,136,264,392},{9,137,265,393},{10,138,266,394},{11,139,267,395},{12,1..., dimensions={0} | all-to-all | bytes 1703936 | tf_op jit(solution)/shard_map/all_to_all | solution.py:344
  34.1 0.2 shard_map.98
  34.3 16.8 %all_to_all.16.got_ref = bf16[16,4,1664]{2,1,0:T(4,128)(2,1)S(1)} all-to-all(bf16[16,4,1664]{2,1,0:T(4,128)(2,1)S(1)} %shard_map.98), channel_id=1, replica_groups={{8,9,24,25,40,41,56,57,72,73,88,89,104,105,120,121},{10,11,26,27,42,43,..., dimensions={0} | all-to-all | bytes 425984 | tf_op jit(solution)/shard_map/all_to_all | solution.py:349
  51.2 18.3 %all_to_all.17.got_ref = bf16[8,4,1664]{2,1,0:T(4,128)(2,1)S(1)} all-to-all(bf16[8,4,1664]{2,1,0:T(4,128)(2,1)S(1)} %shard_map.99), channel_id=1, replica_groups=mesh['x_hi'=2,'x_lo'=2,'y_hi'=4,'y_lo'=2,'core'=2,'rows'=8] {'rows'}, dimensions={0} | all-to-all | bytes 212992 | tf_op jit(solution)/shard_map/all_to_all | solution.py:351
  69.5 0.6 shard_map.100
  (1 shorter events, 0.0 us)
Async XLA Ops:
  0.6 9.2 %copy-start = (bf16[256,2304]{1,0:T(8,128)(2,1)S(1)}, bf16[256,2304]{1,0:T(8,128)(2,1)}, u32[]{:S(2)}) copy-start(bf16[256,2304]{1,0:T(8,128)(2,1)} %conv_ref.5) | copy-start | bytes 3538948
  2.8 7.1 %collective-permute-start = (bf16[192,256]{1,0:T(8,128)(2,1)S(1)}, bf16[192,256]{1,0:T(8,128)(2,1)S(1)}, u32[]{:S(2)}, u32[]{:S(2)}) collective-permute-start(bf16[192,256]{1,0:T(8,128)(2,1)S(1)} %get-tuple-element.32), channel_id=1, source_target_pairs={{1,0},{2,1},{3,2},{4,3},{5,4},{6,5},{7,6},{9,8},{10,9},{11,10},{12... | collective-permute-start | bytes 294920 | tf_op jit(solution)/shard_map/ppermute | solution.py:316
  4.1 7.7 %collective-permute-start.1 = (bf16[192,256]{1,0:T(8,128)(2,1)S(1)}, bf16[192,256]{1,0:T(8,128)(2,1)S(1)}, u32[]{:S(2)}, u32[]{:S(2)}) collective-permute-start(bf16[192,256]{1,0:T(8,128)(2,1)S(1)} %get-tuple-element.35), channel_id=1, source_target_pairs={{0,1},{1,2},{2,3},{3,4},{4,5},{5,6},{6,7},{8,9},{9,10},{10,11},{11... | collective-permute-start | bytes 294920 | tf_op jit(solution)/shard_map/ppermute | solution.py:317
  13.6 4.3 %collective-permute-start.2 = (bf16[4,416,256]{2,1,0:T(8,128)(2,1)S(1)}, bf16[4,416,256]{2,1,0:T(8,128)(2,1)S(1)}, u32[]{:S(2)}, u32[]{:S(2)}) collective-permute-start(bf16[4,416,256]{2,1,0:T(8,128)(2,1)S(1)} %get-tuple-element.46), channel_id=1, source_target_pairs={{0,8},{8,0},{1,9},{9,1},{2,10},{10,2},{3,11},{11,3},{4,12},{12,4},... | collective-permute-start | bytes 2555912 | tf_op jit(solution)/shard_map/ppermute | solution.py:336
